TPU v7x, 32 devices: a whole 2x2x4 slice. The times are simulated.
32 devices in a mesh: img: 8 (over z, x), ch: 4 (over y, core).
Axes of the slice: x: 2, y: 2, z: 4, core: 2. Of those that a mesh axis runs over, the one named last changes fastest.
Arguments:
- tokens: bfloat16 [32, 576, 1024], P(('img', 'ch')), may hold values from -6 to 6
- features: bfloat16 [32, 1536, 1024], P('img', 'ch'), may hold values from -6 to 6
- sample_of: int32 [32], P(('img', 'ch')), may hold values from 0 to 11, never falling along the last dimension, each value on 1 to 4 neighbouring positions
- cotangent: bfloat16 [32, 576, 1024], P(('img', 'ch')), may hold values from -6 to 6
- ln1_gain: bfloat16 [1024], P(('img', 'ch')), may hold values from 0.5 to 1.5
- ln1_bias: bfloat16 [1024], P(('img', 'ch')), may hold values from -1.75 to 1.75
- w_qkv: bfloat16 [1024, 3072], P(('img', 'ch')), may hold values from -0.1875 to 0.1875
- bias_qv: bfloat16 [2048], P(('img', 'ch')), may hold values from -3 to 3
- w_attn_out: bfloat16 [1024, 1024], P(('img', 'ch')), may hold values from -0.75 to 0.75
- bias_attn_out: bfloat16 [1024], P(('img', 'ch')), may hold values from -3 to 3
- ln2_gain: bfloat16 [1024], P(('img', 'ch')), may hold values from 0.5 to 1.5
- ln2_bias: bfloat16 [1024], P(('img', 'ch')), may hold values from -1.75 to 1.75
- w_fc1: bfloat16 [1024, 4096], P(('img', 'ch')), may hold values from -0.1875 to 0.1875
- bias_fc1: bfloat16 [4096], P(('img', 'ch')), may hold values from -3 to 3
- w_fc2: bfloat16 [4096, 1024], P(('img', 'ch')), may hold values from -0.125 to 0.125
- bias_fc2: bfloat16 [1024], P(('img', 'ch')), may hold values from -3 to 3
- w_proj: bfloat16 [1536, 1024], P(('img', 'ch')), may hold values from -0.3125 to 0.3125
- bias_proj: bfloat16 [1024], P(('img', 'ch')), may hold values from -3 to 3
- w_depth: bfloat16 [9, 1024], P(None, ('img', 'ch')), may hold values from -2 to 2
- bias_depth: bfloat16 [1024], P(('img', 'ch')), may hold values from -3 to 3
- w_gate_in: bfloat16 [1024, 512], P(('img', 'ch')), may hold values from -0.375 to 0.375
- w_gate_out: bfloat16 [512, 1024], P(None, ('img', 'ch')), may hold values from -0.375 to 0.375
Outputs:
- layer_out: bfloat16 [32, 576, 1024], P(('img', 'ch'))
- grad_tokens: bfloat16 [32, 576, 1024], P(('img', 'ch'))
- grad_features: bfloat16 [32, 1536, 1024], P('img', 'ch')
- grad_ln1_gain: float32 [1024], P(('img', 'ch'))
- grad_ln1_bias: float32 [1024], P(('img', 'ch'))
- grad_w_qkv: float32 [1024, 3072], P(('img', 'ch'))
- grad_bias_qv: float32 [2048], P(('img', 'ch'))
- grad_w_attn_out: float32 [1024, 1024], P(('img', 'ch'))
- grad_bias_attn_out: float32 [1024], P(('img', 'ch'))
- grad_ln2_gain: float32 [1024], P(('img', 'ch'))
- grad_ln2_bias: float32 [1024], P(('img', 'ch'))
- grad_w_fc1: float32 [1024, 4096], P(('img', 'ch'))
- grad_bias_fc1: float32 [4096], P(('img', 'ch'))
- grad_w_fc2: float32 [4096, 1024], P(('img', 'ch'))
- grad_bias_fc2: float32 [1024], P(('img', 'ch'))
- grad_w_proj: float32 [1536, 1024], P(('img', 'ch'))
- grad_bias_proj: float32 [1024], P(('img', 'ch'))
- grad_w_depth: float32 [9, 1024], P(None, ('img', 'ch'))
- grad_bias_depth: float32 [1024], P(('img', 'ch'))
- grad_w_gate_in: float32 [1024, 512], P(('img', 'ch'))
- grad_w_gate_out: float32 [512, 1024], P(None, ('img', 'ch'))
- gate_mean: float32 [], replicated
Inputs may be any that keep to these rules, and one draw needn't show every extreme that they name: `sample_of`: the images of one sample are consecutive; every sample has 1 to 4 images, and sample numbers never fall along the images.
All inputs are finite; a program needn't handle non-finite values.
Results may differ from a plain program's by a relative error of at most 0.012.
Values may be sent and summed in bfloat16 or wider, within the bound.
No kernel may reach another device: no remote copies, remote signals or barrier semaphores. Data moves between devices by JAX's collectives and lax.ppermute only.
A program may use at most 256 MiB of HBM per device.

v0:
```python
import jax
import jax.numpy as jnp
from jax import lax
from jax.sharding import PartitionSpec as P

HEAD = 64
PS = 24
FS = 32


norm_eps = 1e-05
highest = lax.Precision.HIGHEST


def shifted(x, axis, by):
    devices = lax.axis_size(axis)
    pairs = [(i, i + by) for i in range(devices) if 0 <= i + by < devices]
    return lax.ppermute(x, axis, pairs)


def layer_norm(inputs, scale_gain, offset_bias):
    centre = jnp.mean(inputs, axis=-1, keepdims=True)
    centred = inputs - centre
    spread = jnp.mean(centred * centred, axis=-1, keepdims=True)
    return centred * lax.rsqrt(spread + norm_eps) * scale_gain + offset_bias


def pool_table(coarse_side, fine_side):
    coarse_index = jnp.arange(coarse_side)[:, None]
    fine_index = jnp.arange(fine_side)[None, :]
    window_start = coarse_index * fine_side // coarse_side
    window_end = ((coarse_index + 1) * fine_side + coarse_side - 1) // coarse_side
    inside = jnp.logical_and(fine_index >= window_start, fine_index < window_end)
    single = jnp.where(inside, 1.0, 0.0).astype(jnp.float32) / (window_end - window_start).astype(
        jnp.float32
    )
    return jnp.kron(single, single)


def depth_filter(projected, kernel, offset_bias):
    count_images = projected.shape[0]
    grid_cells = projected.reshape(count_images, PS, PS, -1)
    padded = jnp.pad(grid_cells, ((0, 0), (1, 1), (1, 1), (0, 0)))
    summed = jnp.zeros_like(grid_cells)
    for tap_row in range(3):
        for tap_col in range(3):
            summed = (
                summed
                + padded[:, tap_row : tap_row + PS, tap_col : tap_col + PS, :]
                * kernel[3 * tap_row + tap_col]
            )
    return summed.reshape(count_images, PS * PS, -1) + offset_bias


def gate_of(sample_mean, w_gate_in, w_gate_out):
    hidden_gate = jax.nn.gelu(jnp.dot(sample_mean, w_gate_in, precision=highest), approximate=False)
    return jnp.tanh(jnp.dot(hidden_gate, w_gate_out, precision=highest))


def gelu_exact(inputs):
    return jax.nn.gelu(inputs, approximate=False)


def attend(items):
    query_heads, key_heads, value_heads = items
    scores = jnp.einsum(
        "qhe,she->hqs", query_heads, key_heads, preferred_element_type=jnp.float32
    ) * HEAD ** (-0.5)
    largest = jnp.max(scores, axis=-1, keepdims=True)
    lifted = jnp.exp(scores - largest)
    summed = jnp.sum(lifted, axis=-1, keepdims=True)
    soft_weights = (lifted / summed).astype(jnp.bfloat16)
    attended = jnp.einsum(
        "hqs,she->qhe", soft_weights, value_heads, preferred_element_type=jnp.float32
    )
    return (attended.astype(jnp.bfloat16), largest + jnp.log(summed))


def attend_back(items):
    query_heads, key_heads, value_heads, log_total, d_attended = items
    scores = jnp.einsum(
        "qhe,she->hqs", query_heads, key_heads, preferred_element_type=jnp.float32
    ) * HEAD ** (-0.5)
    soft_full = jnp.exp(scores - log_total)
    soft_weights = soft_full.astype(jnp.bfloat16)
    d_value_heads = jnp.einsum(
        "hqs,qhe->she", soft_weights, d_attended, preferred_element_type=jnp.float32
    ).astype(jnp.bfloat16)
    d_soft = jnp.einsum("qhe,she->hqs", d_attended, value_heads, preferred_element_type=jnp.float32)
    inner = jnp.sum(soft_full * d_soft, axis=-1, keepdims=True)
    d_scores = (soft_full * (d_soft - inner) * HEAD ** (-0.5)).astype(jnp.bfloat16)
    d_query_heads = jnp.einsum(
        "hqs,she->qhe", d_scores, key_heads, preferred_element_type=jnp.float32
    ).astype(jnp.bfloat16)
    d_key_heads = jnp.einsum(
        "hqs,qhe->she", d_scores, query_heads, preferred_element_type=jnp.float32
    ).astype(jnp.bfloat16)
    return (d_query_heads, d_key_heads, d_value_heads)


def token_sum(values_in):
    return jnp.sum(values_in.astype(jnp.float32), axis=(0, 1))


def shards(
    tokens,
    features,
    sample_of,
    cotangent,
    ln1_gain,
    ln1_bias,
    w_qkv,
    bias_qv,
    w_attn_out,
    bias_attn_out,
    ln2_gain,
    ln2_bias,
    w_fc1,
    bias_fc1,
    w_fc2,
    bias_fc2,
    w_proj,
    bias_proj,
    w_depth,
    bias_depth,
    w_gate_in,
    w_gate_out,
):
    (
        full_ln1_gain,
        full_ln1_bias,
        full_qkv,
        full_bias_qv,
        full_attn_out,
        full_bias_out,
        full_ln2_gain,
        full_ln2_bias,
        full_fc1,
        full_bias_fc1,
        full_fc2,
        full_bias_fc2,
        full_proj,
        full_bias_proj,
        full_depth,
        full_bias_depth,
        full_gate_in,
        full_gate_out,
    ) = (
        lax.all_gather(ln1_gain, ("img", "ch"), axis=0, tiled=True),
        lax.all_gather(ln1_bias, ("img", "ch"), axis=0, tiled=True),
        lax.all_gather(w_qkv, ("img", "ch"), axis=0, tiled=True),
        lax.all_gather(bias_qv, ("img", "ch"), axis=0, tiled=True),
        lax.all_gather(w_attn_out, ("img", "ch"), axis=0, tiled=True),
        lax.all_gather(bias_attn_out, ("img", "ch"), axis=0, tiled=True),
        lax.all_gather(ln2_gain, ("img", "ch"), axis=0, tiled=True),
        lax.all_gather(ln2_bias, ("img", "ch"), axis=0, tiled=True),
        lax.all_gather(w_fc1, ("img", "ch"), axis=0, tiled=True),
        lax.all_gather(bias_fc1, ("img", "ch"), axis=0, tiled=True),
        lax.all_gather(w_fc2, ("img", "ch"), axis=0, tiled=True),
        lax.all_gather(bias_fc2, ("img", "ch"), axis=0, tiled=True),
        lax.all_gather(w_proj, ("img", "ch"), axis=0, tiled=True),
        lax.all_gather(bias_proj, ("img", "ch"), axis=0, tiled=True),
        lax.all_gather(w_depth, ("img", "ch"), axis=1, tiled=True),
        lax.all_gather(bias_depth, ("img", "ch"), axis=0, tiled=True),
        lax.all_gather(w_gate_in, ("img", "ch"), axis=0, tiled=True),
        lax.all_gather(w_gate_out, ("img", "ch"), axis=1, tiled=True),
    )
    count_images = tokens.shape[0]
    length_tok = tokens.shape[1]
    model_width = tokens.shape[2]
    heads_count = model_width // HEAD
    head_shape = (count_images, length_tok, heads_count, HEAD)
    reach = (3 + count_images - 1) // count_images
    inputs32 = tokens.astype(jnp.float32)
    normed1 = layer_norm(
        inputs32, full_ln1_gain.astype(jnp.float32), full_ln1_bias.astype(jnp.float32)
    ).astype(jnp.bfloat16)
    mixed_qkv = jnp.einsum("kpd,de->kpe", normed1, full_qkv, preferred_element_type=jnp.float32)
    bias_pair = full_bias_qv.astype(jnp.float32)
    query_heads = (
        (mixed_qkv[..., :model_width] + bias_pair[:model_width])
        .astype(jnp.bfloat16)
        .reshape(head_shape)
    )
    key_heads = (
        mixed_qkv[..., model_width : 2 * model_width].astype(jnp.bfloat16).reshape(head_shape)
    )
    value_heads = (
        (mixed_qkv[..., 2 * model_width :] + bias_pair[model_width:])
        .astype(jnp.bfloat16)
        .reshape(head_shape)
    )
    attended, log_total = lax.map(attend, (query_heads, key_heads, value_heads))
    attended = attended.reshape(count_images, length_tok, model_width)
    first_sum = (
        inputs32
        + jnp.einsum("kpd,de->kpe", attended, full_attn_out, preferred_element_type=jnp.float32)
        + full_bias_out.astype(jnp.float32)
    )
    normed2 = layer_norm(
        first_sum, full_ln2_gain.astype(jnp.float32), full_ln2_bias.astype(jnp.float32)
    ).astype(jnp.bfloat16)
    pre_act = jnp.einsum(
        "kpd,df->kpf", normed2, full_fc1, preferred_element_type=jnp.float32
    ) + full_bias_fc1.astype(jnp.float32)
    activation = gelu_exact(pre_act).astype(jnp.bfloat16)
    second_sum = (
        first_sum
        + jnp.einsum("kpf,fd->kpd", activation, full_fc2, preferred_element_type=jnp.float32)
        + full_bias_fc2.astype(jnp.float32)
    )
    pool_weights = pool_table(PS, FS).T.astype(jnp.bfloat16)
    local_pooled = jnp.einsum(
        "kcf,fp->kcp", features, pool_weights, preferred_element_type=jnp.float32
    ).astype(jnp.bfloat16)
    pooled = lax.all_to_all(local_pooled, "ch", split_axis=0, concat_axis=1, tiled=True)
    projected = jnp.einsum(
        "kcp,cd->kpd", pooled, full_proj, preferred_element_type=jnp.float32
    ) + full_bias_proj.astype(jnp.float32)
    spatial = depth_filter(
        projected, full_depth.astype(jnp.float32), full_bias_depth.astype(jnp.float32)
    )
    row_sums = jnp.sum(spatial, axis=1)
    ids_plus = sample_of.astype(jnp.float32) + 1.0
    near_sums = [row_sums]
    near_ids = [ids_plus]
    for offset in range(1, reach + 1):
        for sign in (1, -1):
            moved_sums, moved_ids = shifted((row_sums, ids_plus), ("img", "ch"), sign * offset)
            near_sums.append(moved_sums)
            near_ids.append(moved_ids)
    all_sums = jnp.concatenate(near_sums, axis=0)
    all_ids = jnp.concatenate(near_ids, axis=0)
    match = (ids_plus[:, None] == all_ids[None, :]).astype(jnp.float32)
    counts = jnp.sum(match, axis=1, keepdims=True)
    sample_mean = jnp.dot(match, all_sums, precision=highest) / (counts * length_tok)
    gate_values, gate_back = jax.vjp(
        gate_of, sample_mean, full_gate_in.astype(jnp.float32), full_gate_out.astype(jnp.float32)
    )
    layer_out = (second_sum + gate_values[:, None, :] * spatial).astype(jnp.bfloat16)
    gate_total = lax.psum(jnp.sum(gate_values), ("img", "ch"))
    gate_mean = gate_total / (lax.axis_size(("img", "ch")) * count_images * model_width)
    d_output = cotangent.astype(jnp.float32)
    d_gate = jnp.sum(d_output * spatial, axis=1)
    d_mean, d_gate_in, d_gate_out = gate_back(d_gate)
    near_dmean = [d_mean]
    for offset in range(1, reach + 1):
        for sign in (1, -1):
            near_dmean.append(shifted(d_mean, ("img", "ch"), sign * offset))
    all_dmean = jnp.concatenate(near_dmean, axis=0)
    d_rows = jnp.dot(match, all_dmean, precision=highest) / (counts * length_tok)
    d_spatial = d_output * gate_values[:, None, :] + d_rows[:, None, :]
    depth_primal, depth_back = jax.vjp(
        depth_filter, projected, full_depth.astype(jnp.float32), full_bias_depth.astype(jnp.float32)
    )
    d_projected, d_depth, d_bias_depth = depth_back(d_spatial)
    d_projected = d_projected.astype(jnp.bfloat16)
    d_bias_proj = token_sum(d_projected)
    d_proj = jnp.einsum("kcp,kpd->cd", pooled, d_projected, preferred_element_type=jnp.float32)
    d_pooled = jnp.einsum(
        "kpd,cd->kcp", d_projected, full_proj, preferred_element_type=jnp.float32
    ).astype(jnp.bfloat16)
    d_local = lax.all_to_all(d_pooled, "ch", split_axis=1, concat_axis=0, tiled=True)
    grad_features = jnp.einsum(
        "kcp,fp->kcf", d_local, pool_weights, preferred_element_type=jnp.float32
    ).astype(jnp.bfloat16)
    d_bias_fc2 = jnp.sum(d_output, axis=(0, 1))
    d_fc2 = jnp.einsum("kpf,kpd->fd", activation, cotangent, preferred_element_type=jnp.float32)
    d_activation = jnp.einsum(
        "kpd,fd->kpf", cotangent, full_fc2, preferred_element_type=jnp.float32
    )
    gelu_primal, gelu_back = jax.vjp(gelu_exact, pre_act)
    d_pre = gelu_back(d_activation)[0].astype(jnp.bfloat16)
    d_bias_fc1 = token_sum(d_pre)
    d_fc1 = jnp.einsum("kpd,kpf->df", normed2, d_pre, preferred_element_type=jnp.float32)
    d_normed2 = jnp.einsum("kpf,df->kpd", d_pre, full_fc1, preferred_element_type=jnp.float32)
    norm_primal, norm_two_back = jax.vjp(
        layer_norm, first_sum, full_ln2_gain.astype(jnp.float32), full_ln2_bias.astype(jnp.float32)
    )
    d_first_norm, d_ln2_gain, d_ln2_bias = norm_two_back(d_normed2)
    d_first = d_output + d_first_norm
    d_branch = d_first.astype(jnp.bfloat16)
    d_bias_out = token_sum(d_branch)
    d_attn_out = jnp.einsum("kpd,kpe->de", attended, d_branch, preferred_element_type=jnp.float32)
    d_attended = (
        jnp.einsum("kpe,de->kpd", d_branch, full_attn_out, preferred_element_type=jnp.float32)
        .astype(jnp.bfloat16)
        .reshape(head_shape)
    )
    d_query_heads, d_key_heads, d_value_heads = lax.map(
        attend_back, (query_heads, key_heads, value_heads, log_total, d_attended)
    )
    flat_shape = (count_images, length_tok, model_width)
    d_query_flat = d_query_heads.reshape(flat_shape)
    d_value_flat = d_value_heads.reshape(flat_shape)
    d_bias_qv = jnp.concatenate([token_sum(d_query_flat), token_sum(d_value_flat)])
    d_mixed = jnp.concatenate(
        [d_query_flat, d_key_heads.reshape(flat_shape), d_value_flat], axis=-1
    )
    d_qkv = jnp.einsum("kpd,kpe->de", normed1, d_mixed, preferred_element_type=jnp.float32)
    d_normed1 = jnp.einsum("kpe,de->kpd", d_mixed, full_qkv, preferred_element_type=jnp.float32)
    norm_one_primal, norm_one_back = jax.vjp(
        layer_norm, inputs32, full_ln1_gain.astype(jnp.float32), full_ln1_bias.astype(jnp.float32)
    )
    d_input_norm, d_ln1_gain, d_ln1_bias = norm_one_back(d_normed1)
    grad_tokens = (d_first + d_input_norm).astype(jnp.bfloat16)
    (
        g_ln1_gain,
        g_ln1_bias,
        g_qkv,
        g_bias_qv,
        g_attn_out,
        g_bias_out,
        g_ln2_gain,
        g_ln2_bias,
        g_fc1,
        g_bias_fc1,
        g_fc2,
        g_bias_fc2,
        g_proj,
        g_bias_proj,
        g_depth,
        g_bias_depth,
        g_gate_in,
        g_gate_out,
    ) = (
        lax.psum_scatter(d_ln1_gain, ("img", "ch"), scatter_dimension=0, tiled=True),
        lax.psum_scatter(d_ln1_bias, ("img", "ch"), scatter_dimension=0, tiled=True),
        lax.psum_scatter(d_qkv, ("img", "ch"), scatter_dimension=0, tiled=True),
        lax.psum_scatter(d_bias_qv, ("img", "ch"), scatter_dimension=0, tiled=True),
        lax.psum_scatter(d_attn_out, ("img", "ch"), scatter_dimension=0, tiled=True),
        lax.psum_scatter(d_bias_out, ("img", "ch"), scatter_dimension=0, tiled=True),
        lax.psum_scatter(d_ln2_gain, ("img", "ch"), scatter_dimension=0, tiled=True),
        lax.psum_scatter(d_ln2_bias, ("img", "ch"), scatter_dimension=0, tiled=True),
        lax.psum_scatter(d_fc1, ("img", "ch"), scatter_dimension=0, tiled=True),
        lax.psum_scatter(d_bias_fc1, ("img", "ch"), scatter_dimension=0, tiled=True),
        lax.psum_scatter(d_fc2, ("img", "ch"), scatter_dimension=0, tiled=True),
        lax.psum_scatter(d_bias_fc2, ("img", "ch"), scatter_dimension=0, tiled=True),
        lax.psum_scatter(d_proj, ("img", "ch"), scatter_dimension=0, tiled=True),
        lax.psum_scatter(d_bias_proj, ("img", "ch"), scatter_dimension=0, tiled=True),
        lax.psum_scatter(d_depth, ("img", "ch"), scatter_dimension=1, tiled=True),
        lax.psum_scatter(d_bias_depth, ("img", "ch"), scatter_dimension=0, tiled=True),
        lax.psum_scatter(d_gate_in, ("img", "ch"), scatter_dimension=0, tiled=True),
        lax.psum_scatter(d_gate_out, ("img", "ch"), scatter_dimension=1, tiled=True),
    )
    return (
        layer_out,
        grad_tokens,
        grad_features,
        g_ln1_gain,
        g_ln1_bias,
        g_qkv,
        g_bias_qv,
        g_attn_out,
        g_bias_out,
        g_ln2_gain,
        g_ln2_bias,
        g_fc1,
        g_bias_fc1,
        g_fc2,
        g_bias_fc2,
        g_proj,
        g_bias_proj,
        g_depth,
        g_bias_depth,
        g_gate_in,
        g_gate_out,
        gate_mean,
    )


def solution(mesh):
    return jax.shard_map(
        shards,
        mesh=mesh,
        in_specs=(
            P(("img", "ch"), None, None),
            P("img", "ch", None),
            P(("img", "ch")),
            P(("img", "ch"), None, None),
            P(("img", "ch")),
            P(("img", "ch")),
            P(("img", "ch"), None),
            P(("img", "ch")),
            P(("img", "ch"), None),
            P(("img", "ch")),
            P(("img", "ch")),
            P(("img", "ch")),
            P(("img", "ch"), None),
            P(("img", "ch")),
            P(("img", "ch"), None),
            P(("img", "ch")),
            P(("img", "ch"), None),
            P(("img", "ch")),
            P(None, ("img", "ch")),
            P(("img", "ch")),
            P(("img", "ch"), None),
            P(None, ("img", "ch")),
        ),
        out_specs=(
            P(("img", "ch"), None, None),
            P(("img", "ch"), None, None),
            P("img", "ch", None),
            P(("img", "ch")),
            P(("img", "ch")),
            P(("img", "ch"), None),
            P(("img", "ch")),
            P(("img", "ch"), None),
            P(("img", "ch")),
            P(("img", "ch")),
            P(("img", "ch")),
            P(("img", "ch"), None),
            P(("img", "ch")),
            P(("img", "ch"), None),
            P(("img", "ch")),
            P(("img", "ch"), None),
            P(("img", "ch")),
            P(None, ("img", "ch")),
            P(("img", "ch")),
            P(("img", "ch"), None),
            P(None, ("img", "ch")),
            P(),
        ),
        check_vma=False,
    )
```

profile of v0, /device:TPU:9, one launch (start us, length us, event | category | flops | bytes accessed | tf_op | source)
XLA Modules:
  0.0 1860.7 jit_solution(16170474861311934529)
XLA Ops:
  50.6 52.3 %all-gather.1 = bf16[32,32,9]{1,2,0:T(8,128)(2,1)S(1)} all-gather(bf16[1,32,9]{1,2,0:T(8,128)(2,1)S(1)} %bitcast.280), channel_id=1, replica_groups=mesh['img'=8,'ch'=4] {'img','ch'}, dimensions={0}, use_global_device_ids=true | all-gather | bytes 19008 | tf_op jit(solution)/shard_map/all_gather | solution.py:163
  105.1 44.8 %all-reduce.39 = (bf16[1024]{0:T(1024)(128)(2,1)S(1)}, bf16[1024]{0:T(1024)(128)(2,1)S(1)}, bf16[2048]{0:T(1024)(128)(2,1)S(1)}, bf16[1024]{0:T(1024)(128)(2,1)S...) all-reduce(bf16[1024]{0:T(1024)(128)(2,1)S(1)} %dynamic-update-slic, ...), channel_id=1, replica_groups=mesh['img'=8,'ch'=4] {'img','ch'}, use_global_device_ids=true, to_apply=%add.20 | all-reduce | flops 10240 | bytes 40960
  164.7 31.0 %all-gather = bf16[32,1,128]{2,1,0:T(2,128)(2,1)S(1)} all-gather(bf16[1,1,128]{2,1,0:T(2,128)(2,1)S(1)} %bitcast.281), channel_id=1, replica_groups=mesh['img'=8,'ch'=4] {'img','ch'}, dimensions={0}, use_global_device_ids=true | all-gather | bytes 8448 | tf_op jit(solution)/shard_map/all_gather | solution.py:158
  234.6 24.1 %all-gather.10.cloned.1.call-done = bf16[1024,3072]{1,0:T(8,128)(2,1)} async-done(((bf16[32,3072]{1,0:T(8,128)(2,1)}), bf16[1024,3072]{1,0:T(8,128)(2,1)}) %all-gather.10.cloned.1.call-update) | async-done | bytes 6291472 | tf_op jit(solution)/shard_map/all_gather | solution.py:151
  273.8 9.6 multiply_reduce_fusion.1
  283.4 10.3 fusion.2
  293.8 11.2 fusion.57
  305.0 10.4 all-gather.12.cloned.1.call-done
  319.7 75.8 %all-gather.14.cloned.1.call-done = bf16[1024,4096]{1,0:T(8,128)(2,1)} async-done(((bf16[32,4096]{1,0:T(8,128)(2,1)}), bf16[1024,4096]{1,0:T(8,128)(2,1)}) %all-gather.14.cloned.1.call-update) | async-done | bytes 8388624 | tf_op jit(solution)/shard_map/all_gather | solution.py:157
  395.5 30.5 %multiply_convert_fusion.2 = (bf16[576,4096]{1,0:T(8,128)(2,1)}, f32[576,4096]{1,0:T(8,128)}, f32[576,4096]{1,0:T(8,128)}) fusion(f32[4096]{0:T(1024)S(1)} %bitcast.262, bf16[1024,4096]{1,0:T(8,128)(2,1)} %all-gather.14.cloned.1.call-done, f32[1,576,1024]{2,1,0:T(8,128)S(1)} %get-tuple-element.145, f32[1024]{0:T(1024)S(1)} %convert_element_type.225, ...), kind=kOutput, calls=%fused_computation.18 | convolution fusion | flops 4990500864 | bytes 34370048 | tf_op jit(solution)/shard_map/kpd,df->kpf/dot_general | solution.py:203
  426.0 48.6 %all-gather.16.cloned.1.call-done = bf16[4096,1024]{1,0:T(8,128)(2,1)} async-done(((bf16[128,1024]{1,0:T(8,128)(2,1)}), bf16[4096,1024]{1,0:T(8,128)(2,1)}) %all-gather.16.cloned.1.call-update) | async-done | bytes 8388624 | tf_op jit(solution)/shard_map/all_gather | solution.py:159
  474.6 15.5 convert_reduce_fusion
  490.1 10.4 fusion.41
  527.3 12.8 fusion.117
  540.1 13.4 convert_reduce_fusion.3
  553.6 32.9 %fusion.51 = bf16[16,64,576]{2,1,0:T(8,128)(2,1)} fusion(bf16[576,16,64]{0,2,1:T(8,128)(2,1)} %bitcast.219, f32[16,576,576]{1,2,0:T(8,128)} %fusion.117, f32[16,576]{1,0:T(8,128)S(1)} %log_add_fusion, f32[16,576,576]{1,2,0:T(8,128)} %get-tuple-element.143, bf16[576,16,64]{0,2,1:T(8,128)(2,1)} %bitcast.212, bf16[576,16,64]{0,2,1:T(8,128)(2,1)} %bitcast.221), kind=kOutput, calls=%fused_computation.115 | convolution fusion | flops 1407329792 | bytes 47222784 | tf_op jit(solution)/shard_map/while/body/eval_jaxpr/hqs,qhe->she/dot_general | solution.py:95
  586.4 33.5 %convert_reduce_fusion.4 = (f32[16,64]{1,0:T(8,128)S(1)}, bf16[16,64,576]{2,1,0:T(8,128)(2,1)}) fusion(bf16[576,16,64]{0,2,1:T(8,128)(2,1)} %bitcast.217, f32[16,576,576]{1,2,0:T(8,128)} %fusion.117, f32[16,576]{1,0:T(8,128)S(1)} %log_add_fusion, f32[16,576,576]{1,2,0:T(8,128)} %get-tuple-element.143, bf16[576,16,64]{0,2,1:T(8,128)(2,1)} %bitcast.213, ...), kind=kOutput, calls=%fused_computation.63 | convolution fusion | flops 1408508416 | bytes 47226880 | tf_op jit(solution)/shard_map/while/body/eval_jaxpr/hqs,she->qhe/dot_general | solution.py:92
  620.0 8.8 fusion.33
  680.4 12.4 fusion.46
  692.9 12.8 fusion.101
  705.9 12.2 fusion.64
  728.2 8.8 copy.115
  737.5 14.0 reduce.35
  764.9 10.1 fusion.45
  775.0 43.9 %all-reduce.38 = (f32[1024]{0:T(1024)S(1)}, f32[1024]{0:T(1024)S(1)}, f32[2048]{0:T(1024)S(1)}, f32[1024]{0:T(1024)S(1)}, f32[1024]{0:T(1024)S(1)}, /*index=5*/f...) all-reduce(f32[1024]{0:T(1024)S(1)} %get-tuple-element.77, ...), channel_id=2, replica_groups=mesh['img'=8,'ch'=4] {'img','ch'}, use_global_device_ids=true, to_apply=%region_15.16.clone | all-reduce | flops 14337 | bytes 114696
  838.9 60.6 %reduce-scatter.21.cloned.1.call-done = f32[32,512]{1,0:T(8,128)} async-done(((f32[1024,512]{1,0:T(8,128)}), f32[32,512]{1,0:T(8,128)}) %reduce-scatter.21.cloned.1.call-update) | async-done | bytes 65552 | tf_op jit(solution)/shard_map/reduce_scatter | solution.py:343
  899.5 135.3 %reduce-scatter.23.cloned.1.call-done = f32[512,32]{0,1:T(8,128)} async-done(((f32[512,1024]{0,1:T(8,128)}), f32[512,32]{0,1:T(8,128)}) %reduce-scatter.23.cloned.1.call-update) | async-done | bytes 65552 | tf_op jit(solution)/shard_map/reduce_scatter | solution.py:344
  1034.8 139.9 %reduce-scatter.13.cloned.1.call-done = f32[32,1024]{1,0:T(8,128)} async-done(((f32[1024,1024]{1,0:T(8,128)}), f32[32,1024]{1,0:T(8,128)}) %reduce-scatter.13.cloned.1.call-update) | async-done | bytes 131088 | tf_op jit(solution)/shard_map/reduce_scatter | solution.py:331
  1174.8 139.8 %reduce-scatter.19.cloned.1.call-done = f32[48,1024]{1,0:T(8,128)} async-done(((f32[1536,1024]{1,0:T(8,128)}), f32[48,1024]{1,0:T(8,128)}) %reduce-scatter.19.cloned.1.call-update) | async-done | bytes 196624 | tf_op jit(solution)/shard_map/reduce_scatter | solution.py:339
  1314.5 161.4 %reduce-scatter.11.cloned.1.call-done = f32[32,3072]{1,0:T(8,128)} async-done(((f32[1024,3072]{1,0:T(8,128)}), f32[32,3072]{1,0:T(8,128)}) %reduce-scatter.11.cloned.1.call-update) | async-done | bytes 393232 | tf_op jit(solution)/shard_map/reduce_scatter | solution.py:329
  1475.9 189.4 %reduce-scatter.15.cloned.1.call-done = f32[32,4096]{1,0:T(8,128)} async-done(((f32[1024,4096]{1,0:T(8,128)}), f32[32,4096]{1,0:T(8,128)}) %reduce-scatter.15.cloned.1.call-update) | async-done | bytes 524304 | tf_op jit(solution)/shard_map/reduce_scatter | solution.py:335
  1665.3 187.4 %reduce-scatter.17.cloned.1.call-done = f32[128,1024]{1,0:T(8,128)} async-done(((f32[4096,1024]{1,0:T(8,128)}), f32[128,1024]{1,0:T(8,128)}) %reduce-scatter.17.cloned.1.call-update) | async-done | bytes 524304 | tf_op jit(solution)/shard_map/reduce_scatter | solution.py:337
  (342 shorter events, 238.3 us)
Async XLA Ops:
  7.2 145.2 %all-gather.18.cloned.1.call-start = ((), (), s32[]{:S(2)}) async-start(), calls=%async_computation.14 | async-start | bytes 3244032 | tf_op jit(solution)/shard_map/all_gather | solution.py:161
  7.9 221.6 %all-gather.20.cloned.1.call-start = ((), (), s32[]{:S(2)}) async-start(), calls=%async_computation.15 | async-start | bytes 1081344 | tf_op jit(solution)/shard_map/all_gather | solution.py:165
  8.7 223.2 %all-gather.22.cloned.1.call-start = ((), (), s32[]{:S(2)}) async-start(), calls=%async_computation.16 | async-start | bytes 1081344 | tf_op jit(solution)/shard_map/all_gather | solution.py:166
  9.4 249.3 %all-gather.10.cloned.1.call-start = ((), (), s32[]{:S(2)}) async-start(), calls=%async_computation.10 | async-start | bytes 6488064 | tf_op jit(solution)/shard_map/all_gather | solution.py:151
  10.0 305.4 %all-gather.12.cloned.1.call-start = ((), (), s32[]{:S(2)}) async-start(), calls=%async_computation.11 | async-start | bytes 2162688 | tf_op jit(solution)/shard_map/all_gather | solution.py:153
  10.6 384.9 %all-gather.14.cloned.1.call-start = ((), (), s32[]{:S(2)}) async-start(), calls=%async_computation.12 | async-start | bytes 8650752 | tf_op jit(solution)/shard_map/all_gather | solution.py:157
  11.8 183.9 %collective-permute-start.5 = (f32[1]{0:T(128)}, f32[1]{0:T(128)}, u32[]{:S(2)}, u32[]{:S(2)}) collective-permute-start(f32[1]{0:T(128)} %add.324), channel_id=1, source_target_pairs={{3,0},{4,1},{5,2},{6,3},{7,4},{8,5},{9,6},{10,7},{11,8},{12,9},{13... | collective-permute-start | bytes 20 | tf_op jit(solution)/shard_map/ppermute | solution.py:18
  17.0 181.8 %collective-permute-start.4 = (f32[1]{0:T(128)}, f32[1]{0:T(128)}, u32[]{:S(2)}, u32[]{:S(2)}) collective-permute-start(f32[1]{0:T(128)} %add.324), channel_id=1, source_target_pairs={{0,3},{1,4},{2,5},{3,6},{4,7},{5,8},{6,9},{7,10},{8,11},{9,12},{10... | collective-permute-start | bytes 20 | tf_op jit(solution)/shard_map/ppermute | solution.py:18
  19.7 183.6 %collective-permute-start.3 = (f32[1]{0:T(128)}, f32[1]{0:T(128)}, u32[]{:S(2)}, u32[]{:S(2)}) collective-permute-start(f32[1]{0:T(128)} %add.324), channel_id=1, source_target_pairs={{2,0},{3,1},{4,2},{5,3},{6,4},{7,5},{8,6},{9,7},{10,8},{11,9},{12,... | collective-permute-start | bytes 20 | tf_op jit(solution)/shard_map/ppermute | solution.py:18
  24.9 178.4 %collective-permute-start.2 = (f32[1]{0:T(128)}, f32[1]{0:T(128)}, u32[]{:S(2)}, u32[]{:S(2)}) collective-permute-start(f32[1]{0:T(128)} %add.324), channel_id=1, source_target_pairs={{0,2},{1,3},{2,4},{3,5},{4,6},{5,7},{6,8},{7,9},{8,10},{9,11},{10,... | collective-permute-start | bytes 20 | tf_op jit(solution)/shard_map/ppermute | solution.py:18
  43.1 107.9 %all-to-all-start = ((bf16[4,384,576]{1,2,0:T(8,128)(2,1)}), bf16[4,384,576]{1,2,0:T(8,128)(2,1)S(1)}, u32[]{:S(2)}, u32[]{:S(2)}) async-start(bf16[4,384,576]{1,2,0:T(8,128)(2,1)} %convert_bitcast_fusion), calls=%async_computation | async-start | bytes 3538944 | tf_op jit(solution)/shard_map/all_to_all | solution.py:216
  49.8 424.7 %all-gather.16.cloned.1.call-start = ((), (), s32[]{:S(2)}) async-start(), calls=%async_computation.13 | async-start | bytes 8650752 | tf_op jit(solution)/shard_map/all_gather | solution.py:159
  50.6 774.8 %reduce-scatter.25.cloned.1.call-start = ((), (), s32[]{:S(2)}) async-start(), calls=%async_computation.24 | async-start | bytes 540672
  161.9 59.9 %collective-permute-start.11 = (f32[1,1024]{1,0:T(1,128)S(1)}, f32[1,1024]{1,0:T(1,128)S(1)}, u32[]{:S(2)}, u32[]{:S(2)}) collective-permute-start(f32[1,1024]{1,0:T(1,128)S(1)} %bitcast.264), channel_id=1, source_target_pairs={{3,0},{4,1},{5,2},{6,3},{7,4},{8,5},{9,6},{10,7},{11,8},{12,9},{13... | collective-permute-start | bytes 12296 | tf_op jit(solution)/shard_map/ppermute | solution.py:18
  195.8 7.6 collective-permute-start.1
  208.0 21.0 %collective-permute-start.10 = (f32[1,1024]{1,0:T(1,128)S(1)}, f32[1,1024]{1,0:T(1,128)S(1)}, u32[]{:S(2)}, u32[]{:S(2)}) collective-permute-start(f32[1,1024]{1,0:T(1,128)S(1)} %bitcast.265), channel_id=1, source_target_pairs={{0,3},{1,4},{2,5},{3,6},{4,7},{5,8},{6,9},{7,10},{8,11},{9,12},{10... | collective-permute-start | bytes 12296 | tf_op jit(solution)/shard_map/ppermute | solution.py:18
  211.3 17.8 collective-permute-start.9
  215.2 13.8 collective-permute-start.8
  217.2 11.9 collective-permute-start.7
  507.5 123.9 %collective-permute-start.17 = (f32[1,1024]{1,0:T(1,128)S(1)}, f32[1,1024]{1,0:T(1,128)S(1)}, u32[]{:S(2)}, u32[]{:S(2)}) collective-permute-start(f32[1,1024]{1,0:T(1,128)S(1)} %fusion.119), channel_id=1, source_target_pairs={{3,0},{4,1},{5,2},{6,3},{7,4},{8,5},{9,6},{10,7},{11,8},{12,9},{13... | collective-permute-start | bytes 12296 | tf_op jit(solution)/shard_map/ppermute | solution.py:18
  510.7 124.3 %collective-permute-start.16 = (f32[1,1024]{1,0:T(1,128)S(1)}, f32[1,1024]{1,0:T(1,128)S(1)}, u32[]{:S(2)}, u32[]{:S(2)}) collective-permute-start(f32[1,1024]{1,0:T(1,128)S(1)} %fusion.119), channel_id=1, source_target_pairs={{0,3},{1,4},{2,5},{3,6},{4,7},{5,8},{6,9},{7,10},{8,11},{9,12},{10... | collective-permute-start | bytes 12296 | tf_op jit(solution)/shard_map/ppermute | solution.py:18
  513.1 121.9 %collective-permute-start.15 = (f32[1,1024]{1,0:T(1,128)S(1)}, f32[1,1024]{1,0:T(1,128)S(1)}, u32[]{:S(2)}, u32[]{:S(2)}) collective-permute-start(f32[1,1024]{1,0:T(1,128)S(1)} %fusion.119), channel_id=1, source_target_pairs={{2,0},{3,1},{4,2},{5,3},{6,4},{7,5},{8,6},{9,7},{10,8},{11,9},{12,... | collective-permute-start | bytes 12296 | tf_op jit(solution)/shard_map/ppermute | solution.py:18
  517.0 118.0 %collective-permute-start.14 = (f32[1,1024]{1,0:T(1,128)S(1)}, f32[1,1024]{1,0:T(1,128)S(1)}, u32[]{:S(2)}, u32[]{:S(2)}) collective-permute-start(f32[1,1024]{1,0:T(1,128)S(1)} %fusion.119), channel_id=1, source_target_pairs={{0,2},{1,3},{2,4},{3,5},{4,6},{5,7},{6,8},{7,9},{8,10},{9,11},{10,... | collective-permute-start | bytes 12296 | tf_op jit(solution)/shard_map/ppermute | solution.py:18
  518.9 116.1 %collective-permute-start.13 = (f32[1,1024]{1,0:T(1,128)S(1)}, f32[1,1024]{1,0:T(1,128)S(1)}, u32[]{:S(2)}, u32[]{:S(2)}) collective-permute-start(f32[1,1024]{1,0:T(1,128)S(1)} %fusion.119), channel_id=1, source_target_pairs={{1,0},{2,1},{3,2},{4,3},{5,4},{6,5},{7,6},{8,7},{9,8},{10,9},{11,1... | collective-permute-start | bytes 12296 | tf_op jit(solution)/shard_map/ppermute | solution.py:18
  651.0 248.5 %reduce-scatter.21.cloned.1.call-start = ((), (), s32[]{:S(2)}) async-start(), calls=%async_computation.22 | async-start | bytes 2162688 | tf_op jit(solution)/shard_map/reduce_scatter | solution.py:343
  652.6 382.2 %reduce-scatter.23.cloned.1.call-start = ((), (), s32[]{:S(2)}) async-start(), calls=%async_computation.23 | async-start | bytes 2162688 | tf_op jit(solution)/shard_map/reduce_scatter | solution.py:344
  654.2 520.5 %reduce-scatter.13.cloned.1.call-start = ((), (), s32[]{:S(2)}) async-start(), calls=%async_computation.18 | async-start | bytes 4325376 | tf_op jit(solution)/shard_map/reduce_scatter | solution.py:331
  660.1 654.4 %reduce-scatter.19.cloned.1.call-start = ((), (), s32[]{:S(2)}) async-start(), calls=%async_computation.21 | async-start | bytes 6488064 | tf_op jit(solution)/shard_map/reduce_scatter | solution.py:339
  679.7 796.2 %reduce-scatter.11.cloned.1.call-start = ((), (), s32[]{:S(2)}) async-start(), calls=%async_computation.17 | async-start | bytes 12976128 | tf_op jit(solution)/shard_map/reduce_scatter | solution.py:329
  692.8 972.5 %reduce-scatter.15.cloned.1.call-start = ((), (), s32[]{:S(2)}) async-start(), calls=%async_computation.19 | async-start | bytes 17301504 | tf_op jit(solution)/shard_map/reduce_scatter | solution.py:335
  705.7 1147.0 %reduce-scatter.17.cloned.1.call-start = ((), (), s32[]{:S(2)}) async-start(), calls=%async_computation.20 | async-start | bytes 17301504 | tf_op jit(solution)/shard_map/reduce_scatter | solution.py:337
  756.3 70.5 %all-to-all-start.1 = ((bf16[4,2,110592]{2,1,0:T(2,128)(2,1)}), bf16[4,2,110592]{2,1,0:T(2,128)(2,1)}, u32[]{:S(2)}, u32[]{:S(2)}) async-start(bf16[4,2,110592]{2,1,0:T(2,128)(2,1)} %reshape.1185), calls=%async_computation.1 | async-start | bytes 3538944 | tf_op jit(solution)/shard_map/all_to_all | solution.py:263
  (81 other events, 2664.5 us)
Sparse Core Ops, SparseCore 0:
  10.9 65.5 all-gather.17
  79.4 51.4 all-gather.19
  133.8 52.7 all-gather.21
  189.3 69.3 all-gather.9
  261.4 53.9 all-gather.11
  318.2 77.3 all-gather.13
  398.4 76.1 all-gather.15
  651.1 112.2 reduce-scatter.24
  766.3 133.0 reduce-scatter.20
  902.2 132.6 reduce-scatter.22
  1037.8 136.9 reduce-scatter.12
  1181.8 132.7 reduce-scatter.18
  1321.1 154.7 reduce-scatter.10
  1478.8 186.5 reduce-scatter.14
  1668.1 184.5 reduce-scatter.16
where the time goes:
time: 1870 us; the launch traced here: 1860 us
  waiting for transfers between devices  1180 us (63%)
  matrix products  276 us (15%)
  blocking collectives  172 us (9%)
  starting transfers between devices  76.9 us (4%)
  other arithmetic  72.2 us (4%)
  local copies, waits for them, and re-layouts  65.9 us (4%)
    reduce_scatter x1, waiting for transfers between devices, shards(): lax.psum_scatter(d_fc1, ('img', 'ch'), scatter_dimension=0, tiled=True)  189 us
    reduce_scatter x1, waiting for transfers between devices, shards(): lax.psum_scatter(d_fc2, ('img', 'ch'), scatter_dimension=0, tiled=True)  187 us
    reduce_scatter x1, waiting for transfers between devices, shards(): lax.psum_scatter(d_qkv, ('img', 'ch'), scatter_dimension=0, tiled=True)  161 us
    reduce_scatter x1, waiting for transfers between devices, shards(): lax.psum_scatter(d_attn_out, ('img', 'ch'), scatter_dimension=0, tiled=True)  140 us
    reduce_scatter x1, waiting for transfers between devices, shards(): lax.psum_scatter(d_proj, ('img', 'ch'), scatter_dimension=0, tiled=True)  140 us
    reduce_scatter x1, waiting for transfers between devices, shards(): lax.psum_scatter(d_gate_out, ('img', 'ch'), scatter_dimension=1, tiled=True)  135 us
    unnamed x2, blocking collectives  88.7 us
    all_gather x1, waiting for transfers between devices, shards(): lax.all_gather(w_fc1, ('img', 'ch'), axis=0, tiled=True)  75.8 us
  transfers between devices with their start and end apart: 35, of which 13 were waited for; matrix products, arithmetic and copies ran while one was open for 19% of the time, Pallas kernels for 0%

commit v1 on v0

v1 whole, which is shorter than its diff:
```python
import jax
import jax.numpy as jnp
from jax import lax
from jax.experimental import pallas as pl
from jax.experimental.pallas import tpu as pltpu
from jax.sharding import PartitionSpec as P

HEAD = 64
PS = 24
FS = 32


norm_eps = 1e-05
highest = lax.Precision.HIGHEST


AXES = ("img", "ch")


class Grid:
    def __init__(self):
        img, ch = lax.axis_size("img"), lax.axis_size("ch")
        depth = 4 if img % 4 == 0 else 1
        self.n = {"z": depth, "x": img // depth, "y": ch // 2, "c": 2}
        self.stride = {"c": 1, "y": 2, "x": ch, "z": ch * (img // depth)}
        self.total = img * ch
        me = lax.axis_index(AXES)
        self.me = me
        self.pos = {a: lax.rem(lax.div(me, self.stride[a]), self.n[a]) for a in self.n}

    def send(self, v, axis, by):
        n, s = self.n[axis], self.stride[axis]
        pairs = []
        for i in range(self.total):
            a = (i // s) % n
            pairs.append((i, i + ((a + by) % n - a) * s))
        return lax.ppermute(v, AXES, pairs)

    def other(self, axis, by):
        return lax.rem(self.pos[axis] + by, self.n[axis])


def gather_small(grid, v):
    v = v[None]
    for axis in ("c", "y", "x", "z"):
        n = grid.n[axis]
        got = [v] + [grid.send(v, axis, k) for k in range(1, n)]
        ring = jnp.stack(got[::-1] + got[::-1])
        start = lax.rem(2 * n - 1 - grid.pos[axis], n)
        v = lax.dynamic_slice_in_dim(ring, start, n, 0).reshape(n * v.shape[0], v.shape[1])
    return v


def scatter_small(grid, v):
    for axis in ("c", "y", "x", "z")[::-1]:
        n = grid.n[axis]
        t = v.reshape(n, -1, v.shape[1])
        total = lax.dynamic_index_in_dim(t, grid.pos[axis], 0, keepdims=False)
        for k in range(1, n):
            total = total + grid.send(
                lax.dynamic_index_in_dim(t, grid.other(axis, k), 0, keepdims=False), axis, k
            )
        v = total
    return v[0]


def gather_pieces(grid, shard):
    r, width = shard.shape
    h, q = width // 2, width // 4
    c = grid.pos["c"]
    mine = lax.dynamic_slice(shard, (0, c * h), (r, h))
    theirs = lax.dynamic_slice(shard, (0, (1 - c) * h), (r, h))
    got = grid.send(theirs, "c", 1)
    both = jnp.where(
        c == 0, jnp.concatenate([mine, got], 0), jnp.concatenate([got, mine], 0)
    )
    along_z = [both] + [grid.send(both, "z", k) for k in range(1, grid.n["z"])]
    out = []
    for part, (first, second) in enumerate((("x", "y"), ("y", "x"))):
        s0 = jnp.stack([p[:, part * q : (part + 1) * q] for p in along_z])
        r1 = [grid.send(s0, first, k) for k in range(1, grid.n[first])]
        s1 = jnp.concatenate([s0] + r1, 0)
        r2 = [grid.send(s1, second, k) for k in range(1, grid.n[second])]
        out.append((first, second, s0, r1, r2))
    return out


def assemble(grid, cores, r, width):
    nz, nx, ny = grid.n["z"], grid.n["x"], grid.n["y"]
    h, q = width // 2, width // 4
    arrays, plan = [], []
    for core_rel, parts in enumerate(cores):
        for part, (first, second, s0, r1, r2) in enumerate(parts):
            for k1, buf in enumerate([s0] + r1):
                for kz in range(nz):
                    plan.append((len(arrays), kz, core_rel, part, kz, {first: k1, second: 0}))
                arrays.append(buf)
            for k2, buf in enumerate(r2, 1):
                for k1 in range(grid.n[first]):
                    for kz in range(nz):
                        rel = {first: k1, second: k2}
                        plan.append((len(arrays), k1 * nz + kz, core_rel, part, kz, rel))
                arrays.append(buf)

    def body(place, *refs):
        ins, out, sem = refs[: len(arrays)], refs[len(arrays)], refs[len(arrays) + 1]
        z, x, y, c = place[0], place[1], place[2], place[3]
        copies = []
        for i, j, core_rel, part, kz, rel in plan:
            zz = lax.rem(z - kz + nz, nz)
            xx = lax.rem(x - rel["x"] + nx, nx)
            yy = lax.rem(y - rel["y"] + ny, ny)
            col = lax.rem(c + core_rel, 2) * h + part * q
            if q % 128 == 0:
                col = pl.multiple_of(col, 128)
            copies.append(
                pltpu.make_async_copy(ins[i].at[j], out.at[zz, xx, yy, :, pl.ds(col, q)], sem)
            )
            copies[-1].start()
        for copy in copies:
            copy.wait()

    place = jnp.stack([grid.pos[a] for a in ("z", "x", "y", "c")]).astype(jnp.int32)
    whole = pl.pallas_call(
        body,
        out_shape=jax.ShapeDtypeStruct((nz, nx, ny, 2 * r, width), jnp.bfloat16),
        in_specs=[pl.BlockSpec(memory_space=pltpu.SMEM)]
        + [pl.BlockSpec(memory_space=pltpu.HBM)] * len(arrays),
        out_specs=pl.BlockSpec(memory_space=pltpu.VMEM),
        scratch_shapes=[pltpu.SemaphoreType.DMA],
        compiler_params=pltpu.CompilerParams(
            vmem_limit_bytes=nz * nx * ny * (2 * r + 16) * width * 2 + (4 << 20)
        ),
        cost_estimate=pl.CostEstimate(
            flops=0, bytes_accessed=nz * nx * ny * 2 * r * width * 4, transcendentals=0
        ),
        name="assemble",
    )(place, *arrays)
    return whole.reshape(nz * nx * ny * 2 * r, width)


def gather(grid, shard):
    own = gather_pieces(grid, shard)

    def over(buf):
        return grid.send(buf, "c", 1)

    away = [
        (first, second, over(s0), [over(b) for b in r1], [over(b) for b in r2])
        for first, second, s0, r1, r2 in own
    ]
    return assemble(grid, [own, away], *shard.shape)


def scatter(grid, mine, theirs, r):
    nz, nx, ny = grid.n["z"], grid.n["x"], grid.n["y"]
    f32 = jnp.float32
    h = mine.shape[1]
    q = h // 2
    got = grid.send(theirs, "c", 1)
    shape = (nz, nx, ny, 2 * r, h)
    base = mine.reshape(shape).astype(f32) + got.reshape(shape).astype(f32)
    parts = []
    for part, (first, second) in enumerate((("y", "x"), ("x", "y"))):
        total = base[..., part * q : (part + 1) * q]
        for axis, dim in ((first, {"x": 1, "y": 2}[first]), (second, 1)):
            t = total
            total = lax.dynamic_index_in_dim(t, grid.pos[axis], dim, keepdims=False)
            for k in range(1, grid.n[axis]):
                piece = lax.dynamic_index_in_dim(t, grid.other(axis, k), dim, keepdims=False)
                total = total + grid.send(piece.astype(jnp.bfloat16), axis, k).astype(f32)
        parts.append(total)
    t = jnp.concatenate(parts, -1)
    total = lax.dynamic_index_in_dim(t, grid.pos["z"], 0, keepdims=False)
    for k in range(1, nz):
        piece = lax.dynamic_index_in_dim(t, grid.other("z", k), 0, keepdims=False)
        total = total + grid.send(piece.astype(jnp.bfloat16), "z", k).astype(f32)
    c = grid.pos["c"]
    own = lax.dynamic_slice(total, (c * r, 0), (r, h))
    away = lax.dynamic_slice(total, ((1 - c) * r, 0), (r, h))
    back = grid.send(away, "c", 1)
    return jnp.where(
        c == 0, jnp.concatenate([own, back], 1), jnp.concatenate([back, own], 1)
    )


def weight_grad(grid, left, right):
    h = right.shape[1] // 2
    c = grid.pos["c"]

    def half(which):
        cols = lax.dynamic_slice(right, (0, which * h), (right.shape[0], h))
        return lax.dot_general(
            left, cols, (((0,), (0,)), ((), ())), preferred_element_type=jnp.float32
        ).astype(jnp.bfloat16)

    theirs = half(1 - c)
    return scatter(grid, half(c), theirs, left.shape[1] // grid.total)


def neighbours(grid, v, reach):
    out = [v]
    for offset in range(1, reach + 1):
        for by in (offset, -offset):
            pairs = [(i, i + by) for i in range(grid.total) if 0 <= i + by < grid.total]
            out.append(lax.ppermute(v, AXES, pairs))
    return out


def layer_norm(inputs, scale_gain, offset_bias):
    centre = jnp.mean(inputs, axis=-1, keepdims=True)
    centred = inputs - centre
    spread = jnp.mean(centred * centred, axis=-1, keepdims=True)
    return centred * lax.rsqrt(spread + norm_eps) * scale_gain + offset_bias


def pool_table(coarse_side, fine_side):
    coarse_index = jnp.arange(coarse_side)[:, None]
    fine_index = jnp.arange(fine_side)[None, :]
    window_start = coarse_index * fine_side // coarse_side
    window_end = ((coarse_index + 1) * fine_side + coarse_side - 1) // coarse_side
    inside = jnp.logical_and(fine_index >= window_start, fine_index < window_end)
    single = jnp.where(inside, 1.0, 0.0).astype(jnp.float32) / (window_end - window_start).astype(
        jnp.float32
    )
    return jnp.kron(single, single)


def depth_filter(projected, kernel, offset_bias):
    count_images = projected.shape[0]
    grid_cells = projected.reshape(count_images, PS, PS, -1)
    padded = jnp.pad(grid_cells, ((0, 0), (1, 1), (1, 1), (0, 0)))
    summed = jnp.zeros_like(grid_cells)
    for tap_row in range(3):
        for tap_col in range(3):
            summed = (
                summed
                + padded[:, tap_row : tap_row + PS, tap_col : tap_col + PS, :]
                * kernel[3 * tap_row + tap_col]
            )
    return summed.reshape(count_images, PS * PS, -1) + offset_bias


def gelu_exact(inputs):
    return jax.nn.gelu(inputs, approximate=False)


def attend(items):
    query_heads, key_heads, value_heads = items
    scores = jnp.einsum(
        "qhe,she->hqs", query_heads, key_heads, preferred_element_type=jnp.float32
    ) * HEAD ** (-0.5)
    largest = jnp.max(scores, axis=-1, keepdims=True)
    lifted = jnp.exp(scores - largest)
    summed = jnp.sum(lifted, axis=-1, keepdims=True)
    soft_weights = (lifted / summed).astype(jnp.bfloat16)
    attended = jnp.einsum(
        "hqs,she->qhe", soft_weights, value_heads, preferred_element_type=jnp.float32
    )
    return (attended.astype(jnp.bfloat16), largest + jnp.log(summed))


def attend_back(items):
    query_heads, key_heads, value_heads, log_total, d_attended = items
    scores = jnp.einsum(
        "qhe,she->hqs", query_heads, key_heads, preferred_element_type=jnp.float32
    ) * HEAD ** (-0.5)
    soft_full = jnp.exp(scores - log_total)
    soft_weights = soft_full.astype(jnp.bfloat16)
    d_value_heads = jnp.einsum(
        "hqs,qhe->she", soft_weights, d_attended, preferred_element_type=jnp.float32
    ).astype(jnp.bfloat16)
    d_soft = jnp.einsum("qhe,she->hqs", d_attended, value_heads, preferred_element_type=jnp.float32)
    inner = jnp.sum(soft_full * d_soft, axis=-1, keepdims=True)
    d_scores = (soft_full * (d_soft - inner) * HEAD ** (-0.5)).astype(jnp.bfloat16)
    d_query_heads = jnp.einsum(
        "hqs,she->qhe", d_scores, key_heads, preferred_element_type=jnp.float32
    ).astype(jnp.bfloat16)
    d_key_heads = jnp.einsum(
        "hqs,qhe->she", d_scores, query_heads, preferred_element_type=jnp.float32
    ).astype(jnp.bfloat16)
    return (d_query_heads, d_key_heads, d_value_heads)


def token_sum(values_in):
    return jnp.sum(values_in.astype(jnp.float32), axis=(0, 1))


def shards(
    tokens,
    features,
    sample_of,
    cotangent,
    ln1_gain,
    ln1_bias,
    w_qkv,
    bias_qv,
    w_attn_out,
    bias_attn_out,
    ln2_gain,
    ln2_bias,
    w_fc1,
    bias_fc1,
    w_fc2,
    bias_fc2,
    w_proj,
    bias_proj,
    w_depth,
    bias_depth,
    w_gate_in,
    w_gate_out,
):
    grid = Grid()
    rows = ln1_gain.shape[0]
    vectors = (
        ("ln1_gain", ln1_gain),
        ("ln1_bias", ln1_bias),
        ("bias_qv", bias_qv),
        ("bias_out", bias_attn_out),
        ("ln2_gain", ln2_gain),
        ("ln2_bias", ln2_bias),
        ("bias_fc1", bias_fc1),
        ("bias_fc2", bias_fc2),
        ("bias_proj", bias_proj),
        ("bias_depth", bias_depth),
        ("depth", w_depth.T.reshape(-1)),
    )
    every = gather_small(grid, jnp.concatenate([v for _, v in vectors])).astype(jnp.float32)
    full, spans, at = {}, {}, 0
    for name, v in vectors:
        spans[name] = (at, at + v.shape[0])
        full[name] = every[:, at : at + v.shape[0]].reshape(-1)
        at += v.shape[0]
    full_ln1_gain, full_ln1_bias, bias_pair = full["ln1_gain"], full["ln1_bias"], full["bias_qv"]
    full_bias_out, full_ln2_gain, full_ln2_bias = full["bias_out"], full["ln2_gain"], full["ln2_bias"]
    full_bias_fc1, full_bias_fc2 = full["bias_fc1"], full["bias_fc2"]
    full_bias_proj, full_bias_depth = full["bias_proj"], full["bias_depth"]
    full_depth = full["depth"].reshape(-1, 9).T
    full_qkv = gather(grid, w_qkv)
    full_proj = gather(grid, w_proj)
    mixed_w = gather(grid, jnp.concatenate([w_attn_out, w_gate_in, w_gate_out.T], 1))
    model_width = tokens.shape[2]
    gate_hidden = w_gate_in.shape[1]
    full_attn_out = mixed_w[:, :model_width]
    full_gate_in = mixed_w[:, model_width : model_width + gate_hidden].astype(jnp.float32)
    full_gate_out = mixed_w[:, model_width + gate_hidden :].astype(jnp.float32).T
    full_fc1 = gather(grid, w_fc1)
    full_fc2 = gather(grid, w_fc2)
    count_images = tokens.shape[0]
    length_tok = tokens.shape[1]
    heads_count = model_width // HEAD
    head_shape = (count_images, length_tok, heads_count, HEAD)
    reach = (3 + count_images - 1) // count_images
    inputs32 = tokens.astype(jnp.float32)
    normed1 = layer_norm(
        inputs32, full_ln1_gain, full_ln1_bias
    ).astype(jnp.bfloat16)
    mixed_qkv = jnp.einsum("kpd,de->kpe", normed1, full_qkv, preferred_element_type=jnp.float32)
    query_heads = (
        (mixed_qkv[..., :model_width] + bias_pair[:model_width])
        .astype(jnp.bfloat16)
        .reshape(head_shape)
    )
    key_heads = (
        mixed_qkv[..., model_width : 2 * model_width].astype(jnp.bfloat16).reshape(head_shape)
    )
    value_heads = (
        (mixed_qkv[..., 2 * model_width :] + bias_pair[model_width:])
        .astype(jnp.bfloat16)
        .reshape(head_shape)
    )
    attended, log_total = lax.map(attend, (query_heads, key_heads, value_heads))
    attended = attended.reshape(count_images, length_tok, model_width)
    first_sum = (
        inputs32
        + jnp.einsum("kpd,de->kpe", attended, full_attn_out, preferred_element_type=jnp.float32)
        + full_bias_out
    )
    normed2 = layer_norm(
        first_sum, full_ln2_gain, full_ln2_bias
    ).astype(jnp.bfloat16)
    pre_act = jnp.einsum(
        "kpd,df->kpf", normed2, full_fc1, preferred_element_type=jnp.float32
    ) + full_bias_fc1
    activation = gelu_exact(pre_act).astype(jnp.bfloat16)
    second_sum = (
        first_sum
        + jnp.einsum("kpf,fd->kpd", activation, full_fc2, preferred_element_type=jnp.float32)
        + full_bias_fc2
    )
    pool_weights = pool_table(PS, FS).T.astype(jnp.bfloat16)
    local_pooled = jnp.einsum(
        "kcf,fp->kcp", features, pool_weights, preferred_element_type=jnp.float32
    ).astype(jnp.bfloat16)
    pooled = lax.all_to_all(local_pooled, "ch", split_axis=0, concat_axis=1, tiled=True)
    projected = jnp.einsum(
        "kcp,cd->kpd", pooled, full_proj, preferred_element_type=jnp.float32
    ) + full_bias_proj
    spatial = depth_filter(
        projected, full_depth, full_bias_depth
    )
    row_sums = jnp.sum(spatial, axis=1)
    ids_plus = sample_of.astype(jnp.float32) + 1.0
    carried = jnp.concatenate([row_sums, jnp.broadcast_to(ids_plus[:, None], (count_images, 128))], 1)
    near = jnp.concatenate(neighbours(grid, carried, reach), axis=0)
    all_sums, all_ids = near[:, :model_width], near[:, model_width]
    match = (ids_plus[:, None] == all_ids[None, :]).astype(jnp.float32)
    counts = jnp.sum(match, axis=1, keepdims=True)
    sample_mean = jnp.dot(match, all_sums, precision=highest) / (counts * length_tok)
    hidden = jnp.dot(sample_mean, full_gate_in, precision=highest)
    gate_act, act_back = jax.vjp(gelu_exact, hidden)
    gate_values = jnp.tanh(jnp.dot(gate_act, full_gate_out, precision=highest))
    layer_out = (second_sum + gate_values[:, None, :] * spatial).astype(jnp.bfloat16)
    d_output = cotangent.astype(jnp.float32)
    d_gate = jnp.sum(d_output * spatial, axis=1)
    d_pre_gate = d_gate * (1.0 - gate_values * gate_values)
    d_hidden = act_back(jnp.dot(d_pre_gate, full_gate_out.T, precision=highest))[0]
    d_mean = jnp.dot(d_hidden, full_gate_in.T, precision=highest)
    gate_sum = jnp.broadcast_to(jnp.sum(gate_values), (128,))
    factors = gather_small(
        grid, jnp.concatenate([sample_mean[0], d_pre_gate[0], d_hidden[0], gate_act[0], gate_sum])
    )
    own_cols = grid.me * rows
    g_gate_in = lax.dot_general(
        lax.dynamic_slice(factors, (0, own_cols), (grid.total, rows)),
        factors[:, 2 * model_width : 2 * model_width + gate_hidden],
        (((0,), (0,)), ((), ())),
        precision=highest,
    )
    g_gate_out = lax.dot_general(
        factors[:, 2 * model_width + gate_hidden : 2 * model_width + 2 * gate_hidden],
        lax.dynamic_slice(factors, (0, model_width + own_cols), (grid.total, rows)),
        (((0,), (0,)), ((), ())),
        precision=highest,
    )
    gate_mean = jnp.sum(factors[:, -1]) / (grid.total * model_width)
    all_dmean = jnp.concatenate(neighbours(grid, d_mean, reach), axis=0)
    d_rows = jnp.dot(match, all_dmean, precision=highest) / (counts * length_tok)
    d_spatial = d_output * gate_values[:, None, :] + d_rows[:, None, :]
    depth_primal, depth_back = jax.vjp(
        depth_filter, projected, full_depth, full_bias_depth
    )
    d_projected, d_depth, d_bias_depth = depth_back(d_spatial)
    d_projected = d_projected.astype(jnp.bfloat16)
    d_bias_proj = token_sum(d_projected)
    g_proj = weight_grad(grid, pooled[0].T, d_projected[0])
    d_pooled = jnp.einsum(
        "kpd,cd->kcp", d_projected, full_proj, preferred_element_type=jnp.float32
    ).astype(jnp.bfloat16)
    d_local = lax.all_to_all(d_pooled, "ch", split_axis=1, concat_axis=0, tiled=True)
    grad_features = jnp.einsum(
        "kcp,fp->kcf", d_local, pool_weights, preferred_element_type=jnp.float32
    ).astype(jnp.bfloat16)
    d_bias_fc2 = jnp.sum(d_output, axis=(0, 1))
    g_fc2 = weight_grad(grid, activation[0], cotangent[0])
    d_activation = jnp.einsum(
        "kpd,fd->kpf", cotangent, full_fc2, preferred_element_type=jnp.float32
    )
    gelu_primal, gelu_back = jax.vjp(gelu_exact, pre_act)
    d_pre = gelu_back(d_activation)[0].astype(jnp.bfloat16)
    d_bias_fc1 = token_sum(d_pre)
    g_fc1 = weight_grad(grid, normed2[0], d_pre[0])
    d_normed2 = jnp.einsum("kpf,df->kpd", d_pre, full_fc1, preferred_element_type=jnp.float32)
    norm_primal, norm_two_back = jax.vjp(
        layer_norm, first_sum, full_ln2_gain, full_ln2_bias
    )
    d_first_norm, d_ln2_gain, d_ln2_bias = norm_two_back(d_normed2)
    d_first = d_output + d_first_norm
    d_branch = d_first.astype(jnp.bfloat16)
    d_bias_out = token_sum(d_branch)
    g_attn_out = weight_grad(grid, attended[0], d_branch[0])
    d_attended = (
        jnp.einsum("kpe,de->kpd", d_branch, full_attn_out, preferred_element_type=jnp.float32)
        .astype(jnp.bfloat16)
        .reshape(head_shape)
    )
    d_query_heads, d_key_heads, d_value_heads = lax.map(
        attend_back, (query_heads, key_heads, value_heads, log_total, d_attended)
    )
    flat_shape = (count_images, length_tok, model_width)
    d_query_flat = d_query_heads.reshape(flat_shape)
    d_value_flat = d_value_heads.reshape(flat_shape)
    d_bias_qv = jnp.concatenate([token_sum(d_query_flat), token_sum(d_value_flat)])
    d_mixed = jnp.concatenate(
        [d_query_flat, d_key_heads.reshape(flat_shape), d_value_flat], axis=-1
    )
    g_qkv = weight_grad(grid, normed1[0], d_mixed[0])
    d_normed1 = jnp.einsum("kpe,de->kpd", d_mixed, full_qkv, preferred_element_type=jnp.float32)
    norm_one_primal, norm_one_back = jax.vjp(
        layer_norm, inputs32, full_ln1_gain, full_ln1_bias
    )
    d_input_norm, d_ln1_gain, d_ln1_bias = norm_one_back(d_normed1)
    grad_tokens = (d_first + d_input_norm).astype(jnp.bfloat16)
    sums = {
        "ln1_gain": d_ln1_gain,
        "ln1_bias": d_ln1_bias,
        "bias_qv": d_bias_qv,
        "bias_out": d_bias_out,
        "ln2_gain": d_ln2_gain,
        "ln2_bias": d_ln2_bias,
        "bias_fc1": d_bias_fc1,
        "bias_fc2": d_bias_fc2,
        "bias_proj": d_bias_proj,
        "bias_depth": d_bias_depth,
        "depth": d_depth.T.reshape(-1),
    }
    summed = scatter_small(
        grid, jnp.concatenate([sums[name].reshape(grid.total, -1) for name, _ in vectors], 1)
    )
    g = {name: summed[spans[name][0] : spans[name][1]] for name, _ in vectors}
    return (
        layer_out,
        grad_tokens,
        grad_features,
        g["ln1_gain"],
        g["ln1_bias"],
        g_qkv,
        g["bias_qv"],
        g_attn_out,
        g["bias_out"],
        g["ln2_gain"],
        g["ln2_bias"],
        g_fc1,
        g["bias_fc1"],
        g_fc2,
        g["bias_fc2"],
        g_proj,
        g["bias_proj"],
        g["depth"].reshape(rows, 9).T,
        g["bias_depth"],
        g_gate_in,
        g_gate_out,
        gate_mean,
    )


def solution(mesh):
    return jax.shard_map(
        shards,
        mesh=mesh,
        in_specs=(
            P(("img", "ch"), None, None),
            P("img", "ch", None),
            P(("img", "ch")),
            P(("img", "ch"), None, None),
            P(("img", "ch")),
            P(("img", "ch")),
            P(("img", "ch"), None),
            P(("img", "ch")),
            P(("img", "ch"), None),
            P(("img", "ch")),
            P(("img", "ch")),
            P(("img", "ch")),
            P(("img", "ch"), None),
            P(("img", "ch")),
            P(("img", "ch"), None),
            P(("img", "ch")),
            P(("img", "ch"), None),
            P(("img", "ch")),
            P(None, ("img", "ch")),
            P(("img", "ch")),
            P(("img", "ch"), None),
            P(None, ("img", "ch")),
        ),
        out_specs=(
            P(("img", "ch"), None, None),
            P(("img", "ch"), None, None),
            P("img", "ch", None),
            P(("img", "ch")),
            P(("img", "ch")),
            P(("img", "ch"), None),
            P(("img", "ch")),
            P(("img", "ch"), None),
            P(("img", "ch")),
            P(("img", "ch")),
            P(("img", "ch")),
            P(("img", "ch"), None),
            P(("img", "ch")),
            P(("img", "ch"), None),
            P(("img", "ch")),
            P(("img", "ch"), None),
            P(("img", "ch")),
            P(None, ("img", "ch")),
            P(("img", "ch")),
            P(("img", "ch"), None),
            P(None, ("img", "ch")),
            P(),
        ),
        check_vma=False,
    )
```

time: 1870 us -> 957 us (0.51)
  waiting for transfers between devices: 1180 us -> 235 us
  blocking collectives: 172 us -> 0 us
  starting transfers between devices: 76.9 us -> 194 us
  local copies, waits for them, and re-layouts: 65.9 us -> 115 us
  other arithmetic: 72.2 us -> 112 us
    reduce_scatter x7 -> x0, waiting for transfers between devices: 1010 us -> none  [the longest x1 189 us: shards(): lax.psum_scatter(d_fc1, ('img', 'ch'), scatter_dimension=0, tiled=True)]
    ppermute x18 -> x145, waiting for transfers between devices: 2.05 us -> 235 us  [the longest x133 232 us: send(): return lax.ppermute(v, AXES, pairs)]
    all_gather x7 -> x0, waiting for transfers between devices: 159 us -> none  [the longest x1 75.8 us: shards(): lax.all_gather(w_fc1, ('img', 'ch'), axis=0, tiled=True)]
    ppermute x18 -> x145, starting transfers between devices: 60.3 us -> 186 us  [the longest x133 151 us: send(): return lax.ppermute(v, AXES, pairs)]
    unnamed x2 -> x0, blocking collectives: 88.7 us -> none
    all_gather x2 -> x0, blocking collectives: 83.3 us -> none  [the longest x1 52.3 us: shards(): lax.all_gather(w_depth, ('img', 'ch'), axis=1, tiled=True)]
    concatenate x4 -> x25, local copies, waits for them, and re-layouts: 7.75 us -> 27.2 us  [the longest x10 9.55 us: gather_pieces(): s1 = jnp.concatenate([s0] + r1, 0)]
    dot_general x9 -> x16, matrix products: 55.8 us -> 56.2 us  [the longest x10 50.2 us: half(): lax.dot_general(left, cols, (((0,), (0,)), ((), ())), preferred_element_t...]
  transfers between devices with their start and end apart: 35 -> 147, of which waited for: 13 -> 46; matrix products, arithmetic and copies ran while one was open for 19% -> 47% of each run, Pallas kernels for 0% -> 1%
where the time goes in v1:
time: 957 us; the launch traced here: 947 us
  matrix products  272 us (28%)
  waiting for transfers between devices  235 us (25%)
  starting transfers between devices  194 us (20%)
  local copies, waits for them, and re-layouts  115 us (12%)
  other arithmetic  112 us (12%)
  Pallas kernels  10.8 us (1%)
    ppermute x133, waiting for transfers between devices, send(): return lax.ppermute(v, AXES, pairs)  232 us
    ppermute x133, starting transfers between devices, send(): return lax.ppermute(v, AXES, pairs)  151 us
    dot_general x10, matrix products, half(): lax.dot_general(left, cols, (((0,), (0,)), ((), ())), preferred_element_t...  50.2 us
    ppermute x12, starting transfers between devices, neighbours(): out.append(lax.ppermute(v, AXES, pairs))  35.1 us
    dot_general x1, matrix products, attend_back(): jnp.einsum('hqs,she->qhe', d_scores, key_heads, preferred_element_type=jn...  34.4 us
    dot_general x1, matrix products, attend_back(): jnp.einsum('hqs,qhe->she', d_scores, query_heads, preferred_element_type=...  33.3 us
    unnamed x319, local copies, waits for them, and re-layouts  30.8 us
    dot_general x1, matrix products, shards(): jnp.einsum('kpd,df->kpf', normed2, full_fc1, preferred_element_type=jnp.f...  30.2 us
  transfers between devices with their start and end apart: 147, of which 46 were waited for; matrix products, arithmetic and copies ran while one was open for 47% of the time, Pallas kernels for 1%

profile of v1, /device:TPU:9, one launch (start us, length us, event | category | flops | bytes accessed | tf_op | source)
XLA Modules:
  0.0 946.8 jit_solution(18072193773144018598)
XLA Ops:
  19.9 7.6 reshape.1243
  38.9 19.1 %collective-permute-done.1 = bf16[2,736]{1,0:T(2,128)(2,1)S(1)} collective-permute-done((bf16[2,736]{1,0:T(2,128)(2,1)S(1)}, bf16[2,736]{1,0:T(2,128)(2,1)S(1)}, u32[]{:S(2)}, u32[]{:S(2)}) %collective-permute-start.1) | collective-permute-done | bytes 2976 | tf_op jit(solution)/shard_map/ppermute | solution.py:37
  107.2 7.7 collective-permute-done.22
  124.5 9.5 %collective-permute-done.8 = bf16[64,1536]{1,0:T(8,128)(2,1)S(1)} collective-permute-done((bf16[64,1536]{1,0:T(8,128)(2,1)S(1)}, bf16[64,1536]{1,0:T(8,128)(2,1)S(1)}, u32[]{:S(2)}, u32[]{:S(2)}) %collective-permute-start.8) | collective-permute-done | bytes 196640 | tf_op jit(solution)/shard_map/ppermute | solution.py:37
  149.0 11.4 %collective-permute-done.49 = bf16[256,512]{1,0:T(8,128)(2,1)S(1)} collective-permute-done((bf16[256,512]{1,0:T(8,128)(2,1)S(1)}, bf16[256,512]{1,0:T(8,128)(2,1)S(1)}, u32[]{:S(2)}, u32[]{:S(2)}) %collective-permute-start.49) | collective-permute-done | bytes 262176 | tf_op jit(solution)/shard_map/ppermute | solution.py:37
  218.4 6.9 collective-permute-done.52.refs_1_
  299.6 12.9 %multiply_reduce_fusion.1 = (f32[16,576]{1,0:T(8,128)S(1)}, f32[16,576,576]{1,2,0:T(8,128)}) fusion(bf16[576,16,64]{0,2,1:T(8,128)(2,1)} %bitcast.680, bf16[576,16,64]{0,2,1:T(8,128)(2,1)} %bitcast.678), kind=kOutput, calls=%fused_computation.8 | convolution fusion | flops 690084864 | bytes 23629824 | tf_op jit(solution)/shard_map/while/body/eval_jaxpr/qhe,she->hqs/dot_general | solution.py:250
  312.4 10.3 %fusion.2 = f32[16,576]{1,0:T(8,128)S(1)} fusion(f32[16,576,576]{1,2,0:T(8,128)} %get-tuple-element.408, f32[16,576]{1,0:T(8,128)S(1)} %get-tuple-element.407), kind=kLoop, calls=%fused_computation.7 | loop fusion | flops 15916032 | bytes 21307392 | tf_op jit(solution)/shard_map/while/body/eval_jaxpr/reduce_sum | solution.py:255
  322.7 11.5 %fusion.78 = bf16[16,64,576]{2,1,0:T(8,128)(2,1)} fusion(bf16[576,16,64]{0,2,1:T(8,128)(2,1)S(1)} %bitcast.685, f32[16,576,576]{1,2,0:T(8,128)} %get-tuple-element.408, f32[16,576]{1,0:T(8,128)S(1)} %fusion.2, f32[16,576]{1,0:T(8,128)S(1)} %get-tuple-element.407), kind=kOutput, calls=%fused_computation.183 | convolution fusion | flops 701300736 | bytes 23666688 | tf_op jit(solution)/shard_map/while/body/eval_jaxpr/hqs,she->qhe/dot_general | solution.py:257
  344.6 14.6 %collective-permute-done.53.refs_2_ = bf16[8,256,256]{2,1,0:T(8,128)(2,1)S(1)} collective-permute-done((bf16[8,256,256]{2,1,0:T(8,128)(2,1)}, bf16[8,256,256]{2,1,0:T(8,128)(2,1)S(1)}, u32[]{:S(2)}, u32[]{:S(2)}) %collective-permute-start.53) | collective-permute-done | bytes 1048608 | tf_op jit(solution)/shard_map/ppermute | solution.py:37
  361.1 30.2 %multiply_convert_fusion.2 = (bf16[576,4096]{1,0:T(8,128)(2,1)}, f32[576,4096]{1,0:T(8,128)}, f32[576,4096]{1,0:T(8,128)}) fusion(f32[4096]{0:T(1024)S(1)} %copy-done.117, bf16[1024,4096]{1,0:T(8,128)(2,1)S(1)} %bitcast.659, f32[1,576,1024]{2,1,0:T(8,128)S(1)} %get-tuple-element.410, f32[1024]{0:T(1024)S(1)} %copy-done.121, f32[1024]{0:T(1024)S(1)} %copy-done.107, ...), kind=kOutput, calls=%fused_computation.26 | convolution fusion | flops 4990500864 | bytes 34370048 | tf_op jit(solution)/shard_map/kpd,df->kpf/dot_general | solution.py:382
  393.2 17.8 %convert_reduce_fusion = (f32[4096]{0:T(1024)}, bf16[576,4096]{1,0:T(8,128)(2,1)}) fusion(f32[576,4096]{1,0:T(8,128)} %get-tuple-element.242, bf16[4096,1024]{1,0:T(8,128)(2,1)S(1)} %bitcast.655, bf16[1,576,1024]{2,1,0:T(8,128)(2,1)} %param.25, f32[576,4096]{1,0:T(8,128)} %get-tuple-element.411, f32[4096]{0:T(1024)S(1)} %copy-done.117), kind=kOutput, calls=%fused_computation.24 | convolution fusion | flops 4871942144 | bytes 33193984 | tf_op jit(solution)/shard_map/kpd,fd->kpf/dot_general | solution.py:456
  411.0 10.0 %fusion.50 = (f32[1024]{0:T(1024)}, f32[576]{0:T(1024)S(1)}, f32[576,1024]{1,0:T(8,128)S(1)}) fusion(f32[1,576,1024]{2,1,0:T(8,128)S(1)} %copy-done.38, f32[576]{0:T(1024)S(1)} %fusion.255, f32[576]{0:T(1024)S(1)} %broadcast_multiply_fusion.9, f32[1024]{0:T(1024)S(1)} %copy-done.107, bf16[576,4096]{1,0:T(8,128)(2,1)} %get-tuple-element.420, ...), kind=kOutput, calls=%fused_computation.132 | convolution fusion | flops 4835965440 | bytes 17840896 | tf_op jit(solution)/shard_map/kpf,df->kpd/dot_general | solution.py:463
  452.9 12.8 %fusion.298 = f32[16,576,576]{1,2,0:T(8,128)} fusion(bf16[576,16,64]{0,2,1:T(8,128)(2,1)} %bitcast.670, bf16[576,16,64]{0,2,1:T(8,128)(2,1)} %bitcast.682), kind=kOutput, calls=%fused_computation.711 | convolution fusion | flops 679477248 | bytes 23592960 | tf_op jit(solution)/shard_map/while/body/eval_jaxpr/qhe,she->hqs/dot_general | solution.py:273
  465.6 14.1 %convert_reduce_fusion.3 = (f32[16,64]{1,0:T(8,128)}, bf16[16,64,576]{2,1,0:T(8,128)(2,1)}) fusion(bf16[576,16,64]{0,2,1:T(8,128)(2,1)} %bitcast.671, f32[16,576]{1,0:T(8,128)S(1)} %copy-done.65, f32[16,576,576]{1,2,0:T(8,128)} %get-tuple-element.408), kind=kOutput, calls=%fused_computation.99 | convolution fusion | flops 697170944 | bytes 23633920 | tf_op jit(solution)/shard_map/while/body/eval_jaxpr/hqs,qhe->she/dot_general | solution.py:270
  479.7 33.3 %fusion.72 = bf16[16,64,576]{2,1,0:T(8,128)(2,1)} fusion(bf16[576,16,64]{0,2,1:T(8,128)(2,1)} %bitcast.681, f32[16,576,576]{1,2,0:T(8,128)} %fusion.298, f32[16,576]{1,0:T(8,128)S(1)} %copy-done.65, f32[16,576,576]{1,2,0:T(8,128)} %get-tuple-element.408, bf16[576,16,64]{0,2,1:T(8,128)(2,1)} %bitcast.672, bf16[576,16,64]{0,2,1:T(8,128)(2,1)} %bitcast.683), kind=kOutput, calls=%fused_computation.181 | convolution fusion | flops 1407329792 | bytes 47222784 | tf_op jit(solution)/shard_map/while/body/eval_jaxpr/hqs,qhe->she/dot_general | solution.py:279
  513.0 34.4 %convert_reduce_fusion.4 = (f32[16,64]{1,0:T(8,128)}, bf16[16,64,576]{2,1,0:T(8,128)(2,1)}) fusion(bf16[576,16,64]{0,2,1:T(8,128)(2,1)} %bitcast.679, f32[16,576,576]{1,2,0:T(8,128)} %fusion.298, f32[16,576]{1,0:T(8,128)} %log_add_fusion, f32[16,576,576]{1,2,0:T(8,128)} %get-tuple-element.408, bf16[576,16,64]{0,2,1:T(8,128)(2,1)} %bitcast.673, ...), kind=kOutput, calls=%fused_computation.100 | convolution fusion | flops 1408508416 | bytes 47226880 | tf_op jit(solution)/shard_map/while/body/eval_jaxpr/hqs,she->qhe/dot_general | solution.py:276
  547.4 8.6 fusion.42
  556.0 8.4 pad_maximum_fusion
  564.5 9.0 convolution_convert_fusion
  615.5 14.0 %multiply_reduce_fusion.9 = (f32[1024]{0:T(1024)S(1)}, f32[1024]{0:T(1024)S(1)}, f32[1024]{0:T(1024)S(1)}, f32[1024]{0:T(1024)S(1)}, f32[1024]{0:T(1024)S(1)}, /...) fusion(f32[1,24,24,1024]{3,2,1,0:T(8,128)} %bitcast.674, ...), kind=kLoop, calls=%fused_computation.149 | loop fusion | flops 14737408 | bytes 26021888 | tf_op jit(solution)/shard_map/transpose(jvp())/reduce_sum | solution.py:238
  634.6 7.5 convert_reduce_fusion.5
  663.0 12.7 %reduce.58 = bf16[1536,576]{1,0:T(8,128)(2,1)S(1)} reduce(bf16[1536,1,576]{2,1,0:T(2,128)(2,1)} %bitcast.668, bf16[]{:T(256)} %broadcast.944), dimensions={1}, to_apply=%bitcast.596.reduce_sub_computation | reduce | bytes 3538946
  685.8 19.0 %collective-permute-done.92 = f32[2,736]{1,0:T(2,128)S(1)} collective-permute-done((f32[2,736]{1,0:T(2,128)S(1)}, f32[2,736]{1,0:T(2,128)S(1)}, u32[]{:S(2)}, u32[]{:S(2)}) %collective-permute-start.92) | collective-permute-done | bytes 5920 | tf_op jit(solution)/shard_map/ppermute | solution.py:37
  763.7 7.7 collective-permute-done.133
  802.6 9.3 collective-permute-done.97
  822.1 8.3 convert_add_fusion.1
  846.7 9.8 %collective-permute-done.100 = bf16[64,1536]{1,0:T(8,128)(2,1)S(1)} collective-permute-done((bf16[64,1536]{1,0:T(8,128)(2,1)S(1)}, bf16[64,1536]{1,0:T(8,128)(2,1)S(1)}, u32[]{:S(2)}, u32[]{:S(2)}) %collective-permute-start.100) | collective-permute-done | bytes 196640 | tf_op jit(solution)/shard_map/ppermute | solution.py:37
  868.7 9.5 collective-permute-done.115
  880.5 8.9 collective-permute-done.123
  916.2 13.6 %collective-permute-done.128 = bf16[256,512]{1,0:T(8,128)(2,1)S(1)} collective-permute-done((bf16[256,512]{1,0:T(8,128)(2,1)S(1)}, bf16[256,512]{1,0:T(8,128)(2,1)S(1)}, u32[]{:S(2)}, u32[]{:S(2)}) %collective-permute-start.128) | collective-permute-done | bytes 262176 | tf_op jit(solution)/shard_map/ppermute | solution.py:37
  933.1 8.0 collective-permute-done.119
  (863 shorter events, 521.2 us)
Async XLA Ops:
  10.7 76.1 %collective-permute-start.62 = (bf16[48,512]{1,0:T(8,128)(2,1)}, bf16[48,512]{1,0:T(8,128)(2,1)}, u32[]{:S(2)}, u32[]{:S(2)}) collective-permute-start(bf16[48,512]{1,0:T(8,128)(2,1)} %get-tuple-element.392), channel_id=1, source_target_pairs={{0,1},{1,0},{2,3},{3,2},{4,5},{5,4},{6,7},{7,6},{8,9},{9,8},{10,11... | collective-permute-start | bytes 147464 | tf_op jit(solution)/shard_map/ppermute | solution.py:37
  12.3 77.5 %collective-permute-start.20 = (bf16[32,1024]{1,0:T(8,128)(2,1)}, bf16[32,1024]{1,0:T(8,128)(2,1)}, u32[]{:S(2)}, u32[]{:S(2)}) collective-permute-start(bf16[32,1024]{1,0:T(8,128)(2,1)} %get-tuple-element.363), channel_id=1, source_target_pairs={{0,1},{1,0},{2,3},{3,2},{4,5},{5,4},{6,7},{7,6},{8,9},{9,8},{10,11... | collective-permute-start | bytes 196616 | tf_op jit(solution)/shard_map/ppermute | solution.py:37
  14.4 77.8 %collective-permute-start.6 = (bf16[32,1536]{1,0:T(8,128)(2,1)}, bf16[32,1536]{1,0:T(8,128)(2,1)}, u32[]{:S(2)}, u32[]{:S(2)}) collective-permute-start(bf16[32,1536]{1,0:T(8,128)(2,1)} %get-tuple-element.343), channel_id=1, source_target_pairs={{0,1},{1,0},{2,3},{3,2},{4,5},{5,4},{6,7},{7,6},{8,9},{9,8},{10,11... | collective-permute-start | bytes 294920 | tf_op jit(solution)/shard_map/ppermute | solution.py:37
  16.0 81.0 %collective-permute-start.34 = (bf16[32,2048]{1,0:T(8,128)(2,1)}, bf16[32,2048]{1,0:T(8,128)(2,1)}, u32[]{:S(2)}, u32[]{:S(2)}) collective-permute-start(bf16[32,2048]{1,0:T(8,128)(2,1)} %get-tuple-element.323), channel_id=1, source_target_pairs={{0,1},{1,0},{2,3},{3,2},{4,5},{5,4},{6,7},{7,6},{8,9},{9,8},{10,11... | collective-permute-start | bytes 393224 | tf_op jit(solution)/shard_map/ppermute | solution.py:37
  32.0 162.6 %all-to-all-start = ((bf16[4,384,576]{1,2,0:T(8,128)(2,1)}), bf16[4,384,576]{1,2,0:T(8,128)(2,1)}, u32[]{:S(2)}, u32[]{:S(2)}) async-start(bf16[4,384,576]{1,2,0:T(8,128)(2,1)} %convert_bitcast_fusion), calls=%async_computation | async-start | bytes 3538944 | tf_op jit(solution)/shard_map/all_to_all | solution.py:395
  123.8 36.7 %collective-permute-start.49 = (bf16[256,512]{1,0:T(8,128)(2,1)S(1)}, bf16[256,512]{1,0:T(8,128)(2,1)S(1)}, u32[]{:S(2)}, u32[]{:S(2)}) collective-permute-start(bf16[256,512]{1,0:T(8,128)(2,1)S(1)} %maximum_select_fusion.4), channel_id=1, source_target_pairs={{0,8},{1,9},{2,10},{3,11},{4,12},{5,13},{6,14},{7,15},{8,16},{9,17... | collective-permute-start | bytes 786440 | tf_op jit(solution)/shard_map/ppermute | solution.py:37
  148.7 40.7 %collective-permute-start.24 = (bf16[4,64,512]{2,1,0:T(8,128)(2,1)}, bf16[4,64,512]{2,1,0:T(8,128)(2,1)S(1)}, u32[]{:S(2)}, u32[]{:S(2)}) collective-permute-start(bf16[4,64,512]{2,1,0:T(8,128)(2,1)} %pad_maximum_fusion.7.refs_0_), channel_id=1, source_target_pairs={{0,4},{1,5},{2,6},{3,7},{4,0},{5,1},{6,2},{7,3},{8,12},{9,13},{10,... | collective-permute-start | bytes 786440 | tf_op jit(solution)/shard_map/ppermute | solution.py:37
  207.3 50.4 %collective-permute-start.25 = (bf16[8,64,512]{2,1,0:T(8,128)(2,1)}, bf16[8,64,512]{2,1,0:T(8,128)(2,1)S(1)}, u32[]{:S(2)}, u32[]{:S(2)}) collective-permute-start(bf16[8,64,512]{2,1,0:T(8,128)(2,1)} %constant_dynamic-update-slice_fusion.18), channel_id=1, source_target_pairs={{0,2},{1,3},{2,0},{3,1},{4,6},{5,7},{6,4},{7,5},{8,10},{9,11},{10,... | collective-permute-start | bytes 1572872 | tf_op jit(solution)/shard_map/ppermute | solution.py:37
  214.2 43.6 %collective-permute-start.27 = (bf16[8,64,512]{2,1,0:T(8,128)(2,1)}, bf16[8,64,512]{2,1,0:T(8,128)(2,1)S(1)}, u32[]{:S(2)}, u32[]{:S(2)}) collective-permute-start(bf16[8,64,512]{2,1,0:T(8,128)(2,1)} %constant_dynamic-update-slice_fusion.23), channel_id=1, source_target_pairs={{0,4},{1,5},{2,6},{3,7},{4,0},{5,1},{6,2},{7,3},{8,12},{9,13},{10,... | collective-permute-start | bytes 1572872 | tf_op jit(solution)/shard_map/ppermute | solution.py:37
  279.5 54.8 %collective-permute-start.42 = (bf16[4,64,1024]{2,1,0:T(8,128)(2,1)}, bf16[4,64,1024]{2,1,0:T(8,128)(2,1)S(1)}, u32[]{:S(2)}, u32[]{:S(2)}) collective-permute-start(bf16[4,64,1024]{2,1,0:T(8,128)(2,1)} %pad_maximum_fusion.1.refs_0_), channel_id=1, source_target_pairs={{0,1},{1,0},{2,3},{3,2},{4,5},{5,4},{6,7},{7,6},{8,9},{9,8},{10,11... | collective-permute-start | bytes 1572872 | tf_op jit(solution)/shard_map/ppermute | solution.py:37
  279.6 55.7 %collective-permute-start.45 = (bf16[4,64,1024]{2,1,0:T(8,128)(2,1)}, bf16[4,64,1024]{2,1,0:T(8,128)(2,1)}, u32[]{:S(2)}, u32[]{:S(2)}) collective-permute-start(bf16[4,64,1024]{2,1,0:T(8,128)(2,1)} %pad_maximum_fusion.2.refs_3_), channel_id=1, source_target_pairs={{0,1},{1,0},{2,3},{3,2},{4,5},{5,4},{6,7},{7,6},{8,9},{9,8},{10,11... | collective-permute-start | bytes 1572872 | tf_op jit(solution)/shard_map/ppermute | solution.py:37
  280.1 55.8 %collective-permute-start.39 = (bf16[8,64,1024]{2,1,0:T(8,128)(2,1)}, bf16[8,64,1024]{2,1,0:T(8,128)(2,1)S(1)}, u32[]{:S(2)}, u32[]{:S(2)}) collective-permute-start(bf16[8,64,1024]{2,1,0:T(8,128)(2,1)} %constant_dynamic-update-slice_fusion.28), channel_id=1, source_target_pairs={{0,2},{1,3},{2,0},{3,1},{4,6},{5,7},{6,4},{7,5},{8,10},{9,11},{10,... | collective-permute-start | bytes 3145736 | tf_op jit(solution)/shard_map/ppermute | solution.py:37
  280.2 55.8 %collective-permute-start.41 = (bf16[8,64,1024]{2,1,0:T(8,128)(2,1)}, bf16[8,64,1024]{2,1,0:T(8,128)(2,1)}, u32[]{:S(2)}, u32[]{:S(2)}) collective-permute-start(bf16[8,64,1024]{2,1,0:T(8,128)(2,1)} %constant_dynamic-update-slice_fusion.33), channel_id=1, source_target_pairs={{0,4},{1,5},{2,6},{3,7},{4,0},{5,1},{6,2},{7,3},{8,12},{9,13},{10,... | collective-permute-start | bytes 3145736 | tf_op jit(solution)/shard_map/ppermute | solution.py:37
  281.6 53.7 %collective-permute-start.43 = (bf16[4,64,1024]{2,1,0:T(8,128)(2,1)}, bf16[4,64,1024]{2,1,0:T(8,128)(2,1)}, u32[]{:S(2)}, u32[]{:S(2)}) collective-permute-start(bf16[4,64,1024]{2,1,0:T(8,128)(2,1)} %collective-permute-done.38.refs_1_), channel_id=1, source_target_pairs={{0,1},{1,0},{2,3},{3,2},{4,5},{5,4},{6,7},{7,6},{8,9},{9,8},{10,11... | collective-permute-start | bytes 1572872 | tf_op jit(solution)/shard_map/ppermute | solution.py:37
  340.7 50.6 %collective-permute-start.59 = (bf16[4,256,256]{2,1,0:T(8,128)(2,1)S(1)}, bf16[4,256,256]{2,1,0:T(8,128)(2,1)S(1)}, u32[]{:S(2)}, u32[]{:S(2)}) collective-permute-start(bf16[4,256,256]{2,1,0:T(8,128)(2,1)S(1)} %copy-done.10), channel_id=1, source_target_pairs={{0,1},{1,0},{2,3},{3,2},{4,5},{5,4},{6,7},{7,6},{8,9},{9,8},{10,11... | collective-permute-start | bytes 1572872 | tf_op jit(solution)/shard_map/ppermute | solution.py:37
  341.1 50.3 %collective-permute-start.57 = (bf16[4,256,256]{2,1,0:T(8,128)(2,1)S(1)}, bf16[4,256,256]{2,1,0:T(8,128)(2,1)S(1)}, u32[]{:S(2)}, u32[]{:S(2)}) collective-permute-start(bf16[4,256,256]{2,1,0:T(8,128)(2,1)S(1)} %collective-permute-done.52.refs_1_), channel_id=1, source_target_pairs={{0,1},{1,0},{2,3},{3,2},{4,5},{5,4},{6,7},{7,6},{8,9},{9,8},{10,11... | collective-permute-start | bytes 1572872 | tf_op jit(solution)/shard_map/ppermute | solution.py:37
  344.3 47.1 %collective-permute-start.60 = (bf16[4,256,256]{2,1,0:T(8,128)(2,1)S(1)}, bf16[4,256,256]{2,1,0:T(8,128)(2,1)S(1)}, u32[]{:S(2)}, u32[]{:S(2)}) collective-permute-start(bf16[4,256,256]{2,1,0:T(8,128)(2,1)S(1)} %collective-permute-done.54.refs_4_), channel_id=1, source_target_pairs={{0,1},{1,0},{2,3},{3,2},{4,5},{5,4},{6,7},{7,6},{8,9},{9,8},{10,11... | collective-permute-start | bytes 1572872 | tf_op jit(solution)/shard_map/ppermute | solution.py:37
  428.5 159.3 %collective-permute-start.87 = (f32[1,1024]{1,0:T(1,128)}, f32[1,1024]{1,0:T(1,128)}, u32[]{:S(2)}, u32[]{:S(2)}) collective-permute-start(f32[1,1024]{1,0:T(1,128)} %fusion.102), channel_id=1, source_target_pairs={{3,0},{4,1},{5,2},{6,3},{7,4},{8,5},{9,6},{10,7},{11,8},{12,9},{13... | collective-permute-start | bytes 12296 | tf_op jit(solution)/shard_map/ppermute | solution.py:206
  430.4 174.9 %collective-permute-start.86 = (f32[1,1024]{1,0:T(1,128)}, f32[1,1024]{1,0:T(1,128)}, u32[]{:S(2)}, u32[]{:S(2)}) collective-permute-start(f32[1,1024]{1,0:T(1,128)} %fusion.102), channel_id=1, source_target_pairs={{0,3},{1,4},{2,5},{3,6},{4,7},{5,8},{6,9},{7,10},{8,11},{9,12},{10... | collective-permute-start | bytes 12296 | tf_op jit(solution)/shard_map/ppermute | solution.py:206
  434.0 171.4 %collective-permute-start.85 = (f32[1,1024]{1,0:T(1,128)}, f32[1,1024]{1,0:T(1,128)}, u32[]{:S(2)}, u32[]{:S(2)}) collective-permute-start(f32[1,1024]{1,0:T(1,128)} %fusion.102), channel_id=1, source_target_pairs={{2,0},{3,1},{4,2},{5,3},{6,4},{7,5},{8,6},{9,7},{10,8},{11,9},{12,... | collective-permute-start | bytes 12296 | tf_op jit(solution)/shard_map/ppermute | solution.py:206
  436.7 169.1 %collective-permute-start.84 = (f32[1,1024]{1,0:T(1,128)}, f32[1,1024]{1,0:T(1,128)}, u32[]{:S(2)}, u32[]{:S(2)}) collective-permute-start(f32[1,1024]{1,0:T(1,128)} %fusion.102), channel_id=1, source_target_pairs={{0,2},{1,3},{2,4},{3,5},{4,6},{5,7},{6,8},{7,9},{8,10},{9,11},{10,... | collective-permute-start | bytes 12296 | tf_op jit(solution)/shard_map/ppermute | solution.py:206
  439.3 166.4 %collective-permute-start.83 = (f32[1,1024]{1,0:T(1,128)}, f32[1,1024]{1,0:T(1,128)}, u32[]{:S(2)}, u32[]{:S(2)}) collective-permute-start(f32[1,1024]{1,0:T(1,128)} %fusion.102), channel_id=1, source_target_pairs={{1,0},{2,1},{3,2},{4,3},{5,4},{6,5},{7,6},{8,7},{9,8},{10,9},{11,1... | collective-permute-start | bytes 12296 | tf_op jit(solution)/shard_map/ppermute | solution.py:206
  605.3 79.5 %collective-permute-start.139 = (f32[1,3200]{1,0:T(1,128)}, f32[1,3200]{1,0:T(1,128)}, u32[]{:S(2)}, u32[]{:S(2)}) collective-permute-start(f32[1,3200]{1,0:T(1,128)} %broadcast_in_dim.121), channel_id=1, source_target_pairs={{0,1},{1,0},{2,3},{3,2},{4,5},{5,4},{6,7},{7,6},{8,9},{9,8},{10,11... | collective-permute-start | bytes 38408 | tf_op jit(solution)/shard_map/ppermute | solution.py:37
  605.4 116.7 %collective-permute-start.103 = (bf16[1024,512]{1,0:T(8,128)(2,1)}, bf16[1024,512]{1,0:T(8,128)(2,1)}, u32[]{:S(2)}, u32[]{:S(2)}) collective-permute-start(bf16[1024,512]{1,0:T(8,128)(2,1)} %convolution_convert_fusion.9), channel_id=1, source_target_pairs={{0,1},{1,0},{2,3},{3,2},{4,5},{5,4},{6,7},{7,6},{8,9},{9,8},{10,11... | collective-permute-start | bytes 3145736 | tf_op jit(solution)/shard_map/ppermute | solution.py:37
  649.6 129.6 %collective-permute-start.94 = (bf16[1024,1536]{1,0:T(8,128)(2,1)}, bf16[1024,1536]{1,0:T(8,128)(2,1)}, u32[]{:S(2)}, u32[]{:S(2)}) collective-permute-start(bf16[1024,1536]{1,0:T(8,128)(2,1)} %convolution_convert_fusion.2), channel_id=1, source_target_pairs={{0,1},{1,0},{2,3},{3,2},{4,5},{5,4},{6,7},{7,6},{8,9},{9,8},{10,11... | collective-permute-start | bytes 9437192 | tf_op jit(solution)/shard_map/ppermute | solution.py:37
  656.1 88.0 %collective-permute-start.130 = (bf16[1536,512]{1,0:T(8,128)(2,1)}, bf16[1536,512]{1,0:T(8,128)(2,1)}, u32[]{:S(2)}, u32[]{:S(2)}) collective-permute-start(bf16[1536,512]{1,0:T(8,128)(2,1)} %convolution_convert_fusion.6), channel_id=1, source_target_pairs={{0,1},{1,0},{2,3},{3,2},{4,5},{5,4},{6,7},{7,6},{8,9},{9,8},{10,11... | collective-permute-start | bytes 4718600 | tf_op jit(solution)/shard_map/ppermute | solution.py:37
  679.0 54.3 %all-to-all-start.1 = ((bf16[4,2,110592]{2,1,0:T(2,128)(2,1)}), bf16[4,2,110592]{2,1,0:T(2,128)(2,1)S(1)}, u32[]{:S(2)}, u32[]{:S(2)}) async-start(bf16[4,2,110592]{2,1,0:T(2,128)(2,1)} %reshape.1271), calls=%async_computation.1 | async-start | bytes 3538944 | tf_op jit(solution)/shard_map/all_to_all | solution.py:450
  755.6 57.9 %collective-permute-start.121 = (bf16[4096,512]{1,0:T(8,128)(2,1)S(1)}, bf16[4096,512]{1,0:T(8,128)(2,1)}, u32[]{:S(2)}, u32[]{:S(2)}) collective-permute-start(bf16[4096,512]{1,0:T(8,128)(2,1)S(1)} %copy-done.129), channel_id=1, source_target_pairs={{0,1},{1,0},{2,3},{3,2},{4,5},{5,4},{6,7},{7,6},{8,9},{9,8},{10,11... | collective-permute-start | bytes 12582920 | tf_op jit(solution)/shard_map/ppermute | solution.py:37
  759.4 62.7 %collective-permute-start.112 = (bf16[1024,2048]{1,0:T(8,128)(2,1)}, bf16[1024,2048]{1,0:T(8,128)(2,1)}, u32[]{:S(2)}, u32[]{:S(2)}) collective-permute-start(bf16[1024,2048]{1,0:T(8,128)(2,1)} %convolution_convert_fusion.4), channel_id=1, source_target_pairs={{0,1},{1,0},{2,3},{3,2},{4,5},{5,4},{6,7},{7,6},{8,9},{9,8},{10,11... | collective-permute-start | bytes 12582920 | tf_op jit(solution)/shard_map/ppermute | solution.py:37
  820.3 42.3 %collective-permute-start.122 = (bf16[4,2,256,256]{3,2,0,1:T(8,128)(2,1)S(1)}, bf16[4,2,256,256]{3,2,0,1:T(8,128)(2,1)}, u32[]{:S(2)}, u32[]{:S(2)}) collective-permute-start(bf16[4,2,256,256]{3,2,0,1:T(8,128)(2,1)S(1)} %fusion.96), channel_id=1, source_target_pairs={{0,2},{1,3},{2,0},{3,1},{4,6},{5,7},{6,4},{7,5},{8,10},{9,11},{10,... | collective-permute-start | bytes 3145736 | tf_op jit(solution)/shard_map/ppermute | solution.py:37
  821.5 43.7 %collective-permute-start.124 = (bf16[4,2,256,256]{3,2,0,1:T(8,128)(2,1)S(1)}, bf16[4,2,256,256]{3,2,0,1:T(8,128)(2,1)}, u32[]{:S(2)}, u32[]{:S(2)}) collective-permute-start(bf16[4,2,256,256]{3,2,0,1:T(8,128)(2,1)S(1)} %fusion.97), channel_id=1, source_target_pairs={{0,4},{1,5},{2,6},{3,7},{4,0},{5,1},{6,2},{7,3},{8,12},{9,13},{10,... | collective-permute-start | bytes 3145736 | tf_op jit(solution)/shard_map/ppermute | solution.py:37
  862.0 80.7 %collective-permute-start.102 = (f32[32,1536]{1,0:T(8,128)S(1)}, f32[32,1536]{1,0:T(8,128)S(1)}, u32[]{:S(2)}, u32[]{:S(2)}) collective-permute-start(f32[32,1536]{1,0:T(8,128)S(1)} %get-tuple-element.287), channel_id=1, source_target_pairs={{0,1},{1,0},{2,3},{3,2},{4,5},{5,4},{6,7},{7,6},{8,9},{9,8},{10,11... | collective-permute-start | bytes 589832 | tf_op jit(solution)/shard_map/ppermute | solution.py:37
  (254 other events, 3996.9 us)

commit v2 on v1

v2 whole, which is shorter than its diff:
```python
import functools
import math

import jax
import numpy as np
import jax.numpy as jnp
from jax import lax
from jax.experimental import pallas as pl
from jax.experimental.pallas import tpu as pltpu
from jax.sharding import PartitionSpec as P

HEAD = 64
PS = 24
FS = 32
REACH = 3
LN1_GAIN, LN1_BIAS, BIAS_OUT, LN2_GAIN, LN2_BIAS, BIAS_FC2, BIAS_PROJ, BIAS_DEPTH, DEPTH = range(9)
LINES = DEPTH + 9

norm_eps = 1e-05
highest = lax.Precision.HIGHEST
f32, bf16 = jnp.float32, jnp.bfloat16
AXES = ("img", "ch")
NN = (((1,), (0,)), ((), ()))
NT = (((1,), (1,)), ((), ()))
TN = (((0,), (0,)), ((), ()))


class Grid:
    def __init__(self):
        img, ch = lax.axis_size("img"), lax.axis_size("ch")
        depth = 4 if img % 4 == 0 else 1
        self.n = {"z": depth, "x": img // depth, "y": ch // 2, "c": 2}
        self.stride = {"c": 1, "y": 2, "x": ch, "z": ch * (img // depth)}
        self.total = img * ch
        me = lax.axis_index(AXES)
        self.me = me
        self.pos = {a: lax.rem(lax.div(me, self.stride[a]), self.n[a]) for a in self.n}

    def send(self, v, axis, by):
        n, s = self.n[axis], self.stride[axis]
        pairs = []
        for i in range(self.total):
            a = (i // s) % n
            pairs.append((i, i + ((a + by) % n - a) * s))
        return lax.ppermute(v, AXES, pairs)

    def other(self, axis, by):
        return lax.rem(self.pos[axis] + by, self.n[axis])


class GatherSmall:
    def __init__(self, grid, v):
        self.grid, self.v, self.left = grid, v[None], ["c", "y", "x", "z"]

    def next(self):
        axis = self.left.pop(0)
        n, v = self.grid.n[axis], self.v
        got = [v] + [self.grid.send(v, axis, k) for k in range(1, n)]
        ring = jnp.stack(got[::-1] + got[::-1])
        start = lax.rem(2 * n - 1 - self.grid.pos[axis], n)
        v = lax.dynamic_slice_in_dim(ring, start, n, 0)
        self.v = v.reshape(n * v.shape[1], v.shape[2])
        return self.v


class ScatterSmall:
    def __init__(self, grid, v):
        self.grid, self.v, self.left = grid, v, ["z", "x", "y", "c"]

    def next(self):
        axis = self.left.pop(0)
        g, n = self.grid, self.grid.n[axis]
        t = self.v.reshape(n, -1, self.v.shape[1])
        total = lax.dynamic_index_in_dim(t, g.pos[axis], 0, keepdims=False)
        for k in range(1, n):
            away = lax.dynamic_index_in_dim(t, g.other(axis, k), 0, keepdims=False)
            total = total + g.send(away, axis, k)
        self.v = total
        return self.v


def assemble(grid, cores, r, width):
    nz, nx, ny = grid.n["z"], grid.n["x"], grid.n["y"]
    q = width // 2
    arrays, plan = [], []
    for core_rel, parts in enumerate(cores):
        for part, (first, second, s0, r1, r2) in enumerate(parts):
            for k1, buf in enumerate([s0] + r1):
                for kz in range(nz):
                    plan.append((len(arrays), kz, core_rel, part, kz, {first: k1, second: 0}))
                arrays.append(buf)
            for k2, buf in enumerate(r2, 1):
                for k1 in range(grid.n[first]):
                    for kz in range(nz):
                        rel = {first: k1, second: k2}
                        plan.append((len(arrays), k1 * nz + kz, core_rel, part, kz, rel))
                arrays.append(buf)

    def body(place, *refs):
        ins, out, sem = refs[: len(arrays)], refs[len(arrays)], refs[len(arrays) + 1]
        z, x, y, c = place[0], place[1], place[2], place[3]
        copies = []
        for i, j, core_rel, part, kz, rel in plan:
            zz = lax.rem(z - kz + nz, nz)
            xx = lax.rem(x - rel["x"] + nx, nx)
            yy = lax.rem(y - rel["y"] + ny, ny)
            cc = lax.rem(c + core_rel, 2)
            copies.append(
                pltpu.make_async_copy(
                    ins[i].at[j], out.at[zz, xx, yy, cc, :, pl.ds(part * q, q)], sem
                )
            )
            copies[-1].start()
        for copy in copies:
            copy.wait()

    place = jnp.stack([grid.pos[a] for a in ("z", "x", "y", "c")]).astype(jnp.int32)
    rows = nz * nx * ny * 2 * r
    whole = pl.pallas_call(
        body,
        out_shape=jax.ShapeDtypeStruct((nz, nx, ny, 2, r, width), bf16),
        in_specs=[pl.BlockSpec(memory_space=pltpu.SMEM)]
        + [pl.BlockSpec(memory_space=pltpu.HBM)] * len(arrays),
        out_specs=pl.BlockSpec(memory_space=pltpu.VMEM),
        scratch_shapes=[pltpu.SemaphoreType.DMA],
        compiler_params=pltpu.CompilerParams(
            vmem_limit_bytes=nz * nx * ny * 2 * (r + 8) * width * 2 + (4 << 20)
        ),
        cost_estimate=pl.CostEstimate(
            flops=0, bytes_accessed=rows * width * 4, transcendentals=0
        ),
        name="assemble",
    )(place, *arrays)
    return whole.reshape(rows, width)


def after(value, done):
    return lax.optimization_barrier((value, done))[0]


class Gather:
    def __init__(self, grid, shard):
        self.grid, self.shard = grid, shard
        self.q = shard.shape[1] // 2

    def along_z(self):
        g = self.grid
        self.z = [self.shard] + [g.send(self.shard, "z", k) for k in range(1, g.n["z"])]

    def first(self):
        self.s0 = [
            jnp.stack([p[:, i * self.q : (i + 1) * self.q] for p in self.z]) for i in range(2)
        ]
        self.r1 = [self.every(self.s0[i], "xy"[i]) for i in range(2)]

    def second(self):
        self.r2 = [
            self.every(jnp.concatenate([self.s0[i]] + self.r1[i], 0), "yx"[i]) for i in range(2)
        ]
        self.c0 = [self.over(s) for s in self.s0]
        self.c1 = [[self.over(b) for b in r] for r in self.r1]

    def cross(self):
        self.c2 = [[self.over(b) for b in r] for r in self.r2]

    def every(self, v, axis):
        return [self.grid.send(v, axis, k) for k in range(1, self.grid.n[axis])]

    def over(self, v):
        return self.grid.send(v, "c", 1)


    def state(self):
        return {k: v for k, v in vars(self).items() if k not in ("grid", "q", "rows")}

    def set_state(self, state):
        for k, v in state.items():
            setattr(self, k, v)

    def whole(self):
        own = [("xy"[i], "yx"[i], self.s0[i], self.r1[i], self.r2[i]) for i in range(2)]
        away = [("xy"[i], "yx"[i], self.c0[i], self.c1[i], self.c2[i]) for i in range(2)]
        return assemble(self.grid, [own, away], *self.shard.shape)


def wgrad_body(n, r2, pos_ref, l0, l1, r0, r1, *outs):
    nx, ny = n
    o = dot(l0[...], r0[...], TN) + dot(l1[...], r1[...], TN)
    h = o.shape[1]
    q = h // 2
    o = o.reshape(nx, ny, r2, h)
    keep_a, keep_b = outs[0], outs[1]
    away_a, away_b = outs[2:2 + ny - 1], outs[2 + ny - 1:]
    for y in range(ny):
        @pl.when(pos_ref[1] == y)
        def _(y=y):
            keep_a[0] = o[:, y, :, :q].astype(bf16)
            for k in range(1, ny):
                away_a[k - 1][0] = o[:, (y + k) % ny, :, :q].astype(bf16)
    for x in range(nx):
        @pl.when(pos_ref[0] == x)
        def _(x=x):
            keep_b[0] = o[x, :, :, q:].astype(bf16)
            for k in range(1, nx):
                away_b[k - 1][0] = o[(x + k) % nx, :, :, q:].astype(bf16)

def wgrad(place, n, left, left_peer, right, right_peer):
    nz, nx, ny = n
    t, rows = left.shape
    h = right_peer.shape[1]
    q = h // 2
    r2 = rows // (nz * nx * ny)
    part = pl.BlockSpec((t, rows // nz), lambda i, p: (0, i))
    a = jax.ShapeDtypeStruct((nz, nx, r2, q), bf16)
    b = jax.ShapeDtypeStruct((nz, ny, r2, q), bf16)
    sa = pl.BlockSpec((1, nx, r2, q), lambda i, p: (i, 0, 0, 0))
    sb = pl.BlockSpec((1, ny, r2, q), lambda i, p: (i, 0, 0, 0))
    return pl.pallas_call(
        functools.partial(wgrad_body, (nx, ny), r2),
        grid_spec=pltpu.PrefetchScalarGridSpec(
            num_scalar_prefetch=1, grid=(nz,),
            in_specs=[part, part, pl.BlockSpec((t, h), lambda i, p: (0, p[2])), pl.BlockSpec((t, h), lambda i, p: (0, 0))],
            out_specs=[sa, sb] + [sa] * (ny - 1) + [sb] * (nx - 1)),
        out_shape=[a, b] + [a] * (ny - 1) + [b] * (nx - 1),
        compiler_params=pltpu.CompilerParams(vmem_limit_bytes=56 << 20),
        name="weight_grad",
    )(place, left, left_peer, right, right_peer)


class Scatter:
    def __init__(self, grid, left, left_peer, right, right_peer):
        self.grid, self.rows = grid, left.shape[1] // grid.total
        n = grid.n
        place = jnp.stack([grid.pos[a] for a in ("x", "y", "c")]).astype(jnp.int32)
        sums = wgrad(place, (n["z"], n["x"], n["y"]), left, left_peer, right, right_peer)
        self.keep = list(sums[:2])
        self.away = [list(sums[2 : 1 + n["y"]]), list(sums[1 + n["y"] :])]

    state, set_state = Gather.state, Gather.set_state

    def first(self):
        self.got = [
            [self.grid.send(v, "yx"[i], k) for k, v in enumerate(self.away[i], 1)] for i in range(2)
        ]
        del self.away

    def total(self, i, at):
        terms = [
            lax.dynamic_index_in_dim(t, at, 1, keepdims=False).astype(f32)
            for t in [self.keep[i]] + self.got[i]
        ]
        return functools.reduce(jnp.add, terms)

    def second(self):
        g = self.grid
        self.more = []
        for i, axis in enumerate("xy"):
            self.more.append(
                [
                    g.send(self.total(i, g.other(axis, k)).astype(bf16), axis, k)
                    for k in range(1, g.n[axis])
                ]
            )

    def along_z(self):
        g = self.grid
        halves = []
        for i, axis in enumerate("xy"):
            terms = [self.total(i, g.pos[axis])] + [t.astype(f32) for t in self.more[i]]
            halves.append(functools.reduce(jnp.add, terms))

        def at(z):
            return [lax.dynamic_index_in_dim(t, z, 0, keepdims=False) for t in halves]

        self.kept = [jnp.concatenate(at(g.pos["z"]), 1)]
        for k in range(1, g.n["z"]):
            away = jnp.concatenate([t.astype(bf16) for t in at(g.other("z", k))], 1)
            self.kept.append(g.send(away, "z", k))
        del self.keep, self.got, self.more

    def last(self):
        total = functools.reduce(jnp.add, [t.astype(f32) for t in self.kept])
        r, c = self.rows, self.grid.pos["c"]
        self.own = lax.dynamic_slice_in_dim(total, c * r, r, 0)
        self.back = self.grid.send(lax.dynamic_slice_in_dim(total, (1 - c) * r, r, 0), "c", 1)
        del self.kept

    def result(self):
        pair = (self.own, self.back)
        return jnp.where(
            self.grid.pos["c"] == 0, jnp.concatenate(pair, 1), jnp.concatenate(pair[::-1], 1)
        )


def neighbours(grid, v, reach):
    out = [v]
    for offset in range(1, reach + 1):
        for by in (offset, -offset):
            pairs = [(i, i + by) for i in range(grid.total) if 0 <= i + by < grid.total]
            out.append(lax.ppermute(v, AXES, pairs))
    return out


def layer_norm(inputs, scale_gain, offset_bias):
    centre = jnp.mean(inputs, axis=-1, keepdims=True)
    centred = inputs - centre
    spread = jnp.mean(centred * centred, axis=-1, keepdims=True)
    return centred * lax.rsqrt(spread + norm_eps) * scale_gain + offset_bias


def dot(a, b, dims=NN):
    return lax.dot_general(a, b, dims, preferred_element_type=f32)

def attend_body(q_ref, k_ref, v_ref, o_ref, lse_ref):
    t = q_ref.shape[0]
    first = lax.broadcasted_iota(jnp.int32, (t, 2 * HEAD), 1) < HEAD
    q, k, v = q_ref[...], k_ref[...], v_ref[...]
    out, totals = [], []
    for side in range(2):
        keep = first if side == 0 else jnp.logical_not(first)
        s = dot(q, jnp.where(keep, k, jnp.zeros_like(k)), NT)
        top = jnp.max(s, axis=-1, keepdims=True)
        p = jnp.exp((s - top) * HEAD ** -0.5)
        total = jnp.sum(p, axis=-1, keepdims=True)
        o = dot((p * (1.0 / total)).astype(bf16), jnp.where(keep, v, jnp.zeros_like(v)))
        out.append(o)
        totals.append(top * HEAD ** -0.5 + jnp.log(total))
    o_ref[...] = (out[0] + out[1]).astype(bf16)
    lse_ref[...] = jnp.where(first, totals[0], totals[1])

def attend(qkv):
    t, width = qkv.shape
    n = width // 3 // (2 * HEAD)
    spec = lambda off: pl.BlockSpec((t, 2 * HEAD), lambda i, off=off: (0, off * n + i))
    return pl.pallas_call(
        attend_body, grid=(n,),
        in_specs=[spec(0), spec(1), spec(2)],
        out_specs=[spec(0), spec(0)],
        out_shape=[jax.ShapeDtypeStruct((t, width // 3), bf16), jax.ShapeDtypeStruct((t, width // 3), f32)],
        compiler_params=pltpu.CompilerParams(vmem_limit_bytes=48 << 20),
        cost_estimate=pl.CostEstimate(flops=4 * t * t * width // 3, bytes_accessed=t * width * 4, transcendentals=t * t * 16),
        name="attend",
    )(qkv, qkv, qkv)

def attend_back_body(q_ref, k_ref, v_ref, do_ref, lse_ref, dq_ref, dk_ref, dv_ref):
    t = q_ref.shape[0]
    first = lax.broadcasted_iota(jnp.int32, (t, 2 * HEAD), 1) < HEAD
    q, k, v, do = q_ref[...], k_ref[...], v_ref[...], do_ref[...]
    zero = jnp.zeros_like(k)
    dq = dk = dv = None
    for side in range(2):
        keep = first if side == 0 else jnp.logical_not(first)
        km, vm = jnp.where(keep, k, zero), jnp.where(keep, v, zero)
        qm, dom = jnp.where(keep, q, zero), jnp.where(keep, do, zero)
        lse = lse_ref[:, side * HEAD:side * HEAD + 1]
        p = jnp.exp(dot(q, km, NT) * HEAD ** -0.5 - lse)
        dp = dot(do, vm, NT)
        inner = jnp.sum(p * dp, axis=-1, keepdims=True)
        ds = (p * ((dp - inner) * HEAD ** -0.5)).astype(bf16)
        dq_ = dot(ds, km)
        dv_ = dot(dom, p.astype(bf16), TN)
        dk_ = dot(qm, ds, TN)
        dq = dq_ if dq is None else dq + dq_
        dv = dv_ if dv is None else dv + dv_
        dk = dk_ if dk is None else dk + dk_
    dq_ref[...] = dq.astype(bf16)
    dk_ref[...] = dk.T.astype(bf16)
    dv_ref[...] = dv.T.astype(bf16)

def attend_back(qkv, d_attended, lse):
    t, width = qkv.shape
    n = width // 3 // (2 * HEAD)
    spec = lambda off: pl.BlockSpec((t, 2 * HEAD), lambda i, off=off: (0, off * n + i))
    shape = jax.ShapeDtypeStruct((t, width // 3), bf16)
    return pl.pallas_call(
        attend_back_body, grid=(n,),
        in_specs=[spec(0), spec(1), spec(2), spec(0), spec(0)],
        out_specs=[spec(0)] * 3,
        out_shape=[shape] * 3,
        compiler_params=pltpu.CompilerParams(vmem_limit_bytes=48 << 20),
        cost_estimate=pl.CostEstimate(flops=10 * t * t * width // 3, bytes_accessed=t * width * 8, transcendentals=t * t * 16),
        name="attend_back",
    )(qkv, qkv, qkv, d_attended, lse)

def gelu_parts(v):
    e = jnp.exp(-0.5 * v * v)
    t = 1.0 / (1.0 + (0.3275911 * 0.5 ** 0.5) * jnp.abs(v))
    poly = t * (0.127414796 + t * (-0.142248368 + t * (0.7107068705 + t * (-0.7265760135 + t * 0.5307027145))))
    tail = poly * e
    phi = jnp.where(v < 0, tail, 1.0 - tail)
    return v * phi, phi + v * (e * (2.0 * math.pi) ** -0.5)

def mlp_in_body(n_ref, w_ref, b_ref, act_ref, slope_ref):
    v = dot(n_ref[...], w_ref[...]) + b_ref[...]
    act, slope = gelu_parts(v)
    act_ref[...] = act.astype(bf16)
    slope_ref[...] = slope.astype(bf16)

def mlp_in(normed, w, bias, block=512):
    t, d = normed.shape
    ff = w.shape[1]
    out = pl.BlockSpec((t, block), lambda i: (0, i))
    shape = jax.ShapeDtypeStruct((t, ff), bf16)
    return pl.pallas_call(
        mlp_in_body, grid=(ff // block,),
        in_specs=[pl.BlockSpec((t, d), lambda i: (0, 0)), pl.BlockSpec((d, block), lambda i: (0, i)), pl.BlockSpec((1, block), lambda i: (0, i))],
        out_specs=[out, out], out_shape=[shape, shape],
        compiler_params=pltpu.CompilerParams(vmem_limit_bytes=48 << 20),
        cost_estimate=pl.CostEstimate(flops=2 * t * d * ff, bytes_accessed=d * ff * 2 + t * ff * 4, transcendentals=t * ff),
        name="mlp_in",
    )(normed, w, bias.reshape(1, -1))

def mlp_back_body(dy_ref, slope_ref, w1_ref, w2_ref, dpre_ref, db_ref, dn_ref):
    g = dot(dy_ref[...], w2_ref[...], NT) * slope_ref[...].astype(f32)
    low = g.astype(bf16)
    dpre_ref[...] = low
    db_ref[...] = jnp.sum(low.astype(f32), axis=0, keepdims=True)
    dn = dot(low, w1_ref[...], NT)
    @pl.when(pl.program_id(0) == 0)
    def _(): dn_ref[...] = dn
    @pl.when(pl.program_id(0) > 0)
    def _(): dn_ref[...] += dn

def mlp_back(dy, slope, w1, w2, block=512):
    t, d = dy.shape
    ff = w1.shape[1]
    whole = pl.BlockSpec((t, d), lambda i: (0, 0))
    part = pl.BlockSpec((t, block), lambda i: (0, i))
    return pl.pallas_call(
        mlp_back_body, grid=(ff // block,),
        in_specs=[whole, part, pl.BlockSpec((d, block), lambda i: (0, i)), pl.BlockSpec((block, d), lambda i: (i, 0))],
        out_specs=[part, pl.BlockSpec((1, block), lambda i: (0, i)), whole],
        out_shape=[jax.ShapeDtypeStruct((t, ff), bf16), jax.ShapeDtypeStruct((1, ff), f32), jax.ShapeDtypeStruct((t, d), f32)],
        compiler_params=pltpu.CompilerParams(vmem_limit_bytes=48 << 20),
        cost_estimate=pl.CostEstimate(flops=4 * t * d * ff, bytes_accessed=d * ff * 4 + t * ff * 4, transcendentals=0),
        name="mlp_back",
    )(dy, slope, w1, w2)

def side_steps(x, side):
    n = x.shape[0]
    b = lax.rem(lax.broadcasted_iota(jnp.int32, x.shape, 0), side)
    before = jnp.where(b == 0, 0.0, pltpu.roll(x, 1, 0))
    after = jnp.where(b == side - 1, 0.0, pltpu.roll(x, n - 1, 0))
    return before, after

def up(x, by):
    return jnp.concatenate([jnp.zeros((by, x.shape[1]), x.dtype), x[:-by]], 0)

def down(x, by):
    return jnp.concatenate([x[by:], jnp.zeros((by, x.shape[1]), x.dtype)], 0)

def adapter_body(n_pieces, side, pos_ref, *refs):
    pieces, (w_ref, table_ref, dy_ref, proj_ref, spat_ref, rows_ref, dg_ref, dys_ref) = refs[:n_pieces], refs[n_pieces:]
    x = table_ref[BIAS_PROJ : BIAS_PROJ + 1]
    for k in range(n_pieces):
        x = x + dot(pieces[k][...], w_ref[lax.rem(pos_ref[0] - k + n_pieces, n_pieces)])
    proj_ref[...] = x
    before, after = side_steps(x, side)
    w = table_ref[DEPTH : DEPTH + 9]
    y = [before * w[3 * s:3 * s + 1] + x * w[3 * s + 1:3 * s + 2] + after * w[3 * s + 2:3 * s + 3] for s in range(3)]
    spatial = up(y[0], side) + y[1] + down(y[2], side) + table_ref[BIAS_DEPTH : BIAS_DEPTH + 1]
    spat_ref[...] = spatial
    rows_ref[...] = jnp.sum(spatial, axis=0, keepdims=True)
    dy = dy_ref[...].astype(f32)
    dg_ref[...] = jnp.sum(dy * spatial, axis=0, keepdims=True)
    dys_ref[...] = jnp.sum(dy, axis=0, keepdims=True)

def adapter(pos, pieces, w_proj, table, dy, side=PS, block=256):
    t, d = dy.shape
    n, width = len(pieces), pieces[0].shape[1]
    whole = pl.BlockSpec((t, width), lambda i: (0, 0))
    part = pl.BlockSpec((t, block), lambda i: (0, i))
    row = pl.BlockSpec((1, block), lambda i: (0, i))
    big, line = jax.ShapeDtypeStruct((t, d), f32), jax.ShapeDtypeStruct((1, d), f32)
    return pl.pallas_call(
        functools.partial(adapter_body, n, side), grid=(d // block,),
        in_specs=[pl.BlockSpec(memory_space=pltpu.SMEM)] + [whole] * n + [pl.BlockSpec((n, width, block), lambda i: (0, 0, i)), pl.BlockSpec((table.shape[0], block), lambda i: (0, i)), part],
        out_specs=[part, part, row, row, row], out_shape=[big, big, line, line, line],
        compiler_params=pltpu.CompilerParams(vmem_limit_bytes=48 << 20),
        cost_estimate=pl.CostEstimate(flops=2 * t * d * n * width, bytes_accessed=t * d * 16, transcendentals=0),
        name="adapter",
    )(pos.reshape(1).astype(jnp.int32), *pieces, w_proj.reshape(n, width, d), table, dy)

def adapter_back_body(side, n_near, dy_ref, proj_ref, gate_ref, share_ref, *refs):
    near, (table_ref, dp_ref, dwd_ref, dbd_ref, dbp_ref) = refs[:n_near], refs[n_near:]
    d_rows = share_ref[0:1, :1] * near[0][...]
    for i in range(1, n_near):
        d_rows = d_rows + share_ref[i:i + 1, :1] * near[i][...]
    ds = dy_ref[...].astype(f32) * gate_ref[...] + d_rows
    dbd_ref[...] = jnp.sum(ds, axis=0, keepdims=True)
    before, after = side_steps(ds, side)
    w = table_ref[DEPTH : DEPTH + 9]
    y = [after * w[3 * s:3 * s + 1] + ds * w[3 * s + 1:3 * s + 2] + before * w[3 * s + 2:3 * s + 3] for s in range(3)]
    low = (down(y[0], side) + y[1] + up(y[2], side)).astype(bf16)
    dp_ref[...] = low
    dbp_ref[...] = jnp.sum(low.astype(f32), axis=0, keepdims=True)
    x = proj_ref[...]
    x_before, x_after = side_steps(x, side)
    for t, c in enumerate((x_before, x, x_after)):
        dwd_ref[t:t + 1] = jnp.sum(ds[side:] * c[:-side], axis=0, keepdims=True)
        dwd_ref[3 + t:4 + t] = jnp.sum(ds * c, axis=0, keepdims=True)
        dwd_ref[6 + t:7 + t] = jnp.sum(ds[:-side] * c[side:], axis=0, keepdims=True)

def adapter_back(dy, projected, gate, share, near, table, side=PS, block=256):
    t, d = dy.shape
    part = pl.BlockSpec((t, block), lambda i: (0, i))
    row = pl.BlockSpec((1, block), lambda i: (0, i))
    nine = pl.BlockSpec((9, block), lambda i: (0, i))
    line = jax.ShapeDtypeStruct((1, d), f32)
    return pl.pallas_call(
        functools.partial(adapter_back_body, side, len(near)), grid=(d // block,),
        in_specs=[part, part, row, pl.BlockSpec((len(near), 128), lambda i: (0, 0))] + [row] * len(near) + [pl.BlockSpec((table.shape[0], block), lambda i: (0, i))], out_specs=[part, nine, row, row],
        out_shape=[jax.ShapeDtypeStruct((t, d), bf16), jax.ShapeDtypeStruct((9, d), f32), line, line],
        compiler_params=pltpu.CompilerParams(vmem_limit_bytes=48 << 20),
        cost_estimate=pl.CostEstimate(flops=60 * t * d, bytes_accessed=t * d * 8, transcendentals=0),
        name="adapter_back",
    )(dy, projected, gate, share, *near, table)

def dot3(x, w, dims=NN):
    a = x.astype(bf16)
    rest = x - a.astype(f32)
    b = rest.astype(bf16)
    c = (rest - b.astype(f32)).astype(bf16)
    return dot(a, w, dims) + dot(b, w, dims) + dot(c, w, dims)


def gate_body(n_near, tokens, *refs):
    near, refs = refs[:n_near], refs[n_near:]
    dg_ref, win_ref, wout_ref, gate_ref, dmean_ref, share_ref, factors_ref = refs
    d = dg_ref.shape[1]
    own = near[0][:, d:]
    match = [(near[i][:, d:] == own).astype(f32) for i in range(n_near)]
    count = functools.reduce(lambda a, b: a + b, match) * tokens
    share = [m / count for m in match]
    for i in range(n_near):
        share_ref[i : i + 1] = share[i]
    mean = share[0][:, :1] * near[0][:, :d]
    for i in range(1, n_near):
        mean = mean + share[i][:, :1] * near[i][:, :d]

    def tall(v):
        return jnp.broadcast_to(v, (8, v.shape[1]))

    win, wout = win_ref[...], wout_ref[...]
    act, slope = gelu_parts(dot3(tall(mean), win))
    gate = jnp.tanh(dot3(act, wout, NT))
    d_pre = dg_ref[...] * (1.0 - gate * gate)
    d_hidden = dot3(d_pre, wout) * slope
    d_mean = dot3(d_hidden, win, NT)
    gate_ref[...] = gate[:1]
    dmean_ref[...] = d_mean[:1]
    parts = (mean, d_pre[:1], d_hidden[:1], act[:1], jnp.zeros((1, 128), f32) + jnp.sum(gate[:1]))
    at = 0
    for v in parts:
        factors_ref[:, at : at + v.shape[1]] = v
        at += v.shape[1]


def gate_step(near, d_gate, mixed_w, d, hidden, tokens):
    n = len(near)

    def line(k):
        return jax.ShapeDtypeStruct((1, k), f32)

    def at(k, i=0):
        return pl.BlockSpec((1, k), lambda j: (0, 0))

    k = 2 * d + 2 * hidden + 128
    return pl.pallas_call(
        functools.partial(gate_body, n, tokens),
        grid=(1,),
        in_specs=[at(d + 128)] * n
        + [at(d)]
        + [pl.BlockSpec((d, hidden), lambda j, b=b: (0, b)) for b in range(2)],
        out_specs=[at(d), at(d), pl.BlockSpec((n, 128), lambda j: (0, 0)), at(k)],
        out_shape=[line(d), line(d), jax.ShapeDtypeStruct((n, 128), f32), line(k)],
        compiler_params=pltpu.CompilerParams(vmem_limit_bytes=32 << 20),
        name="gate",
    )(*near, d_gate, mixed_w, mixed_w)


def pool_table(coarse_side, fine_side):
    coarse, fine = np.arange(coarse_side)[:, None], np.arange(fine_side)[None]
    start = coarse * fine_side // coarse_side
    end = ((coarse + 1) * fine_side + coarse_side - 1) // coarse_side
    single = np.where((fine >= start) & (fine < end), 1.0, 0.0) / (end - start)
    return np.kron(single, single)


def token_sum(values):
    return jnp.sum(values.astype(f32), axis=0)


def shards(
    tokens,
    features,
    sample_of,
    cotangent,
    ln1_gain,
    ln1_bias,
    w_qkv,
    bias_qv,
    w_attn_out,
    bias_attn_out,
    ln2_gain,
    ln2_bias,
    w_fc1,
    bias_fc1,
    w_fc2,
    bias_fc2,
    w_proj,
    bias_proj,
    w_depth,
    bias_depth,
    w_gate_in,
    w_gate_out,
):
    grid = Grid()
    rows = ln1_gain.shape[0]
    total = grid.total
    x, dy = tokens[0], cotangent[0]
    count, d = x.shape
    hidden = w_gate_in.shape[1]

    vectors = [ln1_gain, ln1_bias, bias_attn_out, ln2_gain, ln2_bias, bias_fc2, bias_proj, bias_depth]
    a_small = GatherSmall(
        grid, jnp.concatenate(vectors + [w_depth.reshape(-1), bias_qv, bias_fc1])
    )
    full_qkv = lax.all_gather(w_qkv, AXES, axis=0, tiled=True)
    full_fc2 = lax.all_gather(w_fc2, AXES, axis=0, tiled=True)
    gate_out_rows = dot(jnp.eye(rows, dtype=bf16), w_gate_out, NT).astype(bf16)
    gates = jnp.concatenate([w_gate_in, gate_out_rows], 1)
    held = -(-rows // 16) * 16
    a_mixed = Gather(
        grid,
        jnp.concatenate(
            [jnp.pad(w, ((0, held - rows), (0, 0))) for w in (w_attn_out, gates)] + [w_proj], 0
        ),
    )
    a_fc1 = Gather(grid, w_fc1)

    n_ch = lax.axis_size("ch")
    ch = lax.axis_index("ch")
    n_img, own_ch = features.shape[0], features.shape[1]
    core = grid.pos["c"]

    def along_ch(v, by):
        img = lax.axis_size("img")
        pairs = [
            (i * n_ch + j, i * n_ch + (j + by) % n_ch) for i in range(img) for j in range(n_ch)
        ]
        return lax.ppermute(v, AXES, pairs)

    def peer(v):
        return grid.send(v, "c", 1)

    def peer_half(v):
        h = v.shape[1] // 2
        return grid.send(lax.dynamic_slice(v, (0, (1 - core) * h), (v.shape[0], h)), "c", 1)

    def step(active, *values):
        states, values = lax.optimization_barrier(([a.state() for a in active], values))
        for a, state in zip(active, states):
            a.set_state(state)
        return values

    a_mixed.along_z()
    pool = jnp.asarray(pool_table(PS, FS), bf16)
    pooled_own = dot(pool, features.reshape(n_img * own_ch, -1), NT).astype(bf16)
    pieces = []
    for k in range(n_ch):
        to = lax.rem(ch + k, n_ch)
        piece = lax.dynamic_slice(pooled_own, (0, to * own_ch), (count, own_ch))
        pieces.append(along_ch(piece, k) if k else piece)
    for _ in range(4):
        every = a_small.next()
    every, pieces = step((a_mixed, a_fc1), every, pieces)

    a_mixed.first()
    a_fc1.along_z()
    every = every.astype(f32)
    table = every[:, : LINES * rows].reshape(total, LINES, rows)
    table = table.transpose(1, 0, 2).reshape(LINES, d)
    at = LINES * rows
    full_bias_qv = every[:, at : at + 2 * rows].reshape(-1)
    full_bias_fc1 = every[:, at + 2 * rows :].reshape(1, -1)
    bias_qkv = jnp.concatenate([full_bias_qv[:d], jnp.zeros((d,), f32), full_bias_qv[d:]])
    x32 = x.astype(f32)
    normed1 = layer_norm(x32, table[LN1_GAIN], table[LN1_BIAS]).astype(bf16)
    pooled = jnp.zeros((count, n_ch * own_ch), bf16)
    for k in range(n_ch):
        from_ch = lax.rem(ch - k + n_ch, n_ch)
        pooled = lax.dynamic_update_slice(pooled, pieces[k], (0, from_ch * own_ch))
    dy_far = peer_half(dy)
    normed1, table, full_bias_fc1, bias_qkv, pooled, dy_far = step(
        (a_mixed, a_fc1), normed1, table, full_bias_fc1, bias_qkv, pooled, dy_far
    )

    a_mixed.second()
    a_fc1.first()
    qkv = (dot(normed1, full_qkv) + bias_qkv).astype(bf16)
    attended, log_total = attend(qkv)
    a_mixed.cross()
    normed1_far, pooled_far = peer(normed1), peer(pooled)
    attended, log_total, normed1_far, pooled_far = step(
        (a_mixed, a_fc1), attended, log_total, normed1_far, pooled_far
    )

    a_fc1.second()
    mixed_w = a_mixed.whole().reshape(total, -1, d)
    full_attn_out = mixed_w[:, :rows].reshape(d, d)
    full_gates = mixed_w[:, held : held + rows].reshape(d, 2 * hidden)
    full_proj = mixed_w[:, 2 * held :].reshape(-1, d)
    first_sum = x32 + dot(attended, full_attn_out) + table[BIAS_OUT]
    normed2 = layer_norm(first_sum, table[LN2_GAIN], table[LN2_BIAS]).astype(bf16)
    projected, spatial, row_sums, d_gate, dy_sum = adapter(ch, pieces, full_proj, table, dy)
    ids_plus = sample_of.astype(f32) + 1.0
    carried = jnp.concatenate([row_sums, jnp.broadcast_to(ids_plus[:, None], (1, 128))], 1)
    near = neighbours(grid, carried, REACH)
    attended_far = peer(attended)
    normed2, near, attended_far, full_gates, full_proj, full_attn_out = step(
        (a_fc1,), normed2, near, attended_far, full_gates, full_proj, full_attn_out
    )

    a_fc1.cross()
    gate, d_mean, share, factors = gate_step(near, d_gate, full_gates, d, hidden, count)
    near_dmean = neighbours(grid, d_mean, REACH)
    normed2_far = peer(normed2)
    full_fc1 = a_fc1.whole()
    activation, slope = mlp_in(normed2, full_fc1, full_bias_fc1)
    activation, slope, near_dmean, full_fc1, normed2_far, factors = step(
        (), activation, slope, near_dmean, full_fc1, normed2_far, factors
    )

    activation_far = peer(activation)
    a_factors = GatherSmall(grid, factors[0])
    a_factors.next()
    d_projected, d_depth, d_bias_depth, d_bias_proj = adapter_back(
        dy, projected, gate, share, near_dmean, table
    )
    d_pooled = dot(d_projected, full_proj, NT).astype(bf16)
    activation_far, d_projected, d_pooled, a_factors.v = step(
        (), activation_far, d_projected, d_pooled, a_factors.v
    )

    s_fc2 = Scatter(grid, activation, activation_far, dy, dy_far)
    a_factors.next()
    d_projected_far = peer_half(d_projected)
    back = []
    for k in range(n_ch):
        to = lax.rem(ch + k, n_ch)
        piece = lax.dynamic_slice(d_pooled, (0, to * own_ch), (count, own_ch))
        back.append(along_ch(piece, k) if k else piece)
    slope, d_projected_far, back, a_factors.v = step(
        (s_fc2,), slope, d_projected_far, back, a_factors.v
    )

    s_fc2.first()
    a_factors.next()
    d_pre, d_bias_fc1, d_normed2 = mlp_back(dy, slope, full_fc1, full_fc2)
    s_proj = Scatter(grid, pooled, pooled_far, d_projected, d_projected_far)
    d_pre, d_bias_fc1, d_normed2, full_fc2, back, a_factors.v = step(
        (s_fc2, s_proj), d_pre, d_bias_fc1, d_normed2, full_fc2, back, a_factors.v
    )

    s_fc2.second()
    s_proj.first()
    d_pre_far = peer_half(d_pre)
    _, norm_two_back = jax.vjp(layer_norm, first_sum, table[LN2_GAIN], table[LN2_BIAS])
    d_first_norm, d_ln2_gain, d_ln2_bias = norm_two_back(d_normed2)
    d_first = dy.astype(f32) + d_first_norm
    d_branch = d_first.astype(bf16)
    d_branch_far = peer_half(d_branch)
    d_attended = dot(d_branch, full_attn_out, NT).astype(bf16)
    d_local = jnp.zeros((n_img, count, own_ch), bf16)
    for k in range(n_ch):
        from_ch = lax.rem(ch - k + n_ch, n_ch)
        d_local = lax.dynamic_update_slice(d_local, back[k][None], (from_ch, 0, 0))
    grad_features = jnp.einsum("kpc,pf->kcf", d_local, pool, preferred_element_type=f32).astype(bf16)
    d_attended, d_first, d_pre_far, d_branch_far, grad_features, a_factors.v = step(
        (s_fc2, s_proj), d_attended, d_first, d_pre_far, d_branch_far, grad_features, a_factors.v
    )

    s_fc2.along_z()
    s_proj.second()
    s_fc1 = Scatter(grid, normed2, normed2_far, d_pre, d_pre_far)
    s_attn = Scatter(grid, attended, attended_far, d_branch, d_branch_far)
    (d_attended,) = step((s_fc2, s_proj, s_fc1, s_attn), d_attended)

    s_fc1.first()
    s_attn.first()
    s_proj.along_z()
    d_query, d_key, d_value = attend_back(qkv, d_attended, log_total)
    d_mixed = jnp.concatenate([d_query, d_key, d_value], -1)
    d_mixed, activation, a_factors.v, s_fc2.kept = step(
        (s_fc1, s_attn, s_proj), d_mixed, activation, a_factors.v, s_fc2.kept
    )

    s_fc1.second()
    s_attn.second()
    s_fc2.last()
    d_mixed_far = peer_half(d_mixed)
    second_sum = first_sum + dot(activation, full_fc2) + table[BIAS_FC2]
    layer_out = (second_sum + gate * spatial).astype(bf16)
    d_normed1 = dot(d_mixed, full_qkv, NT)
    d_mixed_far, layer_out, d_normed1, d_mixed = step(
        (s_fc1, s_attn, s_fc2, s_proj), d_mixed_far, layer_out, d_normed1, d_mixed
    )

    s_fc1.along_z()
    s_proj.last()
    a_factors.next()
    s_qkv = Scatter(grid, normed1, normed1_far, d_mixed, d_mixed_far)
    _, norm_one_back = jax.vjp(layer_norm, x32, table[LN1_GAIN], table[LN1_BIAS])
    d_input, d_ln1_gain, d_ln1_bias = norm_one_back(d_normed1)
    grad_tokens = (d_first + d_input).astype(bf16)
    lines = [
        d_ln1_gain,
        d_ln1_bias,
        token_sum(d_branch),
        d_ln2_gain,
        d_ln2_bias,
        dy_sum[0],
        d_bias_proj[0],
        d_bias_depth[0],
    ]
    stacked = jnp.concatenate([jnp.stack(lines), d_depth], 0)
    stacked = stacked.reshape(LINES, total, rows).transpose(1, 0, 2).reshape(total, -1)
    d_bias_qv = jnp.concatenate([token_sum(d_query), token_sum(d_value)])
    s_small = ScatterSmall(
        grid,
        jnp.concatenate([stacked, d_bias_qv.reshape(total, -1), d_bias_fc1.reshape(total, -1)], 1),
    )
    s_small.v, grad_tokens, a_factors.v = step(
        (s_fc1, s_attn, s_qkv, s_fc2, s_proj), s_small.v, grad_tokens, a_factors.v
    )

    s_qkv.first()
    s_attn.along_z()
    s_fc1.last()
    s_small.next()
    g_fc2, g_proj = s_fc2.result(), s_proj.result()
    g_fc2, g_proj, s_small.v = step((s_fc1, s_attn, s_qkv), g_fc2, g_proj, s_small.v)

    s_qkv.second()
    s_attn.last()
    s_small.next()
    s_small.next()
    all_factors = a_factors.v
    g_fc1 = s_fc1.result()
    s_small.v, g_fc1, all_factors = step((s_attn, s_qkv), s_small.v, g_fc1, all_factors)

    s_qkv.along_z()
    summed = s_small.next()[0]
    g_attn_out = s_attn.result()
    own_cols = grid.me * rows
    g_gate_in = lax.dot_general(
        lax.dynamic_slice(all_factors, (0, own_cols), (total, rows)),
        all_factors[:, 2 * d : 2 * d + hidden],
        TN,
        precision=highest,
    )
    g_gate_out = lax.dot_general(
        all_factors[:, 2 * d + hidden : 2 * d + 2 * hidden],
        lax.dynamic_slice(all_factors, (0, d + own_cols), (total, rows)),
        TN,
        precision=highest,
    )
    gate_mean = jnp.sum(all_factors[:, -1]) / (total * d)
    summed, g_gate_in, g_gate_out, gate_mean = step(
        (s_qkv,), summed, g_gate_in, g_gate_out, gate_mean
    )
    s_qkv.last()
    g_qkv = s_qkv.result()

    def owned(i):
        return summed[i * rows : (i + 1) * rows]

    return (
        layer_out[None],
        grad_tokens[None],
        grad_features,
        owned(LN1_GAIN),
        owned(LN1_BIAS),
        g_qkv,
        summed[at : at + 2 * rows],
        g_attn_out,
        owned(BIAS_OUT),
        owned(LN2_GAIN),
        owned(LN2_BIAS),
        g_fc1,
        summed[at + 2 * rows :],
        g_fc2,
        owned(BIAS_FC2),
        g_proj,
        owned(BIAS_PROJ),
        summed[DEPTH * rows : at].reshape(9, rows),
        owned(BIAS_DEPTH),
        g_gate_in,
        g_gate_out,
        gate_mean,
    )


def solution(mesh):
    return jax.shard_map(
        shards,
        mesh=mesh,
        in_specs=(
            P(("img", "ch"), None, None),
            P("img", "ch", None),
            P(("img", "ch")),
            P(("img", "ch"), None, None),
            P(("img", "ch")),
            P(("img", "ch")),
            P(("img", "ch"), None),
            P(("img", "ch")),
            P(("img", "ch"), None),
            P(("img", "ch")),
            P(("img", "ch")),
            P(("img", "ch")),
            P(("img", "ch"), None),
            P(("img", "ch")),
            P(("img", "ch"), None),
            P(("img", "ch")),
            P(("img", "ch"), None),
            P(("img", "ch")),
            P(None, ("img", "ch")),
            P(("img", "ch")),
            P(("img", "ch"), None),
            P(None, ("img", "ch")),
        ),
        out_specs=(
            P(("img", "ch"), None, None),
            P(("img", "ch"), None, None),
            P("img", "ch", None),
            P(("img", "ch")),
            P(("img", "ch")),
            P(("img", "ch"), None),
            P(("img", "ch")),
            P(("img", "ch"), None),
            P(("img", "ch")),
            P(("img", "ch")),
            P(("img", "ch")),
            P(("img", "ch"), None),
            P(("img", "ch")),
            P(("img", "ch"), None),
            P(("img", "ch")),
            P(("img", "ch"), None),
            P(("img", "ch")),
            P(None, ("img", "ch")),
            P(("img", "ch")),
            P(("img", "ch"), None),
            P(None, ("img", "ch")),
            P(),
        ),
        check_vma=False,
    )
```

time: 957 us -> 656 us (0.69)
  matrix products: 272 us -> 41.5 us
  Pallas kernels: 10.8 us -> 146 us
  waiting for transfers between devices: 235 us -> 144 us
  starting transfers between devices: 194 us -> 147 us
  other arithmetic: 112 us -> 73.1 us
  local copies, waits for them, and re-layouts: 115 us -> 76.8 us
  between operations: 7.21 us -> 19.5 us
    dot_general x36 -> x11, matrix products: 272 us -> 41.5 us  [the longest x8 33.8 us: dot(): return lax.dot_general(a, b, dims, preferred_element_type=f32)]
    pallas_call x5 -> x14, Pallas kernels: 10.8 us -> 146 us  [the longest x5 46.7 us: wgrad(): pl.pallas_call(functools.partial(wgrad_body, (nx, ny), r2), grid_spec=plt...]
    ppermute x133 -> x94, waiting for transfers between devices: 232 us -> 122 us  [send(): return lax.ppermute(v, AXES, pairs)]
    ppermute x133 -> x94, starting transfers between devices: 151 us -> 100 us  [send(): return lax.ppermute(v, AXES, pairs)]
    reduce_sum x8 -> x4, other arithmetic: 44.9 us -> 4.84 us  [the longest x3 3.45 us: token_sum(): return jnp.sum(values.astype(f32), axis=0)]
    convert_element_type x25 -> x10, local copies, waits for them, and re-layouts: 22.9 us -> 1.6 us  [along_z(): away = jnp.concatenate([t.astype(bf16) for t in at(g.other('z', k))], 1)]
    ppermute x0 -> x6, waiting for transfers between devices: none -> 21 us  [along_ch(): return lax.ppermute(v, AXES, pairs)]
    unnamed x319 -> x259, local copies, waits for them, and re-layouts: 30.8 us -> 12.7 us
  transfers between devices with their start and end apart: 147 -> 114, of which waited for: 46 -> 30; matrix products, arithmetic and copies ran while one was open for 47% -> 24% of each run, Pallas kernels for 1% -> 23%
where the time goes in v2:
time: 656 us; the launch traced here: 648 us
  starting transfers between devices  147 us (22%)
  Pallas kernels  146 us (22%)
  waiting for transfers between devices  144 us (22%)
  local copies, waits for them, and re-layouts  76.8 us (12%)
  other arithmetic  73.1 us (11%)
  matrix products  41.5 us (6%)
  between operations  19.5 us (3%)
    ppermute x94, waiting for transfers between devices, send(): return lax.ppermute(v, AXES, pairs)  122 us
    ppermute x94, starting transfers between devices, send(): return lax.ppermute(v, AXES, pairs)  100 us
    pallas_call x5, Pallas kernels, wgrad(): pl.pallas_call(functools.partial(wgrad_body, (nx, ny), r2), grid_spec=plt...  46.7 us
    ppermute x12, starting transfers between devices, neighbours(): out.append(lax.ppermute(v, AXES, pairs))  40.2 us
    dot_general x8, matrix products, dot(): return lax.dot_general(a, b, dims, preferred_element_type=f32)  33.8 us
    pallas_call x1, Pallas kernels, attend_back(): pl.pallas_call(attend_back_body, grid=(n,), in_specs=[spec(0), spec(1), s...  25.3 us
    ppermute x6, waiting for transfers between devices, along_ch(): return lax.ppermute(v, AXES, pairs)  21 us
    pallas_call x1, Pallas kernels, mlp_back(): pl.pallas_call(mlp_back_body, grid=(ff // block,), in_specs=[whole, part,...  16.9 us
  transfers between devices with their start and end apart: 114, of which 30 were waited for; matrix products, arithmetic and copies ran while one was open for 24% of the time, Pallas kernels for 23%

profile of v2, /device:TPU:9, one launch (start us, length us, event | category | flops | bytes accessed | tf_op | source)
XLA Modules:
  0.0 647.5 jit_solution(16064059570978865254)
XLA Ops:
  14.6 6.8 %concatenate.155 = bf16[736]{0:T(1024)(128)(2,1)S(1)} concatenate(bf16[32]{0:T(256)(128)(2,1)} %param.27, bf16[32]{0:T(256)(128)(2,1)} %param.28, bf16[32]{0:T(256)(128)(2,1)} %param.32, bf16[32]{0:T(256)(128)(2,1)} %param.33, bf16[32]{0:T(256)(128)(2,1)} %param.34, bf16[32]{0:T(256)(128)(2,1)} %param.38, bf16[32]{0:T(256)(128)(2,1)} %param.40, bf16[32]{0:T(256)(128)(2,1)} %param.42, ...), dimensions={0} | concatenate | bytes 2944 | tf_op jit(solution)/shard_map/concatenate | solution.py:627
  30.2 5.0 collective-permute-done.4
  50.4 8.0 %collective-permute-done.10.refs_2_ = bf16[576,384]{1,0:T(8,128)(2,1)} collective-permute-done((bf16[576,384]{1,0:T(8,128)(2,1)}, bf16[576,384]{1,0:T(8,128)(2,1)}, u32[]{:S(2)}, u32[]{:S(2)}) %collective-permute-start.10) | collective-permute-done | bytes 442400 | tf_op jit(solution)/shard_map/ppermute | solution.py:652
  58.3 6.1 collective-permute-done.11.refs_3_
  64.6 5.8 collective-permute-start.15
  88.9 13.4 %collective-permute-done.15 = bf16[32,4096]{1,0:T(8,128)(2,1)} collective-permute-done((bf16[32,4096]{1,0:T(8,128)(2,1)}, bf16[32,4096]{1,0:T(8,128)(2,1)}, u32[]{:S(2)}, u32[]{:S(2)}) %collective-permute-start.15) | collective-permute-done | bytes 262176 | tf_op jit(solution)/shard_map/ppermute | solution.py:45
  116.0 32.5 %collective-permute-done.26.refs_1_ = bf16[4,32,2048]{2,1,0:T(8,128)(2,1)S(1)} collective-permute-done((bf16[4,32,2048]{2,1,0:T(8,128)(2,1)S(1)}, bf16[4,32,2048]{2,1,0:T(8,128)(2,1)S(1)}, u32[]{:S(2)}, u32[]{:S(2)}) %collective-permute-start.26) | collective-permute-done | bytes 524320 | tf_op jit(solution)/shard_map/ppermute | solution.py:45
  152.9 8.8 %add_convert_fusion.q_ref.k_ref.v_ref = bf16[576,3072]{1,0:T(8,128)(2,1)} fusion(bf16[576,1024]{1,0:T(8,128)(2,1)} %fusion.9.l0, bf16[1024,3072]{1,0:T(8,128)(2,1)} %all-gather.3.cloned.1.call-done, f32[3072]{0:T(1024)S(1)} %copy-done.115), kind=kOutput, calls=%fused_computation | convolution fusion | flops 3627417600 | bytes 11022336 | tf_op jit(solution)/shard_map/dot_general | solution.py:312
  161.7 15.0 %attend.1 = (bf16[576,1024]{1,0:T(8,128)(2,1)S(1)}, f32[576,1024]{1,0:T(8,128)S(1)}) custom-call(bf16[576,3072]{1,0:T(8,128)(2,1)} %add_convert_fusion.q_ref.k_ref.v_ref, bf16[576,3072]{1,0:T(8,128)(2,1)} %add_convert_fusion.q_ref.k_ref.v_ref, bf16[576,3072]{1,0:T(8,128)(2,1)} %add_convert_fusion.q_ref.k_ref.v_ref), custom_call_target="tpu_custom_call" | custom-call | flops 1358954496 | bytes 7077888 | tf_op jit(solution)/shard_map/attend/pallas_call | solution.py:335
  183.4 8.2 %adapter.1 = (f32[576,1024]{1,0:T(8,128)S(1)}, f32[576,1024]{1,0:T(8,128)}, f32[1,1024]{1,0:T(1,128)S(1)}, f32[1,1024]{1,0:T(1,128)S(1)}, f32[1,1024]{1,0:T(1,128)S(1)}) custom-call(s32[1]{0:T(128)} %bitcast.39.pos_ref, bf16[576,384]{1,0:T(8,128)(2,1)S(1)} %copy-done.15, bf16[576,384]{1,0:T(8,128)(2,1)S(1)} %copy-done.28, ...), custom_call_target="tpu_custom_call" | custom-call | flops 1811939328 | bytes 9437184 | tf_op jit(solution)/shard_map/adapter/pallas_call | solution.py:475
  203.8 4.7 collective-permute-start.40
  222.0 18.7 %collective-permute-done.34.refs_2_ = bf16[8,32,2048]{2,1,0:T(8,128)(2,1)S(1)} collective-permute-done((bf16[8,32,2048]{2,1,0:T(8,128)(2,1)S(1)}, bf16[8,32,2048]{2,1,0:T(8,128)(2,1)S(1)}, u32[]{:S(2)}, u32[]{:S(2)}) %collective-permute-start.34) | collective-permute-done | bytes 1048608 | tf_op jit(solution)/shard_map/ppermute | solution.py:45
  253.0 5.1 collective-permute-start.48
  267.7 4.5 collective-permute-start.50
  272.3 15.9 %mlp_in.1 = (bf16[576,4096]{1,0:T(8,128)(2,1)}, bf16[576,4096]{1,0:T(8,128)(2,1)}) custom-call(bf16[576,1024]{1,0:T(8,128)(2,1)S(1)} %add_convert_fusion.3.n_ref.l0, bf16[1024,4096]{1,0:T(8,128)(2,1)} %bitcast.324, f32[1,4096]{1,0:T(1,128)S(1)} %bitcast.326), custom_call_target="tpu_custom_call" | custom-call | flops 4831838208 | bytes 17825792 | tf_op jit(solution)/shard_map/mlp_in/pallas_call | solution.py:404
  295.2 8.3 %adapter_back.1 = (bf16[576,1024]{1,0:T(8,128)(2,1)S(1)}, f32[9,1024]{1,0:T(8,128)S(1)}, f32[1,1024]{1,0:T(1,128)S(1)}, f32[1,1024]{1,0:T(1,128)S(1)}) custom-call(bf16[576,1024]{1,0:T(8,128)(2,1)S(1)} %bitcast.322, f32[576,1024]{1,0:T(8,128)S(1)} %copy-done.9, f32[1,1024]{1,0:T(1,128)S(1)} %get-tuple-element.373.gate_ref, ...), custom_call_target="tpu_custom_call" | custom-call | flops 35389440 | bytes 4718592 | tf_op jit(solution)/shard_map/adapter_back/pallas_call | solution.py:510
  316.2 11.6 %weight_grad.5 = (bf16[4,2,256,256]{3,2,1,0:T(8,128)(2,1)}, bf16[4,2,256,256]{3,2,1,0:T(8,128)(2,1)}, bf16[4,2,256,256]{3,2,1,0:T(8,128)(2,1)}, bf16[4,2,256,256]{3,2,1,0:T(8,128)(2,1)}) custom-call(s32[3]{0:T(128)} %pad_add_fusion.pos_ref, bf16[576,4096]{1,0:T(8,128)(2,1)} %get-tuple-element.495.l0, bf16[576,4096]{1,0:T(8,128)(2,1)} %collective-permute-done.52.l1, ...), custom_call_target="tpu_custom_call" | custom-call | tf_op jit(solution)/shard_map/weight_grad/pallas_call | solution.py:218
  328.6 6.0 collective-permute-done.56
  341.2 16.9 %mlp_back.1 = (bf16[576,4096]{1,0:T(8,128)(2,1)}, f32[1,4096]{1,0:T(1,128)S(1)}, f32[576,1024]{1,0:T(8,128)S(1)}) custom-call(bf16[576,1024]{1,0:T(8,128)(2,1)S(1)} %bitcast.323, bf16[576,4096]{1,0:T(8,128)(2,1)} %get-tuple-element.405.slope_ref, bf16[1024,4096]{1,0:T(8,128)(2,1)} %bitcast.325, bf16[4096,1024]{1,0:T(8,128)(2,1)} %all-gather.5.cloned.1.call-done.w2_ref), custom_call_target="tpu_custom_call" | custom-call | flops 9663676416 | bytes 26214400 | tf_op jit(solution)/shard_map/mlp_back/pallas_call | solution.py:429
  358.1 6.9 %weight_grad.6 = (bf16[4,2,96,256]{3,2,1,0:T(8,128)(2,1)}, bf16[4,2,96,256]{3,2,1,0:T(8,128)(2,1)}, bf16[4,2,96,256]{3,2,1,0:T(8,128)(2,1)}, bf16[4,2,96,256]{3,2,1,0:T(8,128)(2,1)}) custom-call(s32[3]{0:T(128)} %pad_add_fusion.pos_ref, bf16[576,1536]{1,0:T(8,128)(2,1)} %constant_dynamic-update-slice_fusion.l0, ...), custom_call_target="tpu_custom_call" | custom-call | tf_op jit(solution)/shard_map/weight_grad/pallas_call | solution.py:218
  384.5 4.0 convolution_convert_fusion.2
  389.9 5.4 collective-permute-done.64
  400.1 5.5 collective-permute-done.65
  413.9 12.1 %weight_grad.7 = (bf16[4,2,64,1024]{3,2,1,0:T(8,128)(2,1)}, bf16[4,2,64,1024]{3,2,1,0:T(8,128)(2,1)}, bf16[4,2,64,1024]{3,2,1,0:T(8,128)(2,1)}, bf16[4,2,64,1024]{3,2,1,0:T(8,128)(2,1)}) custom-call(s32[3]{0:T(128)} %pad_add_fusion.pos_ref, bf16[576,1024]{1,0:T(8,128)(2,1)} %copy-done.5, bf16[576,1024]{1,0:T(8,128)(2,1)} %copy-done.47, ...), custom_call_target="tpu_custom_call" | custom-call | tf_op jit(solution)/shard_map/weight_grad/pallas_call | solution.py:218
  426.0 6.0 weight_grad.8
  443.9 25.3 %attend_back.1 = (bf16[576,1024]{1,0:T(8,128)(2,1)S(1)}, bf16[576,1024]{1,0:T(8,128)(2,1)S(1)}, bf16[576,1024]{1,0:T(8,128)(2,1)S(1)}) custom-call(bf16[576,3072]{1,0:T(8,128)(2,1)} %add_convert_fusion.q_ref.k_ref.v_ref, bf16[576,3072]{1,0:T(8,128)(2,1)} %add_convert_fusion.q_ref.k_ref.v_ref, bf16[576,3072]{1,0:T(8,128)(2,1)} %add_convert_fusion.q_ref.k_ref.v_ref, ...), custom_call_target="tpu_custom_call" | custom-call | flops 3397386240 | bytes 14155776 | tf_op jit(solution)/shard_map/attend_back/pallas_call | solution.py:375
  498.0 9.0 %fusion.100 = f32[576,1024]{1,0:T(8,128)S(1)} fusion(bf16[576,4096]{1,0:T(8,128)(2,1)} %get-tuple-element.495.l0, bf16[4096,1024]{1,0:T(8,128)(2,1)} %all-gather.5.cloned.1.call-done.w2_ref), kind=kOutput, calls=%fused_computation.338 | convolution fusion | flops 4831838208 | bytes 15466496 | tf_op jit(solution)/shard_map/dot_general | solution.py:312
  514.7 10.9 %collective-permute-start.85 = (bf16[576,1536]{1,0:T(8,128)(2,1)S(1)}, bf16[576,1536]{1,0:T(8,128)(2,1)S(1)}, u32[]{:S(2)}, u32[]{:S(2)}) collective-permute-start(bf16[576,1536]{1,0:T(8,128)(2,1)S(1)} %constant_dynamic-slice_fusion.24), channel_id=1, source_target_pairs={{0,1},{1,0},{2,3},{3,2},{4,5},{5,4},{6,7},{7,6},{8,9},{9,8},{10,11... | collective-permute-start | bytes 5308424 | tf_op jit(solution)/shard_map/ppermute | solution.py:45
  557.7 10.1 %weight_grad.9 = (bf16[4,2,64,768]{3,2,1,0:T(8,128)(2,1)}, bf16[4,2,64,768]{3,2,1,0:T(8,128)(2,1)}, bf16[4,2,64,768]{3,2,1,0:T(8,128)(2,1)}, bf16[4,2,64,768]{3,2,1,0:T(8,128)(2,1)}) custom-call(s32[3]{0:T(128)} %pad_add_fusion.pos_ref, bf16[576,1024]{1,0:T(8,128)(2,1)} %fusion.9.l0, bf16[576,1024]{1,0:T(8,128)(2,1)} %collective-permute-done.28.l1, ...), custom_call_target="tpu_custom_call" | custom-call | tf_op jit(solution)/shard_map/weight_grad/pallas_call | solution.py:218
  597.6 7.8 %collective-permute-done.105 = f32[4,736]{1,0:T(4,128)S(1)} collective-permute-done((f32[4,736]{1,0:T(4,128)S(1)}, f32[4,736]{1,0:T(4,128)S(1)}, u32[]{:S(2)}, u32[]{:S(2)}) %collective-permute-start.105) | collective-permute-done | bytes 11808 | tf_op jit(solution)/shard_map/ppermute | solution.py:45
  624.9 3.9 collective-permute-done.108
  628.9 4.2 collective-permute-done.109
  (694 shorter events, 315.8 us)
Async XLA Ops:
  7.2 145.6 %all-gather.3.cloned.1.call-start = ((), (), s32[]{:S(2)}) async-start(), calls=%async_computation | async-start | bytes 6488064 | tf_op jit(solution)/shard_map/all_gather | solution.py:629
  7.9 333.3 %all-gather.5.cloned.1.call-start = ((), (), s32[]{:S(2)}) async-start(), calls=%async_computation.1 | async-start | bytes 8650752 | tf_op jit(solution)/shard_map/all_gather | solution.py:630
  10.0 38.9 %collective-permute-start = (bf16[112,1024]{1,0:T(8,128)(2,1)S(1)}, bf16[112,1024]{1,0:T(8,128)(2,1)}, u32[]{:S(2)}, u32[]{:S(2)}) collective-permute-start(bf16[112,1024]{1,0:T(8,128)(2,1)S(1)} %pad_maximum_fusion.18), channel_id=1, source_target_pairs={{0,8},{1,9},{2,10},{3,11},{4,12},{5,13},{6,14},{7,15},{8,16},{9,17... | collective-permute-start | bytes 688136 | tf_op jit(solution)/shard_map/ppermute | solution.py:45
  11.3 38.9 %collective-permute-start.1 = (bf16[112,1024]{1,0:T(8,128)(2,1)S(1)}, bf16[112,1024]{1,0:T(8,128)(2,1)}, u32[]{:S(2)}, u32[]{:S(2)}) collective-permute-start(bf16[112,1024]{1,0:T(8,128)(2,1)S(1)} %pad_maximum_fusion.18), channel_id=1, source_target_pairs={{0,16},{1,17},{2,18},{3,19},{4,20},{5,21},{6,22},{7,23},{8,24},{9,... | collective-permute-start | bytes 688136 | tf_op jit(solution)/shard_map/ppermute | solution.py:45
  12.4 38.0 %collective-permute-start.2 = (bf16[112,1024]{1,0:T(8,128)(2,1)S(1)}, bf16[112,1024]{1,0:T(8,128)(2,1)}, u32[]{:S(2)}, u32[]{:S(2)}) collective-permute-start(bf16[112,1024]{1,0:T(8,128)(2,1)S(1)} %pad_maximum_fusion.18), channel_id=1, source_target_pairs={{0,24},{1,25},{2,26},{3,27},{4,28},{5,29},{6,30},{7,31},{8,0},{9,1... | collective-permute-start | bytes 688136 | tf_op jit(solution)/shard_map/ppermute | solution.py:45
  50.2 35.7 %collective-permute-start.17 = (bf16[576,512]{1,0:T(8,128)(2,1)}, bf16[576,512]{1,0:T(8,128)(2,1)}, u32[]{:S(2)}, u32[]{:S(2)}) collective-permute-start(bf16[576,512]{1,0:T(8,128)(2,1)} %dynamic-slice_bitcast_fusion), channel_id=1, source_target_pairs={{0,1},{1,0},{2,3},{3,2},{4,5},{5,4},{6,7},{7,6},{8,9},{9,8},{10,11... | collective-permute-start | bytes 1769480 | tf_op jit(solution)/shard_map/ppermute | solution.py:45
  64.6 37.8 %collective-permute-start.15 = (bf16[32,4096]{1,0:T(8,128)(2,1)}, bf16[32,4096]{1,0:T(8,128)(2,1)}, u32[]{:S(2)}, u32[]{:S(2)}) collective-permute-start(bf16[32,4096]{1,0:T(8,128)(2,1)} %param.35), channel_id=1, source_target_pairs={{0,16},{1,17},{2,18},{3,19},{4,20},{5,21},{6,22},{7,23},{8,24},{9,... | collective-permute-start | bytes 786440 | tf_op jit(solution)/shard_map/ppermute | solution.py:45
  72.6 31.7 %collective-permute-start.12 = (bf16[4,112,512]{2,1,0:T(8,128)(2,1)S(1)}, bf16[4,112,512]{2,1,0:T(8,128)(2,1)S(1)}, u32[]{:S(2)}, u32[]{:S(2)}) collective-permute-start(bf16[4,112,512]{2,1,0:T(8,128)(2,1)S(1)} %pad_maximum_fusion.9.refs_0_), channel_id=1, source_target_pairs={{0,4},{1,5},{2,6},{3,7},{4,0},{5,1},{6,2},{7,3},{8,12},{9,13},{10,... | collective-permute-start | bytes 1376264 | tf_op jit(solution)/shard_map/ppermute | solution.py:45
  74.2 30.0 %collective-permute-start.13 = (bf16[4,112,512]{2,1,0:T(8,128)(2,1)S(1)}, bf16[4,112,512]{2,1,0:T(8,128)(2,1)}, u32[]{:S(2)}, u32[]{:S(2)}) collective-permute-start(bf16[4,112,512]{2,1,0:T(8,128)(2,1)S(1)} %pad_maximum_fusion.10.refs_3_), channel_id=1, source_target_pairs={{0,2},{1,3},{2,0},{3,1},{4,6},{5,7},{6,4},{7,5},{8,10},{9,11},{10,... | collective-permute-start | bytes 1376264 | tf_op jit(solution)/shard_map/ppermute | solution.py:45
  105.7 44.1 %collective-permute-start.22 = (bf16[8,112,512]{2,1,0:T(8,128)(2,1)S(1)}, bf16[8,112,512]{2,1,0:T(8,128)(2,1)}, u32[]{:S(2)}, u32[]{:S(2)}) collective-permute-start(bf16[8,112,512]{2,1,0:T(8,128)(2,1)S(1)} %pad_maximum_fusion.3), channel_id=1, source_target_pairs={{0,2},{1,3},{2,0},{3,1},{4,6},{5,7},{6,4},{7,5},{8,10},{9,11},{10,... | collective-permute-start | bytes 2752520 | tf_op jit(solution)/shard_map/ppermute | solution.py:45
  107.6 45.2 %collective-permute-start.24 = (bf16[8,112,512]{2,1,0:T(8,128)(2,1)S(1)}, bf16[8,112,512]{2,1,0:T(8,128)(2,1)}, u32[]{:S(2)}, u32[]{:S(2)}) collective-permute-start(bf16[8,112,512]{2,1,0:T(8,128)(2,1)S(1)} %pad_maximum_fusion.4), channel_id=1, source_target_pairs={{0,4},{1,5},{2,6},{3,7},{4,0},{5,1},{6,2},{7,3},{8,12},{9,13},{10,... | collective-permute-start | bytes 2752520 | tf_op jit(solution)/shard_map/ppermute | solution.py:45
  112.5 64.1 %collective-permute-start.29 = (bf16[576,1536]{1,0:T(8,128)(2,1)}, bf16[576,1536]{1,0:T(8,128)(2,1)}, u32[]{:S(2)}, u32[]{:S(2)}) collective-permute-start(bf16[576,1536]{1,0:T(8,128)(2,1)} %constant_dynamic-update-slice_fusion.l0), channel_id=1, source_target_pairs={{0,1},{1,0},{2,3},{3,2},{4,5},{5,4},{6,7},{7,6},{8,9},{9,8},{10,11... | collective-permute-start | bytes 5308424 | tf_op jit(solution)/shard_map/ppermute | solution.py:45
  112.7 35.8 %collective-permute-start.26 = (bf16[4,32,2048]{2,1,0:T(8,128)(2,1)S(1)}, bf16[4,32,2048]{2,1,0:T(8,128)(2,1)S(1)}, u32[]{:S(2)}, u32[]{:S(2)}) collective-permute-start(bf16[4,32,2048]{2,1,0:T(8,128)(2,1)S(1)} %pad_maximum_fusion.5.refs_0_), channel_id=1, source_target_pairs={{0,4},{1,5},{2,6},{3,7},{4,0},{5,1},{6,2},{7,3},{8,12},{9,13},{10,... | collective-permute-start | bytes 1572872 | tf_op jit(solution)/shard_map/ppermute | solution.py:45
  115.0 61.7 %collective-permute-start.28 = (bf16[576,1024]{1,0:T(8,128)(2,1)}, bf16[576,1024]{1,0:T(8,128)(2,1)}, u32[]{:S(2)}, u32[]{:S(2)}) collective-permute-start(bf16[576,1024]{1,0:T(8,128)(2,1)} %fusion.9.l0), channel_id=1, source_target_pairs={{0,1},{1,0},{2,3},{3,2},{4,5},{5,4},{6,7},{7,6},{8,9},{9,8},{10,11... | collective-permute-start | bytes 3538952 | tf_op jit(solution)/shard_map/ppermute | solution.py:45
  242.1 46.1 %collective-permute-start.51 = (bf16[576,1024]{1,0:T(8,128)(2,1)S(1)}, bf16[576,1024]{1,0:T(8,128)(2,1)S(1)}, u32[]{:S(2)}, u32[]{:S(2)}) collective-permute-start(bf16[576,1024]{1,0:T(8,128)(2,1)S(1)} %add_convert_fusion.3.n_ref.l0), channel_id=1, source_target_pairs={{0,1},{1,0},{2,3},{3,2},{4,5},{5,4},{6,7},{7,6},{8,9},{9,8},{10,11... | collective-permute-start | bytes 3538952 | tf_op jit(solution)/shard_map/ppermute | solution.py:45
  251.0 37.2 %collective-permute-start.47 = (f32[1,1024]{1,0:T(1,128)S(1)}, f32[1,1024]{1,0:T(1,128)S(1)}, u32[]{:S(2)}, u32[]{:S(2)}) collective-permute-start(f32[1,1024]{1,0:T(1,128)S(1)} %get-tuple-element.375.refs_0_), channel_id=1, source_target_pairs={{0,2},{1,3},{2,4},{3,5},{4,6},{5,7},{6,8},{7,9},{8,10},{9,11},{10,... | collective-permute-start | bytes 12296 | tf_op jit(solution)/shard_map/ppermute | solution.py:300
  253.0 35.1 %collective-permute-start.48 = (f32[1,1024]{1,0:T(1,128)S(1)}, f32[1,1024]{1,0:T(1,128)S(1)}, u32[]{:S(2)}, u32[]{:S(2)}) collective-permute-start(f32[1,1024]{1,0:T(1,128)S(1)} %get-tuple-element.375.refs_0_), channel_id=1, source_target_pairs={{2,0},{3,1},{4,2},{5,3},{6,4},{7,5},{8,6},{9,7},{10,8},{11,9},{12,... | collective-permute-start | bytes 12296 | tf_op jit(solution)/shard_map/ppermute | solution.py:300
  338.0 30.3 %collective-permute-start.59 = (bf16[4,2,256,256]{3,2,0,1:T(8,128)(2,1)}, bf16[4,2,256,256]{3,2,0,1:T(8,128)(2,1)}, u32[]{:S(2)}, u32[]{:S(2)}) collective-permute-start(bf16[4,2,256,256]{3,2,0,1:T(8,128)(2,1)} %copy.141), channel_id=1, source_target_pairs={{0,2},{1,3},{2,0},{3,1},{4,6},{5,7},{6,4},{7,5},{8,10},{9,11},{10,... | collective-permute-start | bytes 3145736 | tf_op jit(solution)/shard_map/ppermute | solution.py:45
  339.7 28.6 %collective-permute-start.60 = (bf16[4,2,256,256]{3,2,1,0:T(8,128)(2,1)}, bf16[4,2,256,256]{3,2,1,0:T(8,128)(2,1)}, u32[]{:S(2)}, u32[]{:S(2)}) collective-permute-start(bf16[4,2,256,256]{3,2,1,0:T(8,128)(2,1)} %get-tuple-element.396), channel_id=1, source_target_pairs={{0,4},{1,5},{2,6},{3,7},{4,0},{5,1},{6,2},{7,3},{8,12},{9,13},{10,... | collective-permute-start | bytes 3145736 | tf_op jit(solution)/shard_map/ppermute | solution.py:45
  370.6 35.0 %collective-permute-start.62 = (bf16[4,256,256]{2,1,0:T(8,128)(2,1)}, bf16[4,256,256]{2,1,0:T(8,128)(2,1)}, u32[]{:S(2)}, u32[]{:S(2)}) collective-permute-start(bf16[4,256,256]{2,1,0:T(8,128)(2,1)} %fusion.14), channel_id=1, source_target_pairs={{0,4},{1,5},{2,6},{3,7},{4,0},{5,1},{6,2},{7,3},{8,12},{9,13},{10,... | collective-permute-start | bytes 1572872 | tf_op jit(solution)/shard_map/ppermute | solution.py:45
  372.9 32.7 %collective-permute-start.63 = (bf16[4,256,256]{2,1,0:T(8,128)(2,1)}, bf16[4,256,256]{2,1,0:T(8,128)(2,1)}, u32[]{:S(2)}, u32[]{:S(2)}) collective-permute-start(bf16[4,256,256]{2,1,0:T(8,128)(2,1)} %fusion.15), channel_id=1, source_target_pairs={{0,2},{1,3},{2,0},{3,1},{4,6},{5,7},{6,4},{7,5},{8,10},{9,11},{10,... | collective-permute-start | bytes 1572872 | tf_op jit(solution)/shard_map/ppermute | solution.py:45
  437.7 47.6 %collective-permute-start.73 = (bf16[4,2,64,1024]{3,2,0,1:T(8,128)(2,1)}, bf16[4,2,64,1024]{3,2,0,1:T(8,128)(2,1)}, u32[]{:S(2)}, u32[]{:S(2)}) collective-permute-start(bf16[4,2,64,1024]{3,2,0,1:T(8,128)(2,1)} %copy.150), channel_id=1, source_target_pairs={{0,2},{1,3},{2,0},{3,1},{4,6},{5,7},{6,4},{7,5},{8,10},{9,11},{10,... | collective-permute-start | bytes 3145736 | tf_op jit(solution)/shard_map/ppermute | solution.py:45
  437.9 47.5 %collective-permute-start.74 = (bf16[4,2,64,1024]{3,2,1,0:T(8,128)(2,1)}, bf16[4,2,64,1024]{3,2,1,0:T(8,128)(2,1)}, u32[]{:S(2)}, u32[]{:S(2)}) collective-permute-start(bf16[4,2,64,1024]{3,2,1,0:T(8,128)(2,1)} %get-tuple-element.455), channel_id=1, source_target_pairs={{0,4},{1,5},{2,6},{3,7},{4,0},{5,1},{6,2},{7,3},{8,12},{9,13},{10,... | collective-permute-start | bytes 3145736 | tf_op jit(solution)/shard_map/ppermute | solution.py:45
  439.3 46.0 %collective-permute-start.75 = (bf16[4,2,64,256]{3,2,0,1:T(8,128)(2,1)}, bf16[4,2,64,256]{3,2,0,1:T(8,128)(2,1)}, u32[]{:S(2)}, u32[]{:S(2)}) collective-permute-start(bf16[4,2,64,256]{3,2,0,1:T(8,128)(2,1)} %copy.151), channel_id=1, source_target_pairs={{0,2},{1,3},{2,0},{3,1},{4,6},{5,7},{6,4},{7,5},{8,10},{9,11},{10,... | collective-permute-start | bytes 786440 | tf_op jit(solution)/shard_map/ppermute | solution.py:45
  440.7 44.7 %collective-permute-start.76 = (bf16[4,2,64,256]{3,2,1,0:T(8,128)(2,1)}, bf16[4,2,64,256]{3,2,1,0:T(8,128)(2,1)}, u32[]{:S(2)}, u32[]{:S(2)}) collective-permute-start(bf16[4,2,64,256]{3,2,1,0:T(8,128)(2,1)} %get-tuple-element.459), channel_id=1, source_target_pairs={{0,4},{1,5},{2,6},{3,7},{4,0},{5,1},{6,2},{7,3},{8,12},{9,13},{10,... | collective-permute-start | bytes 786440 | tf_op jit(solution)/shard_map/ppermute | solution.py:45
  443.7 31.4 %collective-permute-start.77 = (bf16[96,512]{1,0:T(8,128)(2,1)}, bf16[96,512]{1,0:T(8,128)(2,1)}, u32[]{:S(2)}, u32[]{:S(2)}) collective-permute-start(bf16[96,512]{1,0:T(8,128)(2,1)} %pad_maximum_fusion.24), channel_id=1, source_target_pairs={{0,8},{1,9},{2,10},{3,11},{4,12},{5,13},{6,14},{7,15},{8,16},{9,17... | collective-permute-start | bytes 294920 | tf_op jit(solution)/shard_map/ppermute | solution.py:45
  485.3 28.5 %collective-permute-start.90 = (f32[8,3200]{1,0:T(8,128)}, f32[8,3200]{1,0:T(8,128)S(1)}, u32[]{:S(2)}, u32[]{:S(2)}) collective-permute-start(f32[8,3200]{1,0:T(8,128)} %reshape.336), channel_id=1, source_target_pairs={{0,24},{1,25},{2,26},{3,27},{4,28},{5,29},{6,30},{7,31},{8,0},{9,1... | collective-permute-start | bytes 307208 | tf_op jit(solution)/shard_map/ppermute | solution.py:45
  491.9 38.3 %collective-permute-start.80 = (bf16[4,64,1024]{2,1,0:T(8,128)(2,1)S(1)}, bf16[4,64,1024]{2,1,0:T(8,128)(2,1)S(1)}, u32[]{:S(2)}, u32[]{:S(2)}) collective-permute-start(bf16[4,64,1024]{2,1,0:T(8,128)(2,1)S(1)} %fusion.16), channel_id=1, source_target_pairs={{0,4},{1,5},{2,6},{3,7},{4,0},{5,1},{6,2},{7,3},{8,12},{9,13},{10,... | collective-permute-start | bytes 1572872 | tf_op jit(solution)/shard_map/ppermute | solution.py:45
  494.1 36.1 %collective-permute-start.81 = (bf16[4,64,1024]{2,1,0:T(8,128)(2,1)S(1)}, bf16[4,64,1024]{2,1,0:T(8,128)(2,1)S(1)}, u32[]{:S(2)}, u32[]{:S(2)}) collective-permute-start(bf16[4,64,1024]{2,1,0:T(8,128)(2,1)S(1)} %fusion.17), channel_id=1, source_target_pairs={{0,2},{1,3},{2,0},{3,1},{4,6},{5,7},{6,4},{7,5},{8,10},{9,11},{10,... | collective-permute-start | bytes 1572872 | tf_op jit(solution)/shard_map/ppermute | solution.py:45
  536.4 31.6 %collective-permute-start.86 = (bf16[64,2048]{1,0:T(8,128)(2,1)}, bf16[64,2048]{1,0:T(8,128)(2,1)}, u32[]{:S(2)}, u32[]{:S(2)}) collective-permute-start(bf16[64,2048]{1,0:T(8,128)(2,1)} %pad_maximum_fusion.15), channel_id=1, source_target_pairs={{0,8},{1,9},{2,10},{3,11},{4,12},{5,13},{6,14},{7,15},{8,16},{9,17... | collective-permute-start | bytes 786440 | tf_op jit(solution)/shard_map/ppermute | solution.py:45
  537.2 30.9 %collective-permute-start.87 = (bf16[64,2048]{1,0:T(8,128)(2,1)}, bf16[64,2048]{1,0:T(8,128)(2,1)}, u32[]{:S(2)}, u32[]{:S(2)}) collective-permute-start(bf16[64,2048]{1,0:T(8,128)(2,1)} %pad_maximum_fusion.16), channel_id=1, source_target_pairs={{0,16},{1,17},{2,18},{3,19},{4,20},{5,21},{6,22},{7,23},{8,24},{9,... | collective-permute-start | bytes 786440 | tf_op jit(solution)/shard_map/ppermute | solution.py:45
  538.9 29.2 %collective-permute-start.88 = (bf16[64,2048]{1,0:T(8,128)(2,1)}, bf16[64,2048]{1,0:T(8,128)(2,1)}, u32[]{:S(2)}, u32[]{:S(2)}) collective-permute-start(bf16[64,2048]{1,0:T(8,128)(2,1)} %pad_maximum_fusion.17), channel_id=1, source_target_pairs={{0,24},{1,25},{2,26},{3,27},{4,28},{5,29},{6,30},{7,31},{8,0},{9,1... | collective-permute-start | bytes 786440 | tf_op jit(solution)/shard_map/ppermute | solution.py:45
  (204 other events, 2717.8 us)
Sparse Core Ops, SparseCore 0:
  10.9 87.7 all-gather.2
  101.6 90.1 all-gather.4

commit v3 on v2

v3 whole, which is shorter than its diff:
```python
import functools
import math

import jax
import numpy as np
import jax.numpy as jnp
from jax import lax
from jax.experimental import pallas as pl
from jax.experimental.pallas import tpu as pltpu
from jax.sharding import PartitionSpec as P

HEAD = 64
PS = 24
FS = 32
REACH = 3
LN1_GAIN, LN1_BIAS, BIAS_OUT, LN2_GAIN, LN2_BIAS, BIAS_FC2, BIAS_PROJ, BIAS_DEPTH, DEPTH = range(9)
LINES = DEPTH + 9

norm_eps = 1e-05
highest = lax.Precision.HIGHEST
f32, bf16 = jnp.float32, jnp.bfloat16
AXES = ("img", "ch")
FREE = pl.CostEstimate(flops=0, bytes_accessed=0, transcendentals=0)
NN = (((1,), (0,)), ((), ()))
NT = (((1,), (1,)), ((), ()))
TN = (((0,), (0,)), ((), ()))


class Grid:
    def __init__(self):
        img, ch = lax.axis_size("img"), lax.axis_size("ch")
        depth = 4 if img % 4 == 0 else 1
        self.n = {"z": depth, "x": img // depth, "y": ch // 2, "c": 2}
        self.stride = {"c": 1, "y": 2, "x": ch, "z": ch * (img // depth)}
        self.total = img * ch
        me = lax.axis_index(AXES)
        self.me = me
        self.pos = {a: lax.rem(lax.div(me, self.stride[a]), self.n[a]) for a in self.n}

    def send(self, v, axis, by):
        n, s = self.n[axis], self.stride[axis]
        pairs = []
        for i in range(self.total):
            a = (i // s) % n
            pairs.append((i, i + ((a + by) % n - a) * s))
        return lax.ppermute(v, AXES, pairs)

    def other(self, axis, by):
        return lax.rem(self.pos[axis] + by, self.n[axis])

    def swap(self, v, bit):
        return lax.ppermute(v, AXES, [(i, i ^ bit) for i in range(self.total)])


class GatherSmall:
    def __init__(self, grid, v):
        self.grid, self.v, self.bit = grid, v[None], 1

    def next(self):
        got = self.grid.swap(self.v, self.bit)
        pair = (self.v, got)
        upper = jnp.bitwise_and(self.grid.me, self.bit) != 0
        self.v = jnp.where(upper, jnp.concatenate(pair[::-1], 0), jnp.concatenate(pair, 0))
        self.bit *= 2
        return self.bit < self.grid.total


class ScatterSmall:
    def __init__(self, grid, v):
        self.grid, self.v = grid, v
        bits = [1 << i for i in range(grid.total.bit_length() - 1)]
        stride = grid.stride["z"]
        self.left = [b for b in bits if b >= stride][::-1] + [b for b in bits if b < stride][::-1]
        self.shape = {b: 2 for b in bits}

    def next(self):
        bit = self.left.pop(0)
        del self.shape[bit]
        low = 2 ** sum(b < bit for b in self.shape)
        t = self.v.reshape(-1, 2, low, self.v.shape[1])
        upper = (jnp.bitwise_and(self.grid.me, bit) != 0).astype(jnp.int32)
        mine = lax.dynamic_index_in_dim(t, upper, 1, keepdims=False)
        away = lax.dynamic_index_in_dim(t, 1 - upper, 1, keepdims=False)
        mine, away = (u.reshape(-1, t.shape[3]) for u in (mine, away))
        self.v = mine + self.grid.swap(away, bit)


def after(value, done):
    return lax.optimization_barrier((value, done))[0]


class Gather:
    def __init__(self, grid, params):
        self.grid = grid
        self.width = width = min(p.shape[1] for p in params)
        self.q = width // 2
        self.places, blocks, at = [], [], 0
        for i, p in enumerate(params):
            r = p.shape[0]
            held = -(-r // 16) * 16
            for j in range(p.shape[1] // width):
                block = p[:, j * width : (j + 1) * width]
                blocks.append(jnp.pad(block, ((0, held - r), (0, 0))) if held > r else block)
                self.places.append((i, at, r if r % 8 == 0 else held, j * width))
                at += held
        self.shapes = [p.shape for p in params]
        self.shard = jnp.concatenate(blocks, 0)

    def along_z(self):
        g = self.grid
        self.z = [self.shard] + [g.send(self.shard, "z", k) for k in range(1, g.n["z"])]

    def pack_first(self):
        self.s0 = [
            jnp.stack([p[:, i * self.q : (i + 1) * self.q] for p in self.z]) for i in range(2)
        ]
        del self.z

    def first(self):
        self.r1 = [self.every(self.s0[i], "xy"[i]) for i in range(2)]

    def pack_second(self):
        self.s1 = [jnp.concatenate([self.s0[i]] + self.r1[i], 0) for i in range(2)]
        del self.s0, self.r1

    def second(self):
        self.r2 = [self.every(self.s1[i], "yx"[i]) for i in range(2)]

    def early(self):
        self.c1 = [self.over(s) for s in self.s1]

    def cross(self):
        self.c2 = [[self.over(b) for b in r] for r in self.r2]

    def every(self, v, axis):
        return [self.grid.send(v, axis, k) for k in range(1, self.grid.n[axis])]

    def over(self, v):
        return self.grid.send(v, "c", 1)


    def state(self):
        names = ("shard", "z", "s0", "s1", "r1", "r2", "c1", "c2")
        return {k: v for k, v in vars(self).items() if k in names}

    def set_state(self, state):
        for k, v in state.items():
            setattr(self, k, v)

    def whole(self):
        n, q, place_of = self.grid.n, self.q, self.places
        nz, nx, ny = n["z"], n["x"], n["y"]
        arrays, plan = [], []
        for core_rel, (s1, r2) in enumerate(((self.s1, self.r2), (self.c1, self.c2))):
            for part, (first, second) in enumerate((("x", "y"), ("y", "x"))):
                for k2, buf in enumerate([s1[part]] + r2[part]):
                    for k1 in range(n[first]):
                        for kz in range(nz):
                            rel = {first: k1, second: k2}
                            plan.append((len(arrays), k1 * nz + kz, core_rel, part, kz, rel))
                    arrays.append(buf)
        count = len(self.shapes)
        tall = {param: r for param, _, r, _ in place_of}

        def body(place, *refs):
            ins, outs = refs[: len(arrays)], refs[len(arrays) : len(arrays) + count]
            held, (sems, out_sems) = refs[len(arrays) + count : -2], refs[-2:]
            z, x, y, c = place[0], place[1], place[2], place[3]
            waits = [[] for _ in range(nz)]
            for i, j, core_rel, part, kz, rel in plan:
                zz = lax.rem(z - kz + nz, nz)
                xx = lax.rem(x - rel["x"] + nx, nx)
                yy = lax.rem(y - rel["y"] + ny, ny)
                cc = lax.rem(c + core_rel, 2)
                for param, row, r, col in place_of:
                    copy = pltpu.make_async_copy(
                        ins[i].at[j, pl.ds(row, r)],
                        held[param].at[zz, xx, yy, cc, :, pl.ds(col + part * q, q)],
                        sems.at[kz],
                    )
                    copy.start()
                    waits[kz].append(copy)
            after = []
            for kz in range(nz):
                for copy in waits[kz]:
                    copy.wait()
                zz = lax.rem(z - kz + nz, nz)
                for param in range(count):
                    copy = pltpu.make_async_copy(
                        held[param].at[zz], outs[param].at[zz], out_sems.at[kz]
                    )
                    copy.start()
                    after.append(copy)
            for copy in after:
                copy.wait()

        place = jnp.stack([self.grid.pos[a] for a in ("z", "x", "y", "c")]).astype(jnp.int32)
        devices = nz * nx * ny * 2
        room = sum(devices * (r + 8) * w * 2 for r, w in self.shapes)
        shapes = [(nz, nx, ny, 2, tall[i], w) for i, (_, w) in enumerate(self.shapes)]
        whole = pl.pallas_call(
            body,
            out_shape=[jax.ShapeDtypeStruct(s, bf16) for s in shapes],
            in_specs=[pl.BlockSpec(memory_space=pltpu.SMEM)]
            + [pl.BlockSpec(memory_space=pltpu.HBM)] * len(arrays),
            out_specs=[pl.BlockSpec(memory_space=pltpu.HBM)] * count,
            scratch_shapes=[pltpu.VMEM(s, bf16) for s in shapes]
            + [pltpu.SemaphoreType.DMA((nz,)), pltpu.SemaphoreType.DMA((nz,))],
            compiler_params=pltpu.CompilerParams(vmem_limit_bytes=room + (4 << 20)),
            cost_estimate=FREE,
            name="assemble",
        )(place, *arrays)
        return [
            w[:, :, :, :, :r].reshape(devices * r, width) for w, (r, width) in zip(whole, self.shapes)
        ]


def tail_of(r, q, keep):
    extra = r - keep
    return extra, keep // extra, q * extra // keep


def place_share(ref, value, row, col):
    r, q, keep = value.shape[1] // 2, value.shape[2], ref.shape[2] // 2
    if row or r <= keep:
        ref[0, :, row : row + 2 * r, col : col + q] = value
        return
    extra, count, w = tail_of(r, q, keep)
    for c in range(2):
        ref[0, :, c * keep : (c + 1) * keep, col : col + q] = value[:, c * r : c * r + keep]
        for j in range(count):
            at = c * keep + j * extra
            ref[0, :, at : at + extra, col + q : col + q + w] = value[
                :, c * r + keep : (c + 1) * r, j * w : (j + 1) * w
            ]


def weight_grad_body(grid_n, terms, scratch, pos_ref, *refs):
    nx, ny = grid_n
    outs = refs[4 * len(terms) :]
    keep_a, keep_b = outs[0], outs[1]
    away_a, away_b = outs[2 : 1 + ny], outs[1 + ny :]
    for i, (r2, q, row, col) in enumerate(terms):
        l0, l1, r0, r1 = refs[4 * i : 4 * i + 4]
        o = dot(l0[...], r0[...], TN) + dot(l1[...], r1[...], TN)
        o = o.reshape(nx, ny, r2, 2 * q)

        def split_y(y, o=o, row=row, col=col, q=q):
            place_share(keep_a, o[:, y, :, :q].astype(bf16), row, col)
            for k in range(1, ny):
                place_share(away_a[k - 1], o[:, (y + k) % ny, :, :q].astype(bf16), row, col)

        def split_x(x, o=o, row=row, col=col, q=q):
            place_share(keep_b, o[x, :, :, q:].astype(bf16), row, col)
            for k in range(1, nx):
                place_share(away_b[k - 1], o[(x + k) % nx, :, :, q:].astype(bf16), row, col)

        for y in range(ny):
            pl.when(pos_ref[2] == y)(functools.partial(split_y, y))
        for x in range(nx):
            pl.when(pos_ref[1] == x)(functools.partial(split_x, x))


class Scatter:
    def __init__(self, grid, terms, height, width):
        self.grid = grid
        n = grid.n
        nz, nx, ny = n["z"], n["x"], n["y"]
        self.place = jnp.stack([grid.pos[a] for a in ("z", "x", "y", "c")]).astype(jnp.int32)
        self.height, self.width = height, width
        specs, arrays, shapes = [], [], []
        self.parts = []
        for left, left_far, right, right_far, at, at_far, left_at, rows, half, row, col in terms:
            t, band = left.shape[0], rows // nz
            r2, q = band // (nx * ny), half // 2
            lspec = pl.BlockSpec((t, band), lambda i, p, left_at=left_at: (0, left_at + i))
            specs += [lspec, lspec]
            specs += [pl.BlockSpec((t, half), lambda i, p, at=at: (0, at + p[3]))]
            if at_far is None:
                specs += [pl.BlockSpec((t, half), lambda i, p: (0, 0))]
            else:
                specs += [pl.BlockSpec((t, half), lambda i, p, at=at_far: (0, at + p[3]))]
            arrays += [left, left_far, right, right_far]
            shapes.append((r2, q, row, col))
            self.parts.append((r2 // 2, q, row, col))
        a = jax.ShapeDtypeStruct((nz, nx, height, width), bf16)
        b = jax.ShapeDtypeStruct((nz, ny, height, width), bf16)
        sa = pl.BlockSpec((1, nx, height, width), lambda i, p: (i, 0, 0, 0))
        sb = pl.BlockSpec((1, ny, height, width), lambda i, p: (i, 0, 0, 0))
        sums = pl.pallas_call(
            functools.partial(weight_grad_body, (nx, ny), shapes, None),
            grid_spec=pltpu.PrefetchScalarGridSpec(
                num_scalar_prefetch=1,
                grid=(nz,),
                in_specs=specs,
                out_specs=[sa, sb] + [sa] * (ny - 1) + [sb] * (nx - 1),
            ),
            out_shape=[a, b] + [a] * (ny - 1) + [b] * (nx - 1),
            compiler_params=pltpu.CompilerParams(vmem_limit_bytes=56 << 20),
            cost_estimate=FREE,
            name="weight_grad",
        )(self.place, *arrays)
        self.keep = list(sums[:2])
        self.away = [list(sums[2 : 1 + ny]), list(sums[1 + ny :])]

    def state(self):
        names = ("keep", "away", "got", "more", "sent", "kept", "own", "back")
        return {k: v for k, v in vars(self).items() if k in names}

    def set_state(self, state):
        for k, v in state.items():
            setattr(self, k, v)

    def first(self):
        self.got = [
            [self.grid.send(v, "yx"[i], k) for k, v in enumerate(self.away[i], 1)] for i in range(2)
        ]
        del self.away

    def fold_second(self):
        g, n = self.grid, self.grid.n
        nz, counts = n["z"], (n["x"], n["y"])
        block = (nz, 1, self.height, self.width)
        specs, arrays, plan = [], [], []
        for i in range(2):
            for k in range(1, counts[i]):

                def place(_, p, i=i, k=k):
                    return (0, lax.rem(p[1 + i] + k, counts[i]), 0, 0)

                terms = [self.keep[i]] + self.got[i]
                plan.append(len(terms))
                arrays += terms
                specs += [pl.BlockSpec(block, place)] * len(terms)

        def body(pos, *refs):
            at = 0
            for j, count in enumerate(plan):
                total = refs[at][:, 0].astype(f32)
                for ref in refs[at + 1 : at + count]:
                    total = total + ref[:, 0].astype(f32)
                refs[len(arrays) + j][...] = total.astype(bf16)
                at += count

        shape = jax.ShapeDtypeStruct((nz, self.height, self.width), bf16)
        sent = pl.pallas_call(
            body,
            grid_spec=pltpu.PrefetchScalarGridSpec(
                num_scalar_prefetch=1,
                grid=(1,),
                in_specs=specs,
                out_specs=[pl.BlockSpec(shape.shape, lambda i, p: (0, 0, 0))] * len(plan),
            ),
            out_shape=[shape] * len(plan),
            compiler_params=pltpu.CompilerParams(vmem_limit_bytes=56 << 20),
            cost_estimate=FREE,
            name="fold_second",
        )(self.place, *arrays)
        self.sent = list(sent)

    def second(self):
        g, sent = self.grid, self.sent
        counts = (g.n["x"], g.n["y"])
        at = counts[0] - 1
        del self.sent
        self.more = [
            [g.send(sent[k - 1], "x", k) for k in range(1, counts[0])],
            [g.send(sent[at + k - 1], "y", k) for k in range(1, counts[1])],
        ]

    def fold_z(self):
        g, n = self.grid, self.grid.n
        nz, counts = n["z"], (n["x"], n["y"])
        h, w = self.height, self.width
        specs, arrays, plan = [], [], []
        for i in range(2):
            terms = [self.keep[i]] + self.got[i]
            specs += [
                pl.BlockSpec(
                    (1, 1, h, w), lambda s, p, i=i: (lax.rem(p[0] + s, nz), p[1 + i], 0, 0)
                )
            ] * len(terms)
            specs += [
                pl.BlockSpec((1, h, w), lambda s, p: (lax.rem(p[0] + s, nz), 0, 0))
            ] * len(self.more[i])
            arrays += terms + self.more[i]
            plan.append((len(terms), len(self.more[i])))

        def body(pos, *refs):
            at = 0
            for i, (wide, narrow) in enumerate(plan):
                total = refs[at][0, 0].astype(f32)
                for ref in refs[at + 1 : at + wide]:
                    total = total + ref[0, 0].astype(f32)
                for ref in refs[at + wide : at + wide + narrow]:
                    total = total + ref[0].astype(f32)
                at += wide + narrow
                for k in range(nz):

                    def put(k=k, i=i, total=total):
                        out = refs[len(arrays) + k]
                        out[:, i * w : (i + 1) * w] = total.astype(out.dtype)

                    pl.when(pl.program_id(0) == k)(put)

        sent = pl.pallas_call(
            body,
            grid_spec=pltpu.PrefetchScalarGridSpec(
                num_scalar_prefetch=1,
                grid=(nz,),
                in_specs=specs,
                out_specs=[pl.BlockSpec((h, 2 * w), lambda s, p: (0, 0))] * nz,
            ),
            out_shape=[jax.ShapeDtypeStruct((h, 2 * w), bf16 if k else f32) for k in range(nz)],
            compiler_params=pltpu.CompilerParams(vmem_limit_bytes=56 << 20),
            cost_estimate=FREE,
            name="fold_z",
        )(self.place, *arrays)
        self.sent = list(sent)
        del self.keep, self.got, self.more

    def along_z(self):
        sent = self.sent
        self.kept = [sent[0]] + [self.grid.send(v, "z", k) for k, v in enumerate(sent[1:], 1)]
        del self.sent

    def last(self):
        w = self.width
        shape = jax.ShapeDtypeStruct((self.height // 2, 2 * w), f32)
        rows = sorted({(row, min(r, self.height // 2)) for r, _, row, _ in self.parts})

        def body(pos, *refs):
            own, away = refs[-2], refs[-1]
            total = refs[0][...]
            for ref in refs[1:-2]:
                total = total + ref[...].astype(f32)

            def put(c):
                for row, r in rows:
                    to = slice(row // 2, row // 2 + r)
                    own[to] = total[row + c * r : row + c * r + r]
                    away[to] = total[row + (1 - c) * r : row + (1 - c) * r + r]

            for c in range(2):
                pl.when(pos[3] == c)(functools.partial(put, c))

        self.own, away = pl.pallas_call(
            body,
            in_specs=[pl.BlockSpec(memory_space=pltpu.SMEM)]
            + [pl.BlockSpec(memory_space=pltpu.VMEM)] * len(self.kept),
            out_specs=[pl.BlockSpec(memory_space=pltpu.VMEM)] * 2,
            out_shape=[shape, shape],
            compiler_params=pltpu.CompilerParams(vmem_limit_bytes=56 << 20),
            cost_estimate=FREE,
            name="fold_last",
        )(self.place, *self.kept)
        self.back = self.grid.send(away, "c", 1)
        del self.kept

    def results(self):
        w = self.width

        def body(pos, own, back, *outs):
            def put(c):
                for out, (r, q, row, col) in zip(outs, self.parts):
                    keep = r if row else min(r, self.height // 2)
                    rs = slice(row // 2, row // 2 + keep)
                    for half, ref in ((c, own), (1 - c, back)):
                        for part in range(2):
                            at, from_col = 2 * half * q + part * q, part * w + col
                            out[:keep, at : at + q] = ref[rs, from_col : from_col + q]
                            if keep == r:
                                continue
                            extra, count, wide = tail_of(r, q, keep)
                            for j in range(count):
                                to = at + j * wide
                                out[keep:, to : to + wide] = ref[
                                    j * extra : (j + 1) * extra, from_col + q : from_col + q + wide
                                ]

            for c in range(2):
                pl.when(pos[3] == c)(functools.partial(put, c))

        return pl.pallas_call(
            body,
            in_specs=[pl.BlockSpec(memory_space=pltpu.SMEM)]
            + [pl.BlockSpec(memory_space=pltpu.VMEM)] * 2,
            out_specs=[pl.BlockSpec(memory_space=pltpu.VMEM)] * len(self.parts),
            out_shape=[jax.ShapeDtypeStruct((r, 4 * q), f32) for r, q, _, _ in self.parts],
            compiler_params=pltpu.CompilerParams(vmem_limit_bytes=56 << 20),
            cost_estimate=FREE,
            name="fold_out",
        )(self.place, self.own, self.back)


def neighbours(grid, v, reach):
    out = [v]
    for offset in range(1, reach + 1):
        for by in (offset, -offset):
            pairs = [(i, i + by) for i in range(grid.total) if 0 <= i + by < grid.total]
            out.append(lax.ppermute(v, AXES, pairs))
    return out


def layer_norm(inputs, scale_gain, offset_bias):
    centre = jnp.mean(inputs, axis=-1, keepdims=True)
    centred = inputs - centre
    spread = jnp.mean(centred * centred, axis=-1, keepdims=True)
    return centred * lax.rsqrt(spread + norm_eps) * scale_gain + offset_bias


def dot(a, b, dims=NN):
    return lax.dot_general(a, b, dims, preferred_element_type=f32)

def attend_body(q_ref, k_ref, v_ref, o_ref, lse_ref):
    t = q_ref.shape[0]
    first = lax.broadcasted_iota(jnp.int32, (t, 2 * HEAD), 1) < HEAD
    q, k, v = q_ref[...], k_ref[...], v_ref[...]
    out, totals = [], []
    for side in range(2):
        keep = first if side == 0 else jnp.logical_not(first)
        s = dot(q, jnp.where(keep, k, jnp.zeros_like(k)), NT)
        top = jnp.max(s, axis=-1, keepdims=True)
        p = jnp.exp((s - top) * HEAD ** -0.5)
        total = jnp.sum(p, axis=-1, keepdims=True)
        o = dot((p * (1.0 / total)).astype(bf16), jnp.where(keep, v, jnp.zeros_like(v)))
        out.append(o)
        totals.append(top * HEAD ** -0.5 + jnp.log(total))
    o_ref[...] = (out[0] + out[1]).astype(bf16)
    lse_ref[...] = jnp.where(first, totals[0], totals[1])

def attend(qkv):
    t, width = qkv.shape
    n = width // 3 // (2 * HEAD)
    spec = lambda off: pl.BlockSpec((t, 2 * HEAD), lambda i, off=off: (0, off * n + i))
    return pl.pallas_call(
        attend_body, grid=(n,),
        in_specs=[spec(0), spec(1), spec(2)],
        out_specs=[spec(0), spec(0)],
        out_shape=[jax.ShapeDtypeStruct((t, width // 3), bf16), jax.ShapeDtypeStruct((t, width // 3), f32)],
        compiler_params=pltpu.CompilerParams(vmem_limit_bytes=48 << 20),
        cost_estimate=FREE,
        name="attend",
    )(qkv, qkv, qkv)

def attend_back_body(q_ref, k_ref, v_ref, do_ref, lse_ref, dq_ref, dk_ref, dv_ref):
    t = q_ref.shape[0]
    first = lax.broadcasted_iota(jnp.int32, (t, 2 * HEAD), 1) < HEAD
    q, k, v, do = q_ref[...], k_ref[...], v_ref[...], do_ref[...]
    zero = jnp.zeros_like(k)
    dq = dk = dv = None
    for side in range(2):
        keep = first if side == 0 else jnp.logical_not(first)
        km, vm = jnp.where(keep, k, zero), jnp.where(keep, v, zero)
        qm, dom = jnp.where(keep, q, zero), jnp.where(keep, do, zero)
        lse = lse_ref[:, side * HEAD:side * HEAD + 1]
        p = jnp.exp(dot(q, km, NT) * HEAD ** -0.5 - lse)
        dp = dot(do, vm, NT)
        inner = jnp.sum(p * dp, axis=-1, keepdims=True)
        ds = (p * ((dp - inner) * HEAD ** -0.5)).astype(bf16)
        dq_ = dot(ds, km)
        dv_ = dot(dom, p.astype(bf16), TN)
        dk_ = dot(qm, ds, TN)
        dq = dq_ if dq is None else dq + dq_
        dv = dv_ if dv is None else dv + dv_
        dk = dk_ if dk is None else dk + dk_
    dq_ref[...] = dq.astype(bf16)
    dk_ref[...] = dk.T.astype(bf16)
    dv_ref[...] = dv.T.astype(bf16)

def attend_back(qkv, d_attended, lse):
    t, width = qkv.shape
    n = width // 3 // (2 * HEAD)
    spec = lambda off: pl.BlockSpec((t, 2 * HEAD), lambda i, off=off: (0, off * n + i))
    shape = jax.ShapeDtypeStruct((t, width // 3), bf16)
    return pl.pallas_call(
        attend_back_body, grid=(n,),
        in_specs=[spec(0), spec(1), spec(2), spec(0), spec(0)],
        out_specs=[spec(0)] * 3,
        out_shape=[shape] * 3,
        compiler_params=pltpu.CompilerParams(vmem_limit_bytes=48 << 20),
        cost_estimate=FREE,
        name="attend_back",
    )(qkv, qkv, qkv, d_attended, lse)

def gelu_parts(v):
    e = jnp.exp(-0.5 * v * v)
    t = 1.0 / (1.0 + (0.3275911 * 0.5 ** 0.5) * jnp.abs(v))
    poly = t * (0.127414796 + t * (-0.142248368 + t * (0.7107068705 + t * (-0.7265760135 + t * 0.5307027145))))
    tail = poly * e
    phi = jnp.where(v < 0, tail, 1.0 - tail)
    return v * phi, phi + v * (e * (2.0 * math.pi) ** -0.5)

def mlp_in_body(n_ref, w_ref, b_ref, act_ref, slope_ref):
    v = dot(n_ref[...], w_ref[...]) + b_ref[...]
    act, slope = gelu_parts(v)
    act_ref[...] = act.astype(bf16)
    slope_ref[...] = slope.astype(bf16)

def mlp_in(normed, w, bias, block=512):
    t, d = normed.shape
    ff = w.shape[1]
    out = pl.BlockSpec((t, block), lambda i: (0, i))
    shape = jax.ShapeDtypeStruct((t, ff), bf16)
    return pl.pallas_call(
        mlp_in_body, grid=(ff // block,),
        in_specs=[pl.BlockSpec((t, d), lambda i: (0, 0)), pl.BlockSpec((d, block), lambda i: (0, i)), pl.BlockSpec((1, block), lambda i: (0, i))],
        out_specs=[out, out], out_shape=[shape, shape],
        compiler_params=pltpu.CompilerParams(vmem_limit_bytes=48 << 20),
        cost_estimate=FREE,
        name="mlp_in",
    )(normed, w, bias.reshape(1, -1))

def mlp_back_body(dy_ref, slope_ref, w1_ref, w2_ref, dpre_ref, db_ref, dn_ref):
    g = dot(dy_ref[...], w2_ref[...], NT) * slope_ref[...].astype(f32)
    low = g.astype(bf16)
    dpre_ref[...] = low
    db_ref[...] = jnp.sum(low.astype(f32), axis=0, keepdims=True)
    dn = dot(low, w1_ref[...], NT)
    @pl.when(pl.program_id(0) == 0)
    def _(): dn_ref[...] = dn
    @pl.when(pl.program_id(0) > 0)
    def _(): dn_ref[...] += dn

def mlp_back(dy, slope, w1, w2, block=512):
    t, d = dy.shape
    ff = w1.shape[1]
    whole = pl.BlockSpec((t, d), lambda i: (0, 0))
    part = pl.BlockSpec((t, block), lambda i: (0, i))
    return pl.pallas_call(
        mlp_back_body, grid=(ff // block,),
        in_specs=[whole, part, pl.BlockSpec((d, block), lambda i: (0, i)), pl.BlockSpec((block, d), lambda i: (i, 0))],
        out_specs=[part, pl.BlockSpec((1, block), lambda i: (0, i)), whole],
        out_shape=[jax.ShapeDtypeStruct((t, ff), bf16), jax.ShapeDtypeStruct((1, ff), f32), jax.ShapeDtypeStruct((t, d), f32)],
        compiler_params=pltpu.CompilerParams(vmem_limit_bytes=48 << 20),
        cost_estimate=FREE,
        name="mlp_back",
    )(dy, slope, w1, w2)

def side_steps(x, side):
    n = x.shape[0]
    b = lax.rem(lax.broadcasted_iota(jnp.int32, x.shape, 0), side)
    before = jnp.where(b == 0, 0.0, pltpu.roll(x, 1, 0))
    after = jnp.where(b == side - 1, 0.0, pltpu.roll(x, n - 1, 0))
    return before, after

def up(x, by):
    return jnp.concatenate([jnp.zeros((by, x.shape[1]), x.dtype), x[:-by]], 0)

def down(x, by):
    return jnp.concatenate([x[by:], jnp.zeros((by, x.shape[1]), x.dtype)], 0)

def adapter_body(n_pieces, side, pos_ref, *refs):
    pieces, (w_ref, table_ref, dy_ref, proj_ref, spat_ref, rows_ref, dg_ref, dys_ref) = refs[:n_pieces], refs[n_pieces:]
    x = table_ref[BIAS_PROJ : BIAS_PROJ + 1]
    for k in range(n_pieces):
        x = x + dot(pieces[k][...], w_ref[lax.rem(pos_ref[0] - k + n_pieces, n_pieces)])
    proj_ref[...] = x
    before, after = side_steps(x, side)
    w = table_ref[DEPTH : DEPTH + 9]
    y = [before * w[3 * s:3 * s + 1] + x * w[3 * s + 1:3 * s + 2] + after * w[3 * s + 2:3 * s + 3] for s in range(3)]
    spatial = up(y[0], side) + y[1] + down(y[2], side) + table_ref[BIAS_DEPTH : BIAS_DEPTH + 1]
    spat_ref[...] = spatial
    rows_ref[...] = jnp.sum(spatial, axis=0, keepdims=True)
    dy = dy_ref[...].astype(f32)
    dg_ref[...] = jnp.sum(dy * spatial, axis=0, keepdims=True)
    dys_ref[...] = jnp.sum(dy, axis=0, keepdims=True)

def adapter(pos, pieces, w_proj, table, dy, side=PS, block=256):
    t, d = dy.shape
    n, width = len(pieces), pieces[0].shape[1]
    whole = pl.BlockSpec((t, width), lambda i: (0, 0))
    part = pl.BlockSpec((t, block), lambda i: (0, i))
    row = pl.BlockSpec((1, block), lambda i: (0, i))
    big, line = jax.ShapeDtypeStruct((t, d), f32), jax.ShapeDtypeStruct((1, d), f32)
    return pl.pallas_call(
        functools.partial(adapter_body, n, side), grid=(d // block,),
        in_specs=[pl.BlockSpec(memory_space=pltpu.SMEM)] + [whole] * n + [pl.BlockSpec((n, width, block), lambda i: (0, 0, i)), pl.BlockSpec((table.shape[0], block), lambda i: (0, i)), part],
        out_specs=[part, part, row, row, row], out_shape=[big, big, line, line, line],
        compiler_params=pltpu.CompilerParams(vmem_limit_bytes=48 << 20),
        cost_estimate=FREE,
        name="adapter",
    )(pos.reshape(1).astype(jnp.int32), *pieces, w_proj.reshape(n, width, d), table, dy)

def adapter_back_body(side, dy_ref, proj_ref, gate_ref, dr_ref, table_ref, dp_ref, dwd_ref, dbd_ref, dbp_ref):
    ds = dy_ref[...].astype(f32) * gate_ref[...] + dr_ref[...]
    dbd_ref[...] = jnp.sum(ds, axis=0, keepdims=True)
    before, after = side_steps(ds, side)
    w = table_ref[DEPTH : DEPTH + 9]
    y = [after * w[3 * s:3 * s + 1] + ds * w[3 * s + 1:3 * s + 2] + before * w[3 * s + 2:3 * s + 3] for s in range(3)]
    low = (down(y[0], side) + y[1] + up(y[2], side)).astype(bf16)
    dp_ref[...] = low
    dbp_ref[...] = jnp.sum(low.astype(f32), axis=0, keepdims=True)
    x = proj_ref[...]
    x_before, x_after = side_steps(x, side)
    for t, c in enumerate((x_before, x, x_after)):
        dwd_ref[t:t + 1] = jnp.sum(ds[side:] * c[:-side], axis=0, keepdims=True)
        dwd_ref[3 + t:4 + t] = jnp.sum(ds * c, axis=0, keepdims=True)
        dwd_ref[6 + t:7 + t] = jnp.sum(ds[:-side] * c[side:], axis=0, keepdims=True)

def adapter_back(dy, projected, gate, d_rows, table, side=PS, block=256):
    t, d = dy.shape
    part = pl.BlockSpec((t, block), lambda i: (0, i))
    row = pl.BlockSpec((1, block), lambda i: (0, i))
    nine = pl.BlockSpec((9, block), lambda i: (0, i))
    line = jax.ShapeDtypeStruct((1, d), f32)
    return pl.pallas_call(
        functools.partial(adapter_back_body, side), grid=(d // block,),
        in_specs=[part, part, row, row, pl.BlockSpec((table.shape[0], block), lambda i: (0, i))], out_specs=[part, nine, row, row],
        out_shape=[jax.ShapeDtypeStruct((t, d), bf16), jax.ShapeDtypeStruct((9, d), f32), line, line],
        compiler_params=pltpu.CompilerParams(vmem_limit_bytes=48 << 20),
        cost_estimate=FREE,
        name="adapter_back",
    )(dy, projected, gate, d_rows, table)


def rows_call(body, name, t, steps, ins, outs, sums):
    b = t // steps

    def spec(shape, by_rows):
        if by_rows:
            return pl.BlockSpec((b, shape[1]), lambda i: (i, 0))
        return pl.BlockSpec(shape, lambda i: (0, 0))

    out_specs = [pl.BlockSpec((b, w), lambda i: (i, 0)) for w, _ in outs]
    shapes = [jax.ShapeDtypeStruct((t, w), dt) for w, dt in outs]
    if sums:
        out_specs.append(pl.BlockSpec(sums, lambda i: (0, 0)))
        shapes.append(jax.ShapeDtypeStruct(sums, f32))
    return pl.pallas_call(
        body,
        grid=(steps,),
        in_specs=[spec(a.shape, by_rows) for a, by_rows in ins],
        out_specs=out_specs,
        out_shape=shapes,
        compiler_params=pltpu.CompilerParams(vmem_limit_bytes=48 << 20),
        cost_estimate=FREE,
        name=name,
    )(*[a for a, _ in ins])


def add_sums(ref, values):
    total = jnp.concatenate([jnp.sum(v, axis=0, keepdims=True) for v in values], 0)

    @pl.when(pl.program_id(0) == 0)
    def _():
        ref[...] = total

    @pl.when(pl.program_id(0) > 0)
    def _():
        ref[...] += total


def norm_parts(x):
    centred = x - jnp.mean(x, axis=-1, keepdims=True)
    rstd = lax.rsqrt(jnp.mean(centred * centred, axis=-1, keepdims=True) + norm_eps)
    return centred * rstd, rstd


def norm_back(d_normed, x, gain):
    xhat, rstd = norm_parts(x)
    u = d_normed * gain
    shift = jnp.mean(u, axis=-1, keepdims=True)
    slope = jnp.mean(u * xhat, axis=-1, keepdims=True)
    return (u - shift - xhat * slope) * rstd, d_normed * xhat


def attn_out_norm(attended, w, x, table):
    def body(a_ref, w_ref, x_ref, t_ref, first_ref, n_ref):
        first = x_ref[...].astype(f32) + dot(a_ref[...], w_ref[...]) + t_ref[BIAS_OUT : BIAS_OUT + 1]
        first_ref[...] = first
        xhat, _ = norm_parts(first)
        n_ref[...] = (
            xhat * t_ref[LN2_GAIN : LN2_GAIN + 1] + t_ref[LN2_BIAS : LN2_BIAS + 1]
        ).astype(bf16)

    t, d = x.shape
    ins = [(attended, True), (w, False), (x, True), (table, False)]
    return rows_call(body, "attn_out", t, 4, ins, [(d, f32), (d, bf16)], None)


def norm_two_back(d_normed2, first_sum, dy, table, w):
    def body(dn_ref, x_ref, dy_ref, t_ref, w_ref, first_ref, branch_ref, att_ref, sum_ref):
        dn = dn_ref[...]
        dx, scaled = norm_back(dn, x_ref[...], t_ref[LN2_GAIN : LN2_GAIN + 1])
        first = dy_ref[...].astype(f32) + dx
        low = first.astype(bf16)
        first_ref[...] = first
        branch_ref[...] = low
        att_ref[...] = dot(low, w_ref[...], NT).astype(bf16)
        add_sums(sum_ref, (scaled, dn, low.astype(f32)))

    t, d = dy.shape
    ins = [(d_normed2, True), (first_sum, True), (dy, True), (table, False), (w, False)]
    return rows_call(body, "norm_two", t, 4, ins, [(d, f32), (d, bf16), (d, bf16)], (3, d))


def norm_one_back(parts, w, x, d_first, table):
    def body(q_ref, k_ref, v_ref, w_ref, x_ref, first_ref, t_ref, out_ref, sum_ref):
        d = x_ref.shape[1]
        q, k, v = q_ref[...], k_ref[...], v_ref[...]
        dn = dot(q, w_ref[:, :d], NT) + dot(k, w_ref[:, d : 2 * d], NT) + dot(v, w_ref[:, 2 * d :], NT)
        dx, scaled = norm_back(dn, x_ref[...].astype(f32), t_ref[LN1_GAIN : LN1_GAIN + 1])
        out_ref[...] = (first_ref[...] + dx).astype(bf16)
        add_sums(sum_ref, (scaled, dn, q.astype(f32), v.astype(f32)))

    t, d = x.shape
    ins = [(p, True) for p in parts] + [(w, False), (x, True), (d_first, True), (table, False)]
    return rows_call(body, "norm_one", t, 4, ins, [(d, bf16)], (4, d))


def columns_call(body, name, block, ins, width, dtype):
    t = ins[0][0].shape[0]

    def spec(shape, by_columns):
        if by_columns:
            return pl.BlockSpec((shape[0], block), lambda i: (0, i))
        return pl.BlockSpec(shape, lambda i: (0, 0))

    return pl.pallas_call(
        body,
        grid=(width // block,),
        in_specs=[spec(a.shape, by) for a, by in ins],
        out_specs=pl.BlockSpec((t, block), lambda i: (0, i)),
        out_shape=jax.ShapeDtypeStruct((t, width), dtype),
        compiler_params=pltpu.CompilerParams(vmem_limit_bytes=48 << 20),
        cost_estimate=FREE,
        name=name,
    )(*[a for a, _ in ins])


def project(normed, w, bias):
    def body(n_ref, w_ref, b_ref, out_ref):
        out_ref[...] = (dot(n_ref[...], w_ref[...]) + b_ref[...]).astype(bf16)

    ins = [(normed, False), (w, True), (bias, True)]
    return columns_call(body, "project", 512, ins, w.shape[1], bf16)


def layer_output(activation, w, first_sum, table, gate, spatial):
    def body(a_ref, w_ref, x_ref, t_ref, g_ref, s_ref, out_ref):
        total = x_ref[...] + dot(a_ref[...], w_ref[...]) + t_ref[BIAS_FC2 : BIAS_FC2 + 1]
        out_ref[...] = (total + g_ref[...] * s_ref[...]).astype(bf16)

    ins = [(activation, False), (w, True), (first_sum, True), (table, True), (gate, True), (spatial, True)]
    return columns_call(body, "layer_output", 256, ins, w.shape[1], bf16)


def dot3(x, w, dims=NN):
    a = x.astype(bf16)
    rest = x - a.astype(f32)
    b = rest.astype(bf16)
    c = (rest - b.astype(f32)).astype(bf16)
    return dot(a, w, dims) + dot(b, w, dims) + dot(c, w, dims)


def gate_body(n_near, tokens, d, *refs):
    near, refs = refs[:n_near], refs[n_near:]
    win_ref, wout_ref, gate_ref, drows_ref, pack_ref, sum_ref = refs
    own = near[0][:, 2 * d :]
    match = [(near[i][:, 2 * d :] == own).astype(f32) for i in range(n_near)]
    count = functools.reduce(lambda a, b: a + b, match)[:, :1] * tokens
    rows = d_gates = None
    for i in range(n_near):
        weight = match[i][:, :1]
        row, d_gate = weight * near[i][:, :d], weight * near[i][:, d : 2 * d]
        rows = row if i == 0 else rows + row
        d_gates = d_gate if i == 0 else d_gates + d_gate
    second = lax.broadcasted_iota(jnp.int32, (8, d), 0) == 1
    mean = jnp.broadcast_to(rows / count, (8, d))
    d_gate = jnp.where(second, jnp.broadcast_to(d_gates, (8, d)), jnp.broadcast_to(near[0][:, d : 2 * d], (8, d)))
    win, wout = win_ref[...], wout_ref[...]
    act, slope = gelu_parts(dot3(mean, win))
    gate = jnp.tanh(dot3(act, wout, NT))
    d_pre = d_gate * (1.0 - gate * gate)
    d_hidden = dot3(d_pre, wout) * slope
    d_mean = dot3(d_hidden, win, NT)
    gate_ref[...] = gate[:1]
    drows_ref[...] = d_mean[1:2] / count
    sum_ref[...] = jnp.zeros((1, 128), f32) + jnp.sum(gate[:1])
    at = 0
    for v, order in ((mean, (0, 0, 1)), (d_pre, (0, 0, 1)), (d_hidden, (0, 1, 0)), (act, (0, 1, 0))):
        line = jnp.broadcast_to(v[:1], v.shape)
        high = line.astype(bf16)
        low = (line - high.astype(f32)).astype(bf16)
        place = lax.broadcasted_iota(jnp.int32, v.shape, 0)
        kind = jnp.where(place == 1, order[1], jnp.where(place == 2, order[2], 0))
        pick = jnp.where(kind == 1, low.astype(f32), high.astype(f32))
        pack_ref[:, at : at + v.shape[1]] = jnp.where(place < 3, pick, 0.0).astype(bf16)
        at += v.shape[1]


def gate_step(near, gates, d, hidden, tokens):
    n = len(near)

    def line(k):
        return jax.ShapeDtypeStruct((1, k), f32)

    def at(k):
        return pl.BlockSpec((1, k), lambda j: (0, 0))

    k = 2 * d + 2 * hidden
    return pl.pallas_call(
        functools.partial(gate_body, n, tokens, d),
        grid=(1,),
        in_specs=[at(2 * d + 128)] * n
        + [pl.BlockSpec((d, hidden), lambda j, b=b: (0, b)) for b in range(2)],
        out_specs=[at(d), at(d), pl.BlockSpec((8, k), lambda j: (0, 0)), at(128)],
        out_shape=[line(d), line(d), jax.ShapeDtypeStruct((8, k), bf16), line(128)],
        compiler_params=pltpu.CompilerParams(vmem_limit_bytes=32 << 20),
        cost_estimate=FREE,
        name="gate",
    )(*near, gates, gates)


def pool_table(coarse_side, fine_side):
    coarse, fine = np.arange(coarse_side)[:, None], np.arange(fine_side)[None]
    start = coarse * fine_side // coarse_side
    end = ((coarse + 1) * fine_side + coarse_side - 1) // coarse_side
    single = np.where((fine >= start) & (fine < end), 1.0, 0.0) / (end - start)
    return np.kron(single, single)


def token_sum(values):
    return jnp.sum(values.astype(f32), axis=0)


def shards(
    tokens,
    features,
    sample_of,
    cotangent,
    ln1_gain,
    ln1_bias,
    w_qkv,
    bias_qv,
    w_attn_out,
    bias_attn_out,
    ln2_gain,
    ln2_bias,
    w_fc1,
    bias_fc1,
    w_fc2,
    bias_fc2,
    w_proj,
    bias_proj,
    w_depth,
    bias_depth,
    w_gate_in,
    w_gate_out,
):
    grid = Grid()
    rows = ln1_gain.shape[0]
    total = grid.total
    x, dy = tokens[0], cotangent[0]
    count, d = x.shape
    hidden = w_gate_in.shape[1]

    vectors = [ln1_gain, ln1_bias, bias_attn_out, ln2_gain, ln2_bias, bias_fc2, bias_proj, bias_depth]
    a_small = GatherSmall(
        grid, jnp.concatenate(vectors + [w_depth.reshape(-1), bias_qv, bias_fc1])
    )
    gate_out_rows = dot(jnp.eye(rows, dtype=bf16), w_gate_out, NT).astype(bf16)
    gates = jnp.concatenate([w_gate_in, gate_out_rows], 1)
    full_qkv = lax.all_gather(w_qkv, AXES, axis=0, tiled=True)
    a_two = Gather(grid, (w_attn_out, w_fc1))
    a_three = Gather(grid, (gates, w_proj))

    n_ch = lax.axis_size("ch")
    ch = lax.axis_index("ch")
    n_img, own_ch = features.shape[0], features.shape[1]
    core = grid.pos["c"]

    def along_ch(v, by):
        img = lax.axis_size("img")
        pairs = [
            (i * n_ch + j, i * n_ch + (j + by) % n_ch) for i in range(img) for j in range(n_ch)
        ]
        return lax.ppermute(v, AXES, pairs)

    def peer(v):
        return grid.send(v, "c", 1)

    def peer_half(v):
        h = v.shape[1] // 2
        return grid.send(lax.dynamic_slice(v, (0, (1 - core) * h), (v.shape[0], h)), "c", 1)

    def step(active, *values):
        states, values = lax.optimization_barrier(([a.state() for a in active], values))
        for a, state in zip(active, states):
            a.set_state(state)
        return values

    a_two.along_z()
    for _ in range(3):
        a_small.next()
    pool = jnp.asarray(pool_table(PS, FS), bf16)
    pooled_own = dot(pool, features.reshape(n_img * own_ch, -1), NT).astype(bf16)
    a_two.pack_first()
    a_small.v, pooled_own = step((a_two,), a_small.v, pooled_own)

    a_two.first()
    a_two.pack_second()
    while a_small.next():
        pass
    every, pooled_own, w_fc2 = step((a_two, a_three), a_small.v, pooled_own, w_fc2)

    full_fc2 = lax.all_gather(w_fc2, AXES, axis=0, tiled=True)
    a_two.second()
    a_two.early()
    every = every.astype(f32)
    table = every[:, : LINES * rows].reshape(total, LINES, rows)
    table = table.transpose(1, 0, 2).reshape(LINES, d)
    at = LINES * rows
    full_bias_qv = every[:, at : at + 2 * rows].reshape(-1)
    full_bias_fc1 = every[:, at + 2 * rows :].reshape(1, -1)
    bias_qkv = jnp.concatenate([full_bias_qv[:d], jnp.zeros((d,), f32), full_bias_qv[d:]])[None]
    x32 = x.astype(f32)
    normed1 = layer_norm(x32, table[LN1_GAIN], table[LN1_BIAS]).astype(bf16)
    qkv = project(normed1, full_qkv, bias_qkv)
    attended, log_total = attend(qkv)
    attended, log_total, table, full_bias_fc1, pooled_own = step(
        (a_two, a_three), attended, log_total, table, full_bias_fc1, pooled_own
    )

    a_two.cross()
    dy_far = peer_half(dy)
    attended, pooled_own, dy_far = step((a_two, a_three), attended, pooled_own, dy_far)

    a_three.along_z()
    a_three.pack_first()

    def pooled_piece(k):
        to = lax.rem(ch + k, n_ch)
        piece = lax.dynamic_slice(pooled_own, (0, to * own_ch), (count, own_ch))
        return along_ch(piece, k) if k else piece

    early = n_ch // 2 + 1
    pieces = [pooled_piece(k) for k in range(early)]
    full_attn_out, full_fc1 = a_two.whole()
    first_sum, normed2 = attn_out_norm(attended, full_attn_out, x, table)
    activation, slope = mlp_in(normed2, full_fc1, full_bias_fc1)
    activation, slope, normed2, full_attn_out, full_fc1, first_sum, pieces, pooled_own = step(
        (a_three,),
        activation,
        slope,
        normed2,
        full_attn_out,
        full_fc1,
        first_sum,
        pieces,
        pooled_own,
    )

    a_three.first()
    a_three.pack_second()
    activation_far, normed2_far = peer(activation), peer(normed2)
    pieces = pieces + [pooled_piece(k) for k in range(early, n_ch)]
    activation_far, normed2_far, slope, attended, pieces = step(
        (a_three,), activation_far, normed2_far, slope, attended, pieces
    )

    a_three.second()
    ff = activation.shape[1]
    s_one = Scatter(
        grid,
        [(activation, activation_far, dy, dy_far, 0, None, 0, ff, d // 2, 0, 0)],
        2 * ff // total,
        d // 4,
    )
    slope, attended = step((a_three, s_one), slope, attended)

    s_one.first()
    d_pre, d_bias_fc1, d_normed2 = mlp_back(dy, slope, full_fc1, full_fc2)
    d_first, d_branch, d_attended, sums_two = norm_two_back(
        d_normed2, first_sum, dy, table, full_attn_out
    )
    s_one.got, d_attended = lax.optimization_barrier((s_one.got, d_attended))
    s_one.fold_second()
    d_attended, d_first, d_branch, d_pre, full_fc2, attended, pieces = step(
        (s_one, a_three), d_attended, d_first, d_branch, d_pre, full_fc2, attended, pieces
    )

    s_one.second()
    a_three.early()
    a_three.cross()
    d_pre_far, d_branch_far = peer_half(d_pre), peer_half(d_branch)
    attended_far = peer(attended)
    s_one.fold_z()
    d_attended, d_branch, d_pre, d_pre_far, d_branch_far, attended_far = step(
        (s_one, a_three), d_attended, d_branch, d_pre, d_pre_far, d_branch_far, attended_far
    )

    s_one.along_z()
    full_gates, full_proj = a_three.whole()
    s_two = Scatter(
        grid,
        [
            (normed2, normed2_far, d_pre, d_pre_far, 0, None, 0, d, ff // 2, 0, 0),
            (attended, attended_far, d_branch, d_branch_far, 0, None, 0, d, d // 2, 0, ff // 4),
        ],
        2 * rows,
        (ff + d) // 4,
    )
    d_attended, normed1, pieces, full_gates, full_proj = step(
        (s_two,), d_attended, normed1, pieces, full_gates, full_proj
    )

    s_two.first()
    projected, spatial, row_sums, d_gate, dy_sum = adapter(ch, pieces, full_proj, table, dy)
    d_query, d_key, d_value = attend_back(qkv, d_attended, log_total)
    s_two.got, d_query, row_sums = lax.optimization_barrier((s_two.got, d_query, row_sums))
    s_two.fold_second()
    d_query, d_key, d_value, normed1, row_sums, d_gate, dy_sum, pieces = step(
        (s_one, s_two), d_query, d_key, d_value, normed1, row_sums, d_gate, dy_sum, pieces
    )

    ids_plus = sample_of.astype(f32) + 1.0
    carried = jnp.concatenate(
        [row_sums, d_gate, jnp.broadcast_to(ids_plus[:, None], (1, 128))], 1
    )
    near = neighbours(grid, carried, REACH)
    pooled = jnp.zeros((count, n_ch * own_ch), bf16)
    for k in range(n_ch):
        from_ch = lax.rem(ch - k + n_ch, n_ch)
        pooled = lax.dynamic_update_slice(pooled, pieces[k], (0, from_ch * own_ch))
    d_mixed = jnp.concatenate([d_query, d_key, d_value], -1)
    d_mixed_far, normed1_far = peer_half(d_mixed), peer(normed1)
    d_mixed, d_mixed_far, normed1_far, near, pooled = step(
        (s_two,), d_mixed, d_mixed_far, normed1_far, near, pooled
    )

    pooled_far = peer(pooled)
    gate, d_rows, pack, gate_sum = gate_step(near, full_gates, d, hidden, count)
    d_projected, d_depth, d_bias_depth, d_bias_proj = adapter_back(
        dy, projected, gate, d_rows, table
    )
    d_pooled = dot(d_projected, full_proj, NT).astype(bf16)
    pack, d_projected, pooled_far, gate, d_mixed, d_pooled = step(
        (s_two,), pack, d_projected, pooled_far, gate, d_mixed, d_pooled
    )

    pack_far, d_projected_far = peer(pack), peer_half(d_projected)
    lines = jnp.concatenate([sums_two[2:], sums_two[:2], dy_sum, d_bias_proj, d_bias_depth, d_depth], 0)
    lines = lines.reshape(LINES - 2, total, rows).transpose(1, 0, 2).reshape(total, -1)
    small = jnp.concatenate(
        [lines, d_bias_fc1.reshape(total, -1), jnp.broadcast_to(gate_sum, (total, 128))], 1
    )
    s_two.second()
    back = []
    for k in range(n_ch):
        to = lax.rem(ch + k, n_ch)
        piece = lax.dynamic_slice(d_pooled, (0, to * own_ch), (count, own_ch))
        back.append(along_ch(piece, k) if k else piece)
    wide, low = 3 * d // 4, hidden // 4
    half = d // (hidden // 2)
    s_three = Scatter(
        grid,
        [
            (normed1, normed1_far, d_mixed, d_mixed_far, 0, None, 0, d, 3 * d // 2, 0, 0),
            (pack, pack_far, pack, pack_far, 2 * half, 2 * half, 0, d, hidden // 2, 0, wide),
            (
                pack,
                pack_far,
                pack,
                pack_far,
                2 * half + 2,
                2 * half + 2,
                grid.n["z"],
                d,
                hidden // 2,
                0,
                wide + low,
            ),
            (
                pooled,
                pooled_far,
                d_projected,
                d_projected_far,
                0,
                None,
                0,
                pooled.shape[1],
                d // 2,
                0,
                wide + 2 * low,
            ),
        ],
        2 * rows,
        wide + 2 * low + pooled.shape[1] // 4,
    )
    s_two.more, s_three.away = lax.optimization_barrier((s_two.more, s_three.away))
    s_two.fold_z()
    d_query, d_key, d_value, activation, back, small = step(
        (s_one, s_two, s_three), d_query, d_key, d_value, activation, back, small
    )

    s_three.first()
    s_two.along_z()
    grad_tokens, sums_one = norm_one_back(
        (d_query, d_key, d_value), full_qkv, x, d_first, table
    )
    layer_out = layer_output(activation, full_fc2, first_sum, table, gate, spatial)
    s_three.got, layer_out, grad_tokens = lax.optimization_barrier(
        (s_three.got, layer_out, grad_tokens)
    )
    s_three.fold_second()
    layer_out, grad_tokens, sums_one, small, back = step(
        (s_one, s_two, s_three), layer_out, grad_tokens, sums_one, small, back
    )

    s_three.second()
    ones = sums_one[:2].reshape(2, total, rows).transpose(1, 0, 2).reshape(total, -1)
    d_bias_qv = sums_one[2:].reshape(total, -1)
    s_small = ScatterSmall(grid, jnp.concatenate([ones, small, d_bias_qv], 1))
    s_one.last()
    s_two.last()
    s_small.next()
    s_small.next()
    s_three.fold_z()
    s_small.v, back = step((s_one, s_two, s_three), s_small.v, back)

    s_three.along_z()
    while s_small.left:
        s_small.next()
    (g_fc2,) = s_one.results()
    g_fc1, g_attn_out = s_two.results()
    s_small.v, back, g_fc2, g_fc1 = step((s_three,), s_small.v, back, g_fc2, g_fc1)

    d_local = jnp.zeros((n_img, count, own_ch), bf16)
    for k in range(n_ch):
        from_ch = lax.rem(ch - k + n_ch, n_ch)
        d_local = lax.dynamic_update_slice(d_local, back[k][None], (from_ch, 0, 0))
    grad_features = jnp.einsum("kpc,pf->kcf", d_local, pool, preferred_element_type=f32).astype(bf16)
    s_three.last()
    summed = s_small.v[0]
    gate_mean = summed[-2 * rows - 1] / (total * d)
    g_qkv, g_gate_in, g_gate_out, g_proj = s_three.results()

    def owned(i):
        return summed[i * rows : (i + 1) * rows]

    return (
        layer_out[None],
        grad_tokens[None],
        grad_features,
        owned(LN1_GAIN),
        owned(LN1_BIAS),
        g_qkv,
        summed[-2 * rows :],
        g_attn_out,
        owned(BIAS_OUT),
        owned(LN2_GAIN),
        owned(LN2_BIAS),
        g_fc1,
        summed[at : at + 4 * rows],
        g_fc2,
        owned(BIAS_FC2),
        g_proj,
        owned(BIAS_PROJ),
        summed[DEPTH * rows : at].reshape(9, rows),
        owned(BIAS_DEPTH),
        g_gate_in,
        g_gate_out.T,
        gate_mean,
    )


def solution(mesh):
    return jax.shard_map(
        shards,
        mesh=mesh,
        in_specs=(
            P(("img", "ch"), None, None),
            P("img", "ch", None),
            P(("img", "ch")),
            P(("img", "ch"), None, None),
            P(("img", "ch")),
            P(("img", "ch")),
            P(("img", "ch"), None),
            P(("img", "ch")),
            P(("img", "ch"), None),
            P(("img", "ch")),
            P(("img", "ch")),
            P(("img", "ch")),
            P(("img", "ch"), None),
            P(("img", "ch")),
            P(("img", "ch"), None),
            P(("img", "ch")),
            P(("img", "ch"), None),
            P(("img", "ch")),
            P(None, ("img", "ch")),
            P(("img", "ch")),
            P(("img", "ch"), None),
            P(None, ("img", "ch")),
        ),
        out_specs=(
            P(("img", "ch"), None, None),
            P(("img", "ch"), None, None),
            P("img", "ch", None),
            P(("img", "ch")),
            P(("img", "ch")),
            P(("img", "ch"), None),
            P(("img", "ch")),
            P(("img", "ch"), None),
            P(("img", "ch")),
            P(("img", "ch")),
            P(("img", "ch")),
            P(("img", "ch"), None),
            P(("img", "ch")),
            P(("img", "ch"), None),
            P(("img", "ch")),
            P(("img", "ch"), None),
            P(("img", "ch")),
            P(None, ("img", "ch")),
            P(("img", "ch")),
            P(("img", "ch"), None),
            P(None, ("img", "ch")),
            P(),
        ),
        check_vma=False,
    )
```

time: 656 us -> 551 us (0.84)
  Pallas kernels: 146 us -> 224 us
  starting transfers between devices: 147 us -> 81.3 us
  other arithmetic: 73.1 us -> 9 us
  matrix products: 41.5 us -> 10.7 us
  local copies, waits for them, and re-layouts: 76.8 us -> 61.6 us
  waiting for transfers between devices: 144 us -> 137 us
    pallas_call x9 -> x24, Pallas kernels: 64.5 us -> 142 us  [the longest x3 44.4 us: __init__(): pl.pallas_call(functools.partial(weight_grad_body, (nx, ny), shapes, None...]
    ppermute x94 -> x57, starting transfers between devices: 100 us -> 42.8 us  [send(): return lax.ppermute(v, AXES, pairs)]
    ppermute x94 -> x57, waiting for transfers between devices: 122 us -> 94.2 us  [send(): return lax.ppermute(v, AXES, pairs)]
    dot_general x8 -> x3, matrix products: 33.8 us -> 6.66 us  [dot(): return lax.dot_general(a, b, dims, preferred_element_type=f32)]
    all_gather x1, waiting for transfers between devices: 0.01 us -> 22.6 us  [shards(): full_qkv = lax.all_gather(w_qkv, AXES, axis=0, tiled=True)]
    ppermute x12 -> x6, starting transfers between devices: 40.2 us -> 19.7 us  [neighbours(): out.append(lax.ppermute(v, AXES, pairs))]
    convert_element_type x13 -> x0, other arithmetic: 18.9 us -> none  [the longest x10 13.1 us: second(): self.total(i, g.other(axis, k)).astype(bf16)]
    unnamed x259 -> x208, local copies, waits for them, and re-layouts: 12.7 us -> 30.3 us
  transfers between devices with their start and end apart: 114 -> 81, of which waited for: 30 -> 27; matrix products, arithmetic and copies ran while one was open for 24% -> 9% of each run, Pallas kernels for 23% -> 36%
where the time goes in v3:
time: 551 us; the launch traced here: 542 us
  Pallas kernels  224 us (41%)
  waiting for transfers between devices  137 us (25%)
  starting transfers between devices  81.3 us (15%)
  local copies, waits for them, and re-layouts  61.6 us (11%)
  between operations  18.1 us (3%)
  matrix products  10.7 us (2%)
  other arithmetic  9 us (2%)
    ppermute x57, waiting for transfers between devices, send(): return lax.ppermute(v, AXES, pairs)  94.2 us
    pallas_call x3, Pallas kernels, __init__(): pl.pallas_call(functools.partial(weight_grad_body, (nx, ny), shapes, None...  44.4 us
    ppermute x57, starting transfers between devices, send(): return lax.ppermute(v, AXES, pairs)  42.8 us
    unnamed x208, local copies, waits for them, and re-layouts  30.3 us
    pallas_call x1, Pallas kernels, attend_back(): pl.pallas_call(attend_back_body, grid=(n,), in_specs=[spec(0), spec(1), s...  25.4 us
    pallas_call x3, Pallas kernels, rows_call(): pl.pallas_call(body, grid=(steps,), in_specs=[spec(a.shape, by_rows) for...  24.6 us
    all_gather x1, waiting for transfers between devices, shards(): full_qkv = lax.all_gather(w_qkv, AXES, axis=0, tiled=True)  22.6 us
    ppermute x6, starting transfers between devices, neighbours(): out.append(lax.ppermute(v, AXES, pairs))  19.7 us
  transfers between devices with their start and end apart: 81, of which 27 were waited for; matrix products, arithmetic and copies ran while one was open for 9% of the time, Pallas kernels for 36%

profile of v3, /device:TPU:9, one launch (start us, length us, event | category | flops | bytes accessed | tf_op | source)
XLA Modules:
  0.0 541.9 jit_solution(17577369370044356492)
XLA Ops:
  8.9 6.8 %concatenate.80 = bf16[736]{0:T(1024)(128)(2,1)S(1)} concatenate(bf16[32]{0:T(256)(128)(2,1)} %param.27, bf16[32]{0:T(256)(128)(2,1)} %param.28, bf16[32]{0:T(256)(128)(2,1)} %param.32, bf16[32]{0:T(256)(128)(2,1)} %param.33, bf16[32]{0:T(256)(128)(2,1)} %param.34, bf16[32]{0:T(256)(128)(2,1)} %param.38, bf16[32]{0:T(256)(128)(2,1)} %param.40, bf16[32]{0:T(256)(128)(2,1)} %param.42, ...), dimensions={0} | concatenate | bytes 2944 | tf_op jit(solution)/shard_map/concatenate | solution.py:961
  25.7 4.5 convolution_convert_fusion.1
  34.6 19.4 %collective-permute-done.1 = bf16[160,1024]{1,0:T(8,128)(2,1)} collective-permute-done((bf16[160,1024]{1,0:T(8,128)(2,1)S(1)}, bf16[160,1024]{1,0:T(8,128)(2,1)}, u32[]{:S(2)}, u32[]{:S(2)}) %collective-permute-start.1) | collective-permute-done | bytes 327712 | tf_op jit(solution)/shard_map/ppermute | solution.py:46
  65.5 8.1 %collective-permute-done.7 = bf16[4,160,512]{2,1,0:T(8,128)(2,1)S(1)} collective-permute-done((bf16[4,160,512]{2,1,0:T(8,128)(2,1)S(1)}, bf16[4,160,512]{2,1,0:T(8,128)(2,1)S(1)}, u32[]{:S(2)}, u32[]{:S(2)}) %collective-permute-start.7) | collective-permute-done | bytes 655392 | tf_op jit(solution)/shard_map/ppermute | solution.py:46
  84.1 22.6 %all-gather.3.cloned.1.call-done.w_ref = bf16[1024,3072]{1,0:T(8,128)(2,1)} async-done(((bf16[32,3072]{1,0:T(8,128)(2,1)}), bf16[1024,3072]{1,0:T(8,128)(2,1)}) %all-gather.3.cloned.1.call-update) | async-done | bytes 6291472 | tf_op jit(solution)/shard_map/all_gather | solution.py:965
  106.7 7.1 %project.1.q_ref.k_ref.v_ref = bf16[576,3072]{1,0:T(8,128)(2,1)S(1)} custom-call(bf16[576,1024]{1,0:T(8,128)(2,1)S(1)} %fusion.5.n_ref.refs_0_, bf16[1024,3072]{1,0:T(8,128)(2,1)} %all-gather.3.cloned.1.call-done.w_ref, f32[1,3072]{1,0:T(1,128)S(1)} %bitcast.142), custom_call_target="tpu_custom_call" | custom-call | tf_op jit(solution)/shard_map/project/pallas_call | solution.py:820
  115.6 14.7 %attend.1 = (bf16[576,1024]{1,0:T(8,128)(2,1)S(1)}, f32[576,1024]{1,0:T(8,128)S(1)}) custom-call(bf16[576,3072]{1,0:T(8,128)(2,1)} %copy-done.2, bf16[576,3072]{1,0:T(8,128)(2,1)} %copy-done.2, bf16[576,3072]{1,0:T(8,128)(2,1)} %copy-done.2), custom_call_target="tpu_custom_call" | custom-call | tf_op jit(solution)/shard_map/attend/pallas_call | solution.py:536
  145.8 5.1 assemble.2
  158.0 16.4 %mlp_in.1 = (bf16[576,4096]{1,0:T(8,128)(2,1)}, bf16[576,4096]{1,0:T(8,128)(2,1)}) custom-call(bf16[576,1024]{1,0:T(8,128)(2,1)S(1)} %get-tuple-element.389.n_ref.refs_0_, bf16[1024,4096]{1,0:T(8,128)(2,1)} %bitcast.131, f32[1,4096]{1,0:T(1,128)S(1)} %bitcast.141), custom_call_target="tpu_custom_call" | custom-call | tf_op jit(solution)/shard_map/mlp_in/pallas_call | solution.py:605
  181.7 7.9 %collective-permute-done.23 = bf16[4,80,512]{2,1,0:T(8,128)(2,1)} collective-permute-done((bf16[4,80,512]{2,1,0:T(8,128)(2,1)}, bf16[4,80,512]{2,1,0:T(8,128)(2,1)}, u32[]{:S(2)}, u32[]{:S(2)}) %collective-permute-start.23) | collective-permute-done | bytes 327712 | tf_op jit(solution)/shard_map/ppermute | solution.py:46
  195.9 11.8 %weight_grad.3 = (bf16[4,2,256,256]{3,2,1,0:T(8,128)(2,1)}, bf16[4,2,256,256]{3,2,1,0:T(8,128)(2,1)}, bf16[4,2,256,256]{3,2,1,0:T(8,128)(2,1)}, bf16[4,2,256,256]{3,2,1,0:T(8,128)(2,1)}) custom-call(s32[4]{0:T(128)} %copy-done.61, bf16[576,4096]{1,0:T(8,128)(2,1)} %get-tuple-element.587.refs_0_.a_ref, bf16[576,4096]{1,0:T(8,128)(2,1)} %collective-permute-done.24.refs_1_, ...), custom_call_target="tpu_custom_call" | custom-call | tf_op jit(solution)/shard_map/weight_grad/pallas_call | solution.py:290
  213.4 17.1 %mlp_back.1 = (bf16[576,4096]{1,0:T(8,128)(2,1)}, f32[1,4096]{1,0:T(1,128)S(1)}, f32[576,1024]{1,0:T(8,128)S(1)}) custom-call(bf16[576,1024]{1,0:T(8,128)(2,1)S(1)} %bitcast.127, bf16[576,4096]{1,0:T(8,128)(2,1)} %get-tuple-element.407.slope_ref, bf16[1024,4096]{1,0:T(8,128)(2,1)} %bitcast.132, bf16[4096,1024]{1,0:T(8,128)(2,1)} %all-gather.5.cloned.1.call-done.w2_ref.w_ref), custom_call_target="tpu_custom_call" | custom-call | tf_op jit(solution)/shard_map/mlp_back/pallas_call | solution.py:630
  231.9 7.4 %norm_two.1 = (f32[576,1024]{1,0:T(8,128)}, bf16[576,1024]{1,0:T(8,128)(2,1)S(1)}, bf16[576,1024]{1,0:T(8,128)(2,1)S(1)}, f32[3,1024]{1,0:T(4,128)S(1)}) custom-call(f32[576,1024]{1,0:T(8,128)} %copy-done.44, f32[576,1024]{1,0:T(8,128)} %get-tuple-element.411.x_ref, bf16[576,1024]{1,0:T(8,128)(2,1)S(1)} %bitcast.128, f32[17,1024]{1,0:T(8,128)S(1)} %copy-done.16, ...), custom_call_target="tpu_custom_call" | custom-call | tf_op jit(solution)/shard_map/norm_two/pallas_call | solution.py:730
  249.7 11.8 %collective-permute-done.31.refs_2_ = bf16[4,256,256]{2,1,0:T(8,128)(2,1)S(1)} collective-permute-done((bf16[4,256,256]{2,1,0:T(8,128)(2,1)S(1)}, bf16[4,256,256]{2,1,0:T(8,128)(2,1)S(1)}, u32[]{:S(2)}, u32[]{:S(2)}) %collective-permute-start.31) | collective-permute-done | bytes 524320 | tf_op jit(solution)/shard_map/ppermute | solution.py:46
  265.0 4.7 fold_z.3
  269.8 15.4 %weight_grad.4 = (bf16[4,2,64,1280]{3,2,1,0:T(8,128)(2,1)}, bf16[4,2,64,1280]{3,2,1,0:T(8,128)(2,1)}, bf16[4,2,64,1280]{3,2,1,0:T(8,128)(2,1)}, bf16[4,2,64,1280]{3,2,1,0:T(8,128)(2,1)}) custom-call(s32[4]{0:T(128)} %copy-done.61, bf16[576,1024]{1,0:T(8,128)(2,1)} %copy-done.26, bf16[576,1024]{1,0:T(8,128)(2,1)} %collective-permute-done.25.refs_1_, ...), custom_call_target="tpu_custom_call" | custom-call | tf_op jit(solution)/shard_map/weight_grad/pallas_call | solution.py:290
  298.7 25.4 %attend_back.1 = (bf16[576,1024]{1,0:T(8,128)(2,1)S(1)}, bf16[576,1024]{1,0:T(8,128)(2,1)S(1)}, bf16[576,1024]{1,0:T(8,128)(2,1)S(1)}) custom-call(bf16[576,3072]{1,0:T(8,128)(2,1)} %copy-done.2, bf16[576,3072]{1,0:T(8,128)(2,1)} %copy-done.2, bf16[576,3072]{1,0:T(8,128)(2,1)} %copy-done.2, bf16[576,1024]{1,0:T(8,128)(2,1)S(1)} %copy-done.55, ...), custom_call_target="tpu_custom_call" | custom-call | tf_op jit(solution)/shard_map/attend_back/pallas_call | solution.py:576
  324.2 8.6 %adapter.1 = (f32[576,1024]{1,0:T(8,128)S(1)}, f32[576,1024]{1,0:T(8,128)}, f32[1,1024]{1,0:T(1,128)S(1)}, f32[1,1024]{1,0:T(1,128)S(1)}, f32[1,1024]{1,0:T(1,128)S(1)}) custom-call(s32[1]{0:T(128)} %bitcast.31.pos_ref, bf16[576,384]{1,0:T(8,128)(2,1)S(1)} %copy-done.30, bf16[576,384]{1,0:T(8,128)(2,1)S(1)} %copy-done.46, bf16[576,384]{1,0:T(8,128)(2,1)S(1)} %copy-done.49, ...), custom_call_target="tpu_custom_call" | custom-call | tf_op jit(solution)/shard_map/adapter/pallas_call | solution.py:676
  351.2 4.6 collective-permute-start.50
  355.8 3.7 collective-permute-start.51
  370.4 5.5 %adapter_back.1 = (bf16[576,1024]{1,0:T(8,128)(2,1)S(1)}, f32[9,1024]{1,0:T(8,128)S(1)}, f32[1,1024]{1,0:T(1,128)S(1)}, f32[1,1024]{1,0:T(1,128)S(1)}) custom-call(bf16[576,1024]{1,0:T(8,128)(2,1)S(1)} %bitcast.130, f32[576,1024]{1,0:T(8,128)S(1)} %copy-done.42, f32[1,1024]{1,0:T(1,128)S(1)} %get-tuple-element.589.gate_ref.g_ref, ...), custom_call_target="tpu_custom_call" | custom-call | tf_op jit(solution)/shard_map/adapter_back/pallas_call | solution.py:707
  386.4 17.2 %weight_grad.5 = (bf16[4,2,64,1408]{3,2,1,0:T(8,128)(2,1)}, bf16[4,2,64,1408]{3,2,1,0:T(8,128)(2,1)}, bf16[4,2,64,1408]{3,2,1,0:T(8,128)(2,1)}, bf16[4,2,64,1408]{3,2,1,0:T(8,128)(2,1)}) custom-call(s32[4]{0:T(128)} %copy-done.61, bf16[576,1024]{1,0:T(8,128)(2,1)} %copy-done.7, bf16[576,1024]{1,0:T(8,128)(2,1)} %collective-permute-done.46.refs_1_, ...), custom_call_target="tpu_custom_call" | custom-call | tf_op jit(solution)/shard_map/weight_grad/pallas_call | solution.py:290
  404.5 5.3 fold_z.4
  409.8 5.9 %collective-permute-done.59 = bf16[576,384]{1,0:T(8,128)(2,1)} collective-permute-done((bf16[576,384]{1,0:T(8,128)(2,1)}, bf16[576,384]{1,0:T(8,128)(2,1)}, u32[]{:S(2)}, u32[]{:S(2)}) %collective-permute-start.59) | collective-permute-done | bytes 442400 | tf_op jit(solution)/shard_map/ppermute | solution.py:979
  422.3 9.9 %layer_output.1 = bf16[576,1024]{1,0:T(8,128)(2,1)} custom-call(bf16[576,4096]{1,0:T(8,128)(2,1)} %get-tuple-element.587.refs_0_.a_ref, bf16[4096,1024]{1,0:T(8,128)(2,1)} %all-gather.5.cloned.1.call-done.w2_ref.w_ref, f32[576,1024]{1,0:T(8,128)S(1)} %copy-done.8, f32[17,1024]{1,0:T(8,128)S(1)} %copy-done.19, ...), custom_call_target="tpu_custom_call" | custom-call | tf_op jit(solution)/shard_map/layer_output/pallas_call | solution.py:820
  432.3 13.6 %norm_one.1 = (bf16[576,1024]{1,0:T(8,128)(2,1)}, f32[4,1024]{1,0:T(4,128)S(1)}) custom-call(bf16[576,1024]{1,0:T(8,128)(2,1)S(1)} %copy-done.21, bf16[576,1024]{1,0:T(8,128)(2,1)S(1)} %copy-done.23, bf16[576,1024]{1,0:T(8,128)(2,1)S(1)} %copy-done.25, bf16[1024,3072]{1,0:T(8,128)(2,1)} %all-gather.3.cloned.1.call-done.w_ref, ...), custom_call_target="tpu_custom_call" | custom-call | tf_op jit(solution)/shard_map/norm_one/pallas_call | solution.py:730
  449.8 3.9 fold_second.5
  465.3 6.1 %collective-permute-done.68.refs_2_ = bf16[4,64,1408]{2,1,0:T(8,128)(2,1)S(1)} collective-permute-done((bf16[4,64,1408]{2,1,0:T(8,128)(2,1)}, bf16[4,64,1408]{2,1,0:T(8,128)(2,1)S(1)}, u32[]{:S(2)}, u32[]{:S(2)}) %collective-permute-start.68) | collective-permute-done | bytes 720928 | tf_op jit(solution)/shard_map/ppermute | solution.py:46
  473.1 5.3 fold_z.5
  492.7 20.0 %collective-permute-done.73.refs_2_ = bf16[64,2816]{1,0:T(8,128)(2,1)S(1)} collective-permute-done((bf16[64,2816]{1,0:T(8,128)(2,1)}, bf16[64,2816]{1,0:T(8,128)(2,1)S(1)}, u32[]{:S(2)}, u32[]{:S(2)}) %collective-permute-start.73) | collective-permute-done | bytes 360480 | tf_op jit(solution)/shard_map/ppermute | solution.py:46
  512.7 5.5 %collective-permute-done.74.refs_3_ = bf16[64,2816]{1,0:T(8,128)(2,1)S(1)} collective-permute-done((bf16[64,2816]{1,0:T(8,128)(2,1)}, bf16[64,2816]{1,0:T(8,128)(2,1)S(1)}, u32[]{:S(2)}, u32[]{:S(2)}) %collective-permute-start.74) | collective-permute-done | bytes 360480 | tf_op jit(solution)/shard_map/ppermute | solution.py:46
  527.7 4.0 convolution_convert_fusion.2
  (471 shorter events, 198.3 us)
Async XLA Ops:
  7.2 99.5 %all-gather.3.cloned.1.call-start = ((), (), s32[]{:S(2)}) async-start(), calls=%async_computation | async-start | bytes 6488064 | tf_op jit(solution)/shard_map/all_gather | solution.py:965
  7.9 205.4 %all-gather.5.cloned.1.call-start = ((), (), s32[]{:S(2)}) async-start(), calls=%async_computation.1 | async-start | bytes 8650752 | tf_op jit(solution)/shard_map/all_gather | solution.py:1008
  21.9 32.1 %collective-permute-start.1 = (bf16[160,1024]{1,0:T(8,128)(2,1)S(1)}, bf16[160,1024]{1,0:T(8,128)(2,1)}, u32[]{:S(2)}, u32[]{:S(2)}) collective-permute-start(bf16[160,1024]{1,0:T(8,128)(2,1)S(1)} %slice_dynamic-update-slice_fusion), channel_id=1, source_target_pairs={{0,16},{1,17},{2,18},{3,19},{4,20},{5,21},{6,22},{7,23},{8,24},{9,... | collective-permute-start | bytes 983048 | tf_op jit(solution)/shard_map/ppermute | solution.py:46
  22.9 33.5 %collective-permute-start.2 = (bf16[160,1024]{1,0:T(8,128)(2,1)S(1)}, bf16[160,1024]{1,0:T(8,128)(2,1)}, u32[]{:S(2)}, u32[]{:S(2)}) collective-permute-start(bf16[160,1024]{1,0:T(8,128)(2,1)S(1)} %slice_dynamic-update-slice_fusion), channel_id=1, source_target_pairs={{0,24},{1,25},{2,26},{3,27},{4,28},{5,29},{6,30},{7,31},{8,0},{9,1... | collective-permute-start | bytes 983048 | tf_op jit(solution)/shard_map/ppermute | solution.py:46
  78.0 54.8 %collective-permute-start.10 = (bf16[8,160,512]{2,1,0:T(8,128)(2,1)}, bf16[8,160,512]{2,1,0:T(8,128)(2,1)}, u32[]{:S(2)}, u32[]{:S(2)}) collective-permute-start(bf16[8,160,512]{2,1,0:T(8,128)(2,1)} %pad_maximum_fusion.refs_0_), channel_id=1, source_target_pairs={{0,1},{1,0},{2,3},{3,2},{4,5},{5,4},{6,7},{7,6},{8,9},{9,8},{10,11... | collective-permute-start | bytes 3932168 | tf_op jit(solution)/shard_map/ppermute | solution.py:46
  78.8 54.0 %collective-permute-start.12 = (bf16[8,160,512]{2,1,0:T(8,128)(2,1)}, bf16[8,160,512]{2,1,0:T(8,128)(2,1)}, u32[]{:S(2)}, u32[]{:S(2)}) collective-permute-start(bf16[8,160,512]{2,1,0:T(8,128)(2,1)} %pad_maximum_fusion.refs_0_), channel_id=1, source_target_pairs={{0,2},{1,3},{2,0},{3,1},{4,6},{5,7},{6,4},{7,5},{8,10},{9,11},{10,... | collective-permute-start | bytes 3932168 | tf_op jit(solution)/shard_map/ppermute | solution.py:46
  80.0 52.8 %collective-permute-start.11 = (bf16[8,160,512]{2,1,0:T(8,128)(2,1)}, bf16[8,160,512]{2,1,0:T(8,128)(2,1)}, u32[]{:S(2)}, u32[]{:S(2)}) collective-permute-start(bf16[8,160,512]{2,1,0:T(8,128)(2,1)} %pad_maximum_fusion.1.refs_2_), channel_id=1, source_target_pairs={{0,1},{1,0},{2,3},{3,2},{4,5},{5,4},{6,7},{7,6},{8,9},{9,8},{10,11... | collective-permute-start | bytes 3932168 | tf_op jit(solution)/shard_map/ppermute | solution.py:46
  80.4 52.5 %collective-permute-start.13 = (bf16[8,160,512]{2,1,0:T(8,128)(2,1)}, bf16[8,160,512]{2,1,0:T(8,128)(2,1)}, u32[]{:S(2)}, u32[]{:S(2)}) collective-permute-start(bf16[8,160,512]{2,1,0:T(8,128)(2,1)} %pad_maximum_fusion.1.refs_2_), channel_id=1, source_target_pairs={{0,4},{1,5},{2,6},{3,7},{4,0},{5,1},{6,2},{7,3},{8,12},{9,13},{10,... | collective-permute-start | bytes 3932168 | tf_op jit(solution)/shard_map/ppermute | solution.py:46
  139.0 35.4 %collective-permute-start.17 = (bf16[80,1024]{1,0:T(8,128)(2,1)}, bf16[80,1024]{1,0:T(8,128)(2,1)S(1)}, u32[]{:S(2)}, u32[]{:S(2)}) collective-permute-start(bf16[80,1024]{1,0:T(8,128)(2,1)} %pad_maximum_fusion.8), channel_id=1, source_target_pairs={{0,8},{1,9},{2,10},{3,11},{4,12},{5,13},{6,14},{7,15},{8,16},{9,17... | collective-permute-start | bytes 491528 | tf_op jit(solution)/shard_map/ppermute | solution.py:46
  139.5 34.9 %collective-permute-start.18 = (bf16[80,1024]{1,0:T(8,128)(2,1)}, bf16[80,1024]{1,0:T(8,128)(2,1)S(1)}, u32[]{:S(2)}, u32[]{:S(2)}) collective-permute-start(bf16[80,1024]{1,0:T(8,128)(2,1)} %pad_maximum_fusion.8), channel_id=1, source_target_pairs={{0,16},{1,17},{2,18},{3,19},{4,20},{5,21},{6,22},{7,23},{8,24},{9,... | collective-permute-start | bytes 491528 | tf_op jit(solution)/shard_map/ppermute | solution.py:46
  141.1 33.4 %collective-permute-start.19 = (bf16[80,1024]{1,0:T(8,128)(2,1)}, bf16[80,1024]{1,0:T(8,128)(2,1)S(1)}, u32[]{:S(2)}, u32[]{:S(2)}) collective-permute-start(bf16[80,1024]{1,0:T(8,128)(2,1)} %pad_maximum_fusion.8), channel_id=1, source_target_pairs={{0,24},{1,25},{2,26},{3,27},{4,28},{5,29},{6,30},{7,31},{8,0},{9,1... | collective-permute-start | bytes 491528 | tf_op jit(solution)/shard_map/ppermute | solution.py:46
  143.3 32.8 %collective-permute-start.20 = (bf16[576,384]{1,0:T(8,128)(2,1)S(1)}, bf16[576,384]{1,0:T(8,128)(2,1)S(1)}, u32[]{:S(2)}, u32[]{:S(2)}) collective-permute-start(bf16[576,384]{1,0:T(8,128)(2,1)S(1)} %get-tuple-element.679), channel_id=1, source_target_pairs={{0,1},{1,2},{2,3},{3,0},{4,5},{5,6},{6,7},{7,4},{8,9},{9,10},{10,1... | collective-permute-start | bytes 1327112 | tf_op jit(solution)/shard_map/ppermute | solution.py:979
  144.9 31.9 %collective-permute-start.21 = (bf16[576,384]{1,0:T(8,128)(2,1)S(1)}, bf16[576,384]{1,0:T(8,128)(2,1)S(1)}, u32[]{:S(2)}, u32[]{:S(2)}) collective-permute-start(bf16[576,384]{1,0:T(8,128)(2,1)S(1)} %get-tuple-element.678), channel_id=1, source_target_pairs={{0,2},{1,3},{2,0},{3,1},{4,6},{5,7},{6,4},{7,5},{8,10},{9,11},{10,... | collective-permute-start | bytes 1327112 | tf_op jit(solution)/shard_map/ppermute | solution.py:979
  211.1 29.2 %collective-permute-start.29 = (bf16[4,2,256,256]{3,2,1,0:T(8,128)(2,1)}, bf16[4,2,256,256]{3,2,1,0:T(8,128)(2,1)}, u32[]{:S(2)}, u32[]{:S(2)}) collective-permute-start(bf16[4,2,256,256]{3,2,1,0:T(8,128)(2,1)} %get-tuple-element.405), channel_id=1, source_target_pairs={{0,2},{1,3},{2,0},{3,1},{4,6},{5,7},{6,4},{7,5},{8,10},{9,11},{10,... | collective-permute-start | bytes 3145736 | tf_op jit(solution)/shard_map/ppermute | solution.py:46
  212.0 28.3 %collective-permute-start.30 = (bf16[4,2,256,256]{3,2,1,0:T(8,128)(2,1)}, bf16[4,2,256,256]{3,2,1,0:T(8,128)(2,1)}, u32[]{:S(2)}, u32[]{:S(2)}) collective-permute-start(bf16[4,2,256,256]{3,2,1,0:T(8,128)(2,1)} %get-tuple-element.406), channel_id=1, source_target_pairs={{0,4},{1,5},{2,6},{3,7},{4,0},{5,1},{6,2},{7,3},{8,12},{9,13},{10,... | collective-permute-start | bytes 3145736 | tf_op jit(solution)/shard_map/ppermute | solution.py:46
  291.5 42.6 %collective-permute-start.43 = (bf16[4,2,64,1280]{3,2,1,0:T(8,128)(2,1)}, bf16[4,2,64,1280]{3,2,1,0:T(8,128)(2,1)}, u32[]{:S(2)}, u32[]{:S(2)}) collective-permute-start(bf16[4,2,64,1280]{3,2,1,0:T(8,128)(2,1)} %get-tuple-element.480), channel_id=1, source_target_pairs={{0,2},{1,3},{2,0},{3,1},{4,6},{5,7},{6,4},{7,5},{8,10},{9,11},{10,... | collective-permute-start | bytes 3932168 | tf_op jit(solution)/shard_map/ppermute | solution.py:46
  292.3 41.9 %collective-permute-start.44 = (bf16[4,2,64,1280]{3,2,1,0:T(8,128)(2,1)}, bf16[4,2,64,1280]{3,2,1,0:T(8,128)(2,1)}, u32[]{:S(2)}, u32[]{:S(2)}) collective-permute-start(bf16[4,2,64,1280]{3,2,1,0:T(8,128)(2,1)} %get-tuple-element.481), channel_id=1, source_target_pairs={{0,4},{1,5},{2,6},{3,7},{4,0},{5,1},{6,2},{7,3},{8,12},{9,13},{10,... | collective-permute-start | bytes 3932168 | tf_op jit(solution)/shard_map/ppermute | solution.py:46
  293.7 44.1 %collective-permute-start.40 = (bf16[256,512]{1,0:T(8,128)(2,1)}, bf16[256,512]{1,0:T(8,128)(2,1)}, u32[]{:S(2)}, u32[]{:S(2)}) collective-permute-start(bf16[256,512]{1,0:T(8,128)(2,1)} %get-tuple-element.452), channel_id=1, source_target_pairs={{0,8},{1,9},{2,10},{3,11},{4,12},{5,13},{6,14},{7,15},{8,16},{9,17... | collective-permute-start | bytes 786440 | tf_op jit(solution)/shard_map/ppermute | solution.py:46
  294.6 43.1 %collective-permute-start.41 = (bf16[256,512]{1,0:T(8,128)(2,1)}, bf16[256,512]{1,0:T(8,128)(2,1)}, u32[]{:S(2)}, u32[]{:S(2)}) collective-permute-start(bf16[256,512]{1,0:T(8,128)(2,1)} %get-tuple-element.453), channel_id=1, source_target_pairs={{0,16},{1,17},{2,18},{3,19},{4,20},{5,21},{6,22},{7,23},{8,24},{9,... | collective-permute-start | bytes 786440 | tf_op jit(solution)/shard_map/ppermute | solution.py:46
  296.6 41.2 %collective-permute-start.42 = (bf16[256,512]{1,0:T(8,128)(2,1)}, bf16[256,512]{1,0:T(8,128)(2,1)}, u32[]{:S(2)}, u32[]{:S(2)}) collective-permute-start(bf16[256,512]{1,0:T(8,128)(2,1)} %get-tuple-element.454), channel_id=1, source_target_pairs={{0,24},{1,25},{2,26},{3,27},{4,28},{5,29},{6,30},{7,31},{8,0},{9,1... | collective-permute-start | bytes 786440 | tf_op jit(solution)/shard_map/ppermute | solution.py:46
  340.4 24.3 %collective-permute-start.45 = (bf16[576,1536]{1,0:T(8,128)(2,1)}, bf16[576,1536]{1,0:T(8,128)(2,1)}, u32[]{:S(2)}, u32[]{:S(2)}) collective-permute-start(bf16[576,1536]{1,0:T(8,128)(2,1)} %constant_dynamic-slice_fusion.9), channel_id=1, source_target_pairs={{0,1},{1,0},{2,3},{3,2},{4,5},{5,4},{6,7},{7,6},{8,9},{9,8},{10,11... | collective-permute-start | bytes 5308424 | tf_op jit(solution)/shard_map/ppermute | solution.py:46
  378.2 25.5 %collective-permute-start.54 = (bf16[4,64,1280]{2,1,0:T(8,128)(2,1)}, bf16[4,64,1280]{2,1,0:T(8,128)(2,1)S(1)}, u32[]{:S(2)}, u32[]{:S(2)}) collective-permute-start(bf16[4,64,1280]{2,1,0:T(8,128)(2,1)} %get-tuple-element.547), channel_id=1, source_target_pairs={{0,4},{1,5},{2,6},{3,7},{4,0},{5,1},{6,2},{7,3},{8,12},{9,13},{10,... | collective-permute-start | bytes 1966088 | tf_op jit(solution)/shard_map/ppermute | solution.py:46
  382.3 27.5 %collective-permute-start.58 = (bf16[576,384]{1,0:T(8,128)(2,1)}, bf16[576,384]{1,0:T(8,128)(2,1)S(1)}, u32[]{:S(2)}, u32[]{:S(2)}) collective-permute-start(bf16[576,384]{1,0:T(8,128)(2,1)} %get-tuple-element.676), channel_id=1, source_target_pairs={{0,1},{1,2},{2,3},{3,0},{4,5},{5,6},{6,7},{7,4},{8,9},{9,10},{10,1... | collective-permute-start | bytes 1327112 | tf_op jit(solution)/shard_map/ppermute | solution.py:979
  383.9 31.8 %collective-permute-start.59 = (bf16[576,384]{1,0:T(8,128)(2,1)}, bf16[576,384]{1,0:T(8,128)(2,1)}, u32[]{:S(2)}, u32[]{:S(2)}) collective-permute-start(bf16[576,384]{1,0:T(8,128)(2,1)} %get-tuple-element.675), channel_id=1, source_target_pairs={{0,2},{1,3},{2,0},{3,1},{4,6},{5,7},{6,4},{7,5},{8,10},{9,11},{10,... | collective-permute-start | bytes 1327112 | tf_op jit(solution)/shard_map/ppermute | solution.py:979
  384.1 32.4 %collective-permute-start.60 = (bf16[576,384]{1,0:T(8,128)(2,1)}, bf16[576,384]{1,0:T(8,128)(2,1)}, u32[]{:S(2)}, u32[]{:S(2)}) collective-permute-start(bf16[576,384]{1,0:T(8,128)(2,1)} %get-tuple-element.674), channel_id=1, source_target_pairs={{0,3},{1,0},{2,1},{3,2},{4,7},{5,4},{6,5},{7,6},{8,11},{9,8},{10,9... | collective-permute-start | bytes 1327112 | tf_op jit(solution)/shard_map/ppermute | solution.py:979
  416.5 32.9 %collective-permute-start.64 = (bf16[4,2,64,1408]{3,2,1,0:T(8,128)(2,1)}, bf16[4,2,64,1408]{3,2,1,0:T(8,128)(2,1)}, u32[]{:S(2)}, u32[]{:S(2)}) collective-permute-start(bf16[4,2,64,1408]{3,2,1,0:T(8,128)(2,1)} %get-tuple-element.585), channel_id=1, source_target_pairs={{0,2},{1,3},{2,0},{3,1},{4,6},{5,7},{6,4},{7,5},{8,10},{9,11},{10,... | collective-permute-start | bytes 4325384 | tf_op jit(solution)/shard_map/ppermute | solution.py:46
  416.5 33.3 %collective-permute-start.65 = (bf16[4,2,64,1408]{3,2,1,0:T(8,128)(2,1)}, bf16[4,2,64,1408]{3,2,1,0:T(8,128)(2,1)}, u32[]{:S(2)}, u32[]{:S(2)}) collective-permute-start(bf16[4,2,64,1408]{3,2,1,0:T(8,128)(2,1)} %get-tuple-element.586), channel_id=1, source_target_pairs={{0,4},{1,5},{2,6},{3,7},{4,0},{5,1},{6,2},{7,3},{8,12},{9,13},{10,... | collective-permute-start | bytes 4325384 | tf_op jit(solution)/shard_map/ppermute | solution.py:46
  416.5 37.2 %collective-permute-start.61 = (bf16[64,2560]{1,0:T(8,128)(2,1)}, bf16[64,2560]{1,0:T(8,128)(2,1)S(1)}, u32[]{:S(2)}, u32[]{:S(2)}) collective-permute-start(bf16[64,2560]{1,0:T(8,128)(2,1)} %get-tuple-element.582), channel_id=1, source_target_pairs={{0,8},{1,9},{2,10},{3,11},{4,12},{5,13},{6,14},{7,15},{8,16},{9,17... | collective-permute-start | bytes 983048 | tf_op jit(solution)/shard_map/ppermute | solution.py:46
  416.5 37.2 %collective-permute-start.62 = (bf16[64,2560]{1,0:T(8,128)(2,1)}, bf16[64,2560]{1,0:T(8,128)(2,1)S(1)}, u32[]{:S(2)}, u32[]{:S(2)}) collective-permute-start(bf16[64,2560]{1,0:T(8,128)(2,1)} %get-tuple-element.583), channel_id=1, source_target_pairs={{0,16},{1,17},{2,18},{3,19},{4,20},{5,21},{6,22},{7,23},{8,24},{9,... | collective-permute-start | bytes 983048 | tf_op jit(solution)/shard_map/ppermute | solution.py:46
  419.0 34.7 %collective-permute-start.63 = (bf16[64,2560]{1,0:T(8,128)(2,1)}, bf16[64,2560]{1,0:T(8,128)(2,1)S(1)}, u32[]{:S(2)}, u32[]{:S(2)}) collective-permute-start(bf16[64,2560]{1,0:T(8,128)(2,1)} %get-tuple-element.584), channel_id=1, source_target_pairs={{0,24},{1,25},{2,26},{3,27},{4,28},{5,29},{6,30},{7,31},{8,0},{9,1... | collective-permute-start | bytes 983048 | tf_op jit(solution)/shard_map/ppermute | solution.py:46
  483.5 29.2 %collective-permute-start.73 = (bf16[64,2816]{1,0:T(8,128)(2,1)}, bf16[64,2816]{1,0:T(8,128)(2,1)S(1)}, u32[]{:S(2)}, u32[]{:S(2)}) collective-permute-start(bf16[64,2816]{1,0:T(8,128)(2,1)} %get-tuple-element.642), channel_id=1, source_target_pairs={{0,16},{1,17},{2,18},{3,19},{4,20},{5,21},{6,22},{7,23},{8,24},{9,... | collective-permute-start | bytes 1081352 | tf_op jit(solution)/shard_map/ppermute | solution.py:46
  486.0 32.3 %collective-permute-start.74 = (bf16[64,2816]{1,0:T(8,128)(2,1)}, bf16[64,2816]{1,0:T(8,128)(2,1)S(1)}, u32[]{:S(2)}, u32[]{:S(2)}) collective-permute-start(bf16[64,2816]{1,0:T(8,128)(2,1)} %get-tuple-element.643), channel_id=1, source_target_pairs={{0,24},{1,25},{2,26},{3,27},{4,28},{5,29},{6,30},{7,31},{8,0},{9,1... | collective-permute-start | bytes 1081352 | tf_op jit(solution)/shard_map/ppermute | solution.py:46
  (150 other events, 1653.6 us)
Sparse Core Ops, SparseCore 0:
  10.9 95.6 all-gather.2
  109.5 87.6 all-gather.4

commit v4 on v3

--- a/solution.py
+++ b/solution.py
@@ -493,13 +493,15 @@
         )(self.place, self.own, self.back)
 
 
-def neighbours(grid, v, reach):
-    out = [v]
-    for offset in range(1, reach + 1):
-        for by in (offset, -offset):
-            pairs = [(i, i + by) for i in range(grid.total) if 0 <= i + by < grid.total]
-            out.append(lax.ppermute(v, AXES, pairs))
-    return out
+def neighbours(grid, v):
+    def move(u, by):
+        pairs = [(i, i + by) for i in range(grid.total) if 0 <= i + by < grid.total]
+        return lax.ppermute(u, AXES, pairs)
+
+    left, right = move(v, 1), move(v, -1)
+    lefts = move(jnp.concatenate([v, left], 0), 2)
+    rights = move(jnp.concatenate([v, right], 0), -2)
+    return v, left, right, lefts, rights
 
 
 def layer_norm(inputs, scale_gain, offset_bias):
@@ -591,20 +593,29 @@
     phi = jnp.where(v < 0, tail, 1.0 - tail)
     return v * phi, phi + v * (e * (2.0 * math.pi) ** -0.5)
 
+def flat(ref):
+    w = ref[...]
+    return w.reshape(-1, w.shape[-1])
+
+def joined_spec(joined, block):
+    n, _, rows, d = joined.shape
+    per = d // block
+    return pl.BlockSpec((n, 1, rows, block), lambda i: (0, 1 + i // per, 0, i % per))
+
 def mlp_in_body(n_ref, w_ref, b_ref, act_ref, slope_ref):
-    v = dot(n_ref[...], w_ref[...]) + b_ref[...]
+    v = dot(n_ref[...], flat(w_ref)) + b_ref[...]
     act, slope = gelu_parts(v)
     act_ref[...] = act.astype(bf16)
     slope_ref[...] = slope.astype(bf16)
 
 def mlp_in(normed, w, bias, block=512):
     t, d = normed.shape
-    ff = w.shape[1]
+    ff = bias.shape[-1]
     out = pl.BlockSpec((t, block), lambda i: (0, i))
     shape = jax.ShapeDtypeStruct((t, ff), bf16)
     return pl.pallas_call(
         mlp_in_body, grid=(ff // block,),
-        in_specs=[pl.BlockSpec((t, d), lambda i: (0, 0)), pl.BlockSpec((d, block), lambda i: (0, i)), pl.BlockSpec((1, block), lambda i: (0, i))],
+        in_specs=[pl.BlockSpec((t, d), lambda i: (0, 0)), joined_spec(w, block), pl.BlockSpec((1, block), lambda i: (0, i))],
         out_specs=[out, out], out_shape=[shape, shape],
         compiler_params=pltpu.CompilerParams(vmem_limit_bytes=48 << 20),
         cost_estimate=FREE,
@@ -616,7 +627,7 @@
     low = g.astype(bf16)
     dpre_ref[...] = low
     db_ref[...] = jnp.sum(low.astype(f32), axis=0, keepdims=True)
-    dn = dot(low, w1_ref[...], NT)
+    dn = dot(low, flat(w1_ref), NT)
     @pl.when(pl.program_id(0) == 0)
     def _(): dn_ref[...] = dn
     @pl.when(pl.program_id(0) > 0)
@@ -624,12 +635,12 @@
 
 def mlp_back(dy, slope, w1, w2, block=512):
     t, d = dy.shape
-    ff = w1.shape[1]
+    ff = w2.shape[0]
     whole = pl.BlockSpec((t, d), lambda i: (0, 0))
     part = pl.BlockSpec((t, block), lambda i: (0, i))
     return pl.pallas_call(
         mlp_back_body, grid=(ff // block,),
-        in_specs=[whole, part, pl.BlockSpec((d, block), lambda i: (0, i)), pl.BlockSpec((block, d), lambda i: (i, 0))],
+        in_specs=[whole, part, joined_spec(w1, block), pl.BlockSpec((block, d), lambda i: (i, 0))],
         out_specs=[part, pl.BlockSpec((1, block), lambda i: (0, i)), whole],
         out_shape=[jax.ShapeDtypeStruct((t, ff), bf16), jax.ShapeDtypeStruct((1, ff), f32), jax.ShapeDtypeStruct((t, d), f32)],
         compiler_params=pltpu.CompilerParams(vmem_limit_bytes=48 << 20),
@@ -720,6 +731,8 @@
     def spec(shape, by_rows):
         if by_rows:
             return pl.BlockSpec((b, shape[1]), lambda i: (i, 0))
+        if len(shape) == 4:
+            return pl.BlockSpec((shape[0], 1) + shape[2:], lambda i: (0, 0, 0, 0))
         return pl.BlockSpec(shape, lambda i: (0, 0))
 
     out_specs = [pl.BlockSpec((b, w), lambda i: (i, 0)) for w, _ in outs]
@@ -767,7 +780,7 @@
 
 def attn_out_norm(attended, w, x, table):
     def body(a_ref, w_ref, x_ref, t_ref, first_ref, n_ref):
-        first = x_ref[...].astype(f32) + dot(a_ref[...], w_ref[...]) + t_ref[BIAS_OUT : BIAS_OUT + 1]
+        first = x_ref[...].astype(f32) + dot(a_ref[...], flat(w_ref)) + t_ref[BIAS_OUT : BIAS_OUT + 1]
         first_ref[...] = first
         xhat, _ = norm_parts(first)
         n_ref[...] = (
@@ -787,7 +800,7 @@
         low = first.astype(bf16)
         first_ref[...] = first
         branch_ref[...] = low
-        att_ref[...] = dot(low, w_ref[...], NT).astype(bf16)
+        att_ref[...] = dot(low, flat(w_ref), NT).astype(bf16)
         add_sums(sum_ref, (scaled, dn, low.astype(f32)))
 
     t, d = dy.shape
@@ -855,8 +868,10 @@
 
 
 def gate_body(n_near, tokens, d, *refs):
-    near, refs = refs[:n_near], refs[n_near:]
+    near_refs, refs = refs[:n_near], refs[n_near:]
     win_ref, wout_ref, gate_ref, drows_ref, pack_ref, sum_ref = refs
+    near = [ref[i : i + 1] for ref in near_refs for i in range(ref.shape[0])]
+    n_near = len(near)
     own = near[0][:, 2 * d :]
     match = [(near[i][:, 2 * d :] == own).astype(f32) for i in range(n_near)]
     count = functools.reduce(lambda a, b: a + b, match)[:, :1] * tokens
@@ -903,7 +918,7 @@
     return pl.pallas_call(
         functools.partial(gate_body, n, tokens, d),
         grid=(1,),
-        in_specs=[at(2 * d + 128)] * n
+        in_specs=[pl.BlockSpec(v.shape, lambda j: (0, 0)) for v in near]
         + [pl.BlockSpec((d, hidden), lambda j, b=b: (0, b)) for b in range(2)],
         out_specs=[at(d), at(d), pl.BlockSpec((8, k), lambda j: (0, 0)), at(128)],
         out_shape=[line(d), line(d), jax.ShapeDtypeStruct((8, k), bf16), line(128)],
@@ -962,9 +977,18 @@
     )
     gate_out_rows = dot(jnp.eye(rows, dtype=bf16), w_gate_out, NT).astype(bf16)
     gates = jnp.concatenate([w_gate_in, gate_out_rows], 1)
+    gate_out_rows = dot(jnp.eye(rows, dtype=bf16), w_gate_out, NT).astype(bf16)
+    gates = jnp.concatenate([w_gate_in, gate_out_rows], 1)
     full_qkv = lax.all_gather(w_qkv, AXES, axis=0, tiled=True)
-    a_two = Gather(grid, (w_attn_out, w_fc1))
-    a_three = Gather(grid, (gates, w_proj))
+    joined = lax.all_gather(
+        jnp.concatenate([w_attn_out] + [w_fc1[:, i : i + d] for i in range(0, w_fc1.shape[1], d)], 0),
+        AXES,
+    )
+    joined = joined.reshape(total, -1, rows, d)
+    if rows % 16:
+        joined = joined.transpose(1, 0, 2, 3).reshape(1, -1, d, d)
+    mixed_shard = jnp.concatenate([gates, w_proj], 0)
+    a_qkv, a_fc2 = Gather(grid, (w_qkv,)), Gather(grid, (w_fc2,))
 
     n_ch = lax.axis_size("ch")
     ch = lax.axis_index("ch")
@@ -991,23 +1015,23 @@
             a.set_state(state)
         return values
 
-    a_two.along_z()
+    a_qkv.along_z()
     for _ in range(3):
         a_small.next()
     pool = jnp.asarray(pool_table(PS, FS), bf16)
     pooled_own = dot(pool, features.reshape(n_img * own_ch, -1), NT).astype(bf16)
-    a_two.pack_first()
-    a_small.v, pooled_own = step((a_two,), a_small.v, pooled_own)
-
-    a_two.first()
-    a_two.pack_second()
+    a_qkv.pack_first()
+    a_small.v, pooled_own = step((a_qkv,), a_small.v, pooled_own)
+
+    a_qkv.first()
+    a_qkv.pack_second()
     while a_small.next():
         pass
-    every, pooled_own, w_fc2 = step((a_two, a_three), a_small.v, pooled_own, w_fc2)
-
-    full_fc2 = lax.all_gather(w_fc2, AXES, axis=0, tiled=True)
-    a_two.second()
-    a_two.early()
+    every, pooled_own = step((a_qkv, a_fc2), a_small.v, pooled_own)
+
+    a_qkv.second()
+    a_fc2.along_z()
+    a_fc2.pack_first()
     every = every.astype(f32)
     table = every[:, : LINES * rows].reshape(total, LINES, rows)
     table = table.transpose(1, 0, 2).reshape(LINES, d)
@@ -1017,50 +1041,56 @@
     bias_qkv = jnp.concatenate([full_bias_qv[:d], jnp.zeros((d,), f32), full_bias_qv[d:]])[None]
     x32 = x.astype(f32)
     normed1 = layer_norm(x32, table[LN1_GAIN], table[LN1_BIAS]).astype(bf16)
+    cuts = []
+    for k in range(n_ch):
+        to = lax.rem(ch + k, n_ch)
+        cuts.append(lax.dynamic_slice(pooled_own, (0, to * own_ch), (count, own_ch)))
+    normed1, table, full_bias_fc1, bias_qkv, cuts = step(
+        (a_qkv, a_fc2), normed1, table, full_bias_fc1, bias_qkv, cuts
+    )
+
+    a_qkv.early()
+    a_qkv.cross()
+    dy_far = peer_half(dy)
+    normed1, cuts, dy_far = step((a_qkv, a_fc2), normed1, cuts, dy_far)
+
+    def pooled_piece(k):
+        return along_ch(cuts[k], k) if k else cuts[k]
+
+    a_fc2.first()
+    early = n_ch // 2 + 1
+    pieces = [pooled_piece(k) for k in range(early)]
+    (full_qkv,) = a_qkv.whole()
     qkv = project(normed1, full_qkv, bias_qkv)
     attended, log_total = attend(qkv)
-    attended, log_total, table, full_bias_fc1, pooled_own = step(
-        (a_two, a_three), attended, log_total, table, full_bias_fc1, pooled_own
-    )
-
-    a_two.cross()
-    dy_far = peer_half(dy)
-    attended, pooled_own, dy_far = step((a_two, a_three), attended, pooled_own, dy_far)
-
-    a_three.along_z()
-    a_three.pack_first()
-
-    def pooled_piece(k):
-        to = lax.rem(ch + k, n_ch)
-        piece = lax.dynamic_slice(pooled_own, (0, to * own_ch), (count, own_ch))
-        return along_ch(piece, k) if k else piece
-
-    early = n_ch // 2 + 1
-    pieces = [pooled_piece(k) for k in range(early)]
-    full_attn_out, full_fc1 = a_two.whole()
-    first_sum, normed2 = attn_out_norm(attended, full_attn_out, x, table)
-    activation, slope = mlp_in(normed2, full_fc1, full_bias_fc1)
-    activation, slope, normed2, full_attn_out, full_fc1, first_sum, pieces, pooled_own = step(
-        (a_three,),
-        activation,
-        slope,
-        normed2,
-        full_attn_out,
-        full_fc1,
-        first_sum,
-        pieces,
-        pooled_own,
-    )
-
-    a_three.first()
-    a_three.pack_second()
+    a_fc2.s0, a_fc2.r1, attended = lax.optimization_barrier((a_fc2.s0, a_fc2.r1, attended))
+    a_fc2.pack_second()
+    attended, log_total, pieces, cuts, full_qkv, mixed_shard = step(
+        (a_fc2,), attended, log_total, pieces, cuts, full_qkv, mixed_shard
+    )
+
+    mixed_w = lax.all_gather(mixed_shard, AXES)
+    a_fc2.second()
+    attended_far = peer(attended)
+    first_sum, normed2 = attn_out_norm(attended, joined, x, table)
+    activation, slope = mlp_in(normed2, joined, full_bias_fc1)
+    activation, slope, normed2, first_sum, cuts, attended_far = step(
+        (a_fc2,), activation, slope, normed2, first_sum, cuts, attended_far
+    )
+
     activation_far, normed2_far = peer(activation), peer(normed2)
     pieces = pieces + [pooled_piece(k) for k in range(early, n_ch)]
-    activation_far, normed2_far, slope, attended, pieces = step(
-        (a_three,), activation_far, normed2_far, slope, attended, pieces
-    )
-
-    a_three.second()
+    a_fc2.early()
+    a_fc2.cross()
+    pooled = jnp.zeros((count, n_ch * own_ch), bf16)
+    for k in range(n_ch):
+        from_ch = lax.rem(ch - k + n_ch, n_ch)
+        pooled = lax.dynamic_update_slice(pooled, pieces[k], (0, from_ch * own_ch))
+    activation_far, normed2_far, slope, attended, pieces, pooled = step(
+        (a_fc2,), activation_far, normed2_far, slope, attended, pieces, pooled
+    )
+
+    (full_fc2,) = a_fc2.whole()
     ff = activation.shape[1]
     s_one = Scatter(
         grid,
@@ -1068,31 +1098,35 @@
         2 * ff // total,
         d // 4,
     )
-    slope, attended = step((a_three, s_one), slope, attended)
+    slope, attended, pieces, full_fc2 = step((s_one,), slope, attended, pieces, full_fc2)
 
     s_one.first()
-    d_pre, d_bias_fc1, d_normed2 = mlp_back(dy, slope, full_fc1, full_fc2)
+    d_pre, d_bias_fc1, d_normed2 = mlp_back(dy, slope, joined, full_fc2)
     d_first, d_branch, d_attended, sums_two = norm_two_back(
-        d_normed2, first_sum, dy, table, full_attn_out
+        d_normed2, first_sum, dy, table, joined
     )
     s_one.got, d_attended = lax.optimization_barrier((s_one.got, d_attended))
     s_one.fold_second()
     d_attended, d_first, d_branch, d_pre, full_fc2, attended, pieces = step(
-        (s_one, a_three), d_attended, d_first, d_branch, d_pre, full_fc2, attended, pieces
+        (s_one,), d_attended, d_first, d_branch, d_pre, full_fc2, attended, pieces
     )
 
     s_one.second()
-    a_three.early()
-    a_three.cross()
     d_pre_far, d_branch_far = peer_half(d_pre), peer_half(d_branch)
-    attended_far = peer(attended)
+    full_gates = mixed_w[:, :rows].reshape(d, 2 * hidden)
+    full_proj = mixed_w[:, rows:].reshape(-1, d)
+    projected, spatial, row_sums, d_gate, dy_sum = adapter(ch, pieces, full_proj, table, dy)
+    ids_plus = sample_of.astype(f32) + 1.0
+    carried = jnp.concatenate(
+        [row_sums, d_gate, jnp.broadcast_to(ids_plus[:, None], (1, 128))], 1
+    )
+    s_one.more, carried = lax.optimization_barrier((s_one.more, carried))
     s_one.fold_z()
-    d_attended, d_branch, d_pre, d_pre_far, d_branch_far, attended_far = step(
-        (s_one, a_three), d_attended, d_branch, d_pre, d_pre_far, d_branch_far, attended_far
-    )
-
-    s_one.along_z()
-    full_gates, full_proj = a_three.whole()
+    d_attended, d_branch, d_pre, d_pre_far, d_branch_far, carried, full_gates, full_proj = step(
+        (s_one,), d_attended, d_branch, d_pre, d_pre_far, d_branch_far, carried, full_gates, full_proj
+    )
+
+    near = neighbours(grid, carried)
     s_two = Scatter(
         grid,
         [
@@ -1102,51 +1136,42 @@
         2 * rows,
         (ff + d) // 4,
     )
-    d_attended, normed1, pieces, full_gates, full_proj = step(
-        (s_two,), d_attended, normed1, pieces, full_gates, full_proj
-    )
+    d_attended, normed1, near = step((s_one, s_two), d_attended, normed1, near)
 
     s_two.first()
-    projected, spatial, row_sums, d_gate, dy_sum = adapter(ch, pieces, full_proj, table, dy)
+    s_one.along_z()
     d_query, d_key, d_value = attend_back(qkv, d_attended, log_total)
-    s_two.got, d_query, row_sums = lax.optimization_barrier((s_two.got, d_query, row_sums))
-    s_two.fold_second()
-    d_query, d_key, d_value, normed1, row_sums, d_gate, dy_sum, pieces = step(
-        (s_one, s_two), d_query, d_key, d_value, normed1, row_sums, d_gate, dy_sum, pieces
-    )
-
-    ids_plus = sample_of.astype(f32) + 1.0
-    carried = jnp.concatenate(
-        [row_sums, d_gate, jnp.broadcast_to(ids_plus[:, None], (1, 128))], 1
-    )
-    near = neighbours(grid, carried, REACH)
-    pooled = jnp.zeros((count, n_ch * own_ch), bf16)
-    for k in range(n_ch):
-        from_ch = lax.rem(ch - k + n_ch, n_ch)
-        pooled = lax.dynamic_update_slice(pooled, pieces[k], (0, from_ch * own_ch))
-    d_mixed = jnp.concatenate([d_query, d_key, d_value], -1)
-    d_mixed_far, normed1_far = peer_half(d_mixed), peer(normed1)
-    d_mixed, d_mixed_far, normed1_far, near, pooled = step(
-        (s_two,), d_mixed, d_mixed_far, normed1_far, near, pooled
-    )
-
-    pooled_far = peer(pooled)
     gate, d_rows, pack, gate_sum = gate_step(near, full_gates, d, hidden, count)
     d_projected, d_depth, d_bias_depth, d_bias_proj = adapter_back(
         dy, projected, gate, d_rows, table
     )
+    s_two.got, d_query, d_projected = lax.optimization_barrier((s_two.got, d_query, d_projected))
+    s_two.fold_second()
+    d_query, d_key, d_value, normed1, pack, d_projected, gate, pooled = step(
+        (s_one, s_two), d_query, d_key, d_value, normed1, pack, d_projected, gate, pooled
+    )
+
+    d_mixed = jnp.concatenate([d_query, d_key, d_value], -1)
+    d_mixed_far, normed1_far, pooled_far = peer_half(d_mixed), peer(normed1), peer(pooled)
+    pack_far, d_projected_far = peer(pack), peer_half(d_projected)
     d_pooled = dot(d_projected, full_proj, NT).astype(bf16)
-    pack, d_projected, pooled_far, gate, d_mixed, d_pooled = step(
-        (s_two,), pack, d_projected, pooled_far, gate, d_mixed, d_pooled
-    )
-
-    pack_far, d_projected_far = peer(pack), peer_half(d_projected)
+    d_mixed, d_mixed_far, normed1_far, pooled_far, pack_far, d_projected_far, d_pooled = step(
+        (s_two,),
+        d_mixed,
+        d_mixed_far,
+        normed1_far,
+        pooled_far,
+        pack_far,
+        d_projected_far,
+        d_pooled,
+    )
+
+    s_two.second()
     lines = jnp.concatenate([sums_two[2:], sums_two[:2], dy_sum, d_bias_proj, d_bias_depth, d_depth], 0)
     lines = lines.reshape(LINES - 2, total, rows).transpose(1, 0, 2).reshape(total, -1)
     small = jnp.concatenate(
         [lines, d_bias_fc1.reshape(total, -1), jnp.broadcast_to(gate_sum, (total, 128))], 1
     )
-    s_two.second()
     back = []
     for k in range(n_ch):
         to = lax.rem(ch + k, n_ch)

time: 551 us -> 527 us (0.956)
  waiting for transfers between devices: 137 us -> 92.9 us
  local copies, waits for them, and re-layouts: 61.6 us -> 70.5 us
  starting transfers between devices: 81.3 us -> 88.4 us
    ppermute x57, waiting for transfers between devices: 94.2 us -> 69.8 us  [send(): return lax.ppermute(v, AXES, pairs)]
    all_gather x2, waiting for transfers between devices: 22.6 us -> 0.02 us  [the longest x1 0.02 us: shards(): mixed_w = lax.all_gather(mixed_shard, AXES)]
    ppermute x57, starting transfers between devices: 42.8 us -> 51.4 us  [send(): return lax.ppermute(v, AXES, pairs)]
    slice x0 -> x2, local copies, waits for them, and re-layouts: none -> 7.42 us  [the longest x1 4.06 us: shards(): full_proj = mixed_w[:, rows:].reshape(-1, d)]
    ppermute x6 -> x4, starting transfers between devices: 19.7 us -> 16.9 us  [move(): return lax.ppermute(u, AXES, pairs)]
    unnamed x208 -> x164, local copies, waits for them, and re-layouts: 30.3 us -> 32.1 us
  transfers between devices with their start and end apart: 81 -> 79, of which waited for: 27 -> 27; matrix products, arithmetic and copies ran while one was open for 9% -> 11% of each run, Pallas kernels for 36% -> 42%
where the time goes in v4:
time: 527 us; the launch traced here: 519 us
  Pallas kernels  224 us (43%)
  waiting for transfers between devices  92.9 us (18%)
  starting transfers between devices  88.4 us (17%)
  local copies, waits for them, and re-layouts  70.5 us (13%)
  between operations  18.3 us (3%)
  other arithmetic  13.2 us (3%)
  matrix products  11.5 us (2%)
    ppermute x57, waiting for transfers between devices, send(): return lax.ppermute(v, AXES, pairs)  69.8 us
    ppermute x57, starting transfers between devices, send(): return lax.ppermute(v, AXES, pairs)  51.4 us
    pallas_call x3, Pallas kernels, __init__(): pl.pallas_call(functools.partial(weight_grad_body, (nx, ny), shapes, None...  44.3 us
    unnamed x164, local copies, waits for them, and re-layouts  32.1 us
    pallas_call x3, Pallas kernels, rows_call(): pl.pallas_call(body, grid=(steps,), in_specs=[spec(a.shape, by_rows) for...  26 us
    pallas_call x1, Pallas kernels, attend_back(): pl.pallas_call(attend_back_body, grid=(n,), in_specs=[spec(0), spec(1), s...  25.5 us
    pallas_call x2, Pallas kernels, columns_call(): pl.pallas_call(body, grid=(width // block,), in_specs=[spec(a.shape, by)...  17.1 us
    pallas_call x1, Pallas kernels, mlp_back(): pl.pallas_call(mlp_back_body, grid=(ff // block,), in_specs=[whole, part,...  17 us
  transfers between devices with their start and end apart: 79, of which 27 were waited for; matrix products, arithmetic and copies ran while one was open for 11% of the time, Pallas kernels for 42%

profile of v4, /device:TPU:9, one launch (start us, length us, event | category | flops | bytes accessed | tf_op | source)
XLA Modules:
  0.0 518.8 jit_solution(8824028920082549103)
XLA Ops:
  17.9 6.8 %concatenate.85 = bf16[736]{0:T(1024)(128)(2,1)S(1)} concatenate(bf16[32]{0:T(256)(128)(2,1)} %param.27, bf16[32]{0:T(256)(128)(2,1)} %param.28, bf16[32]{0:T(256)(128)(2,1)} %param.32, bf16[32]{0:T(256)(128)(2,1)} %param.33, bf16[32]{0:T(256)(128)(2,1)} %param.34, bf16[32]{0:T(256)(128)(2,1)} %param.38, bf16[32]{0:T(256)(128)(2,1)} %param.40, bf16[32]{0:T(256)(128)(2,1)} %param.42, ...), dimensions={0} | concatenate | bytes 2944 | tf_op jit(solution)/shard_map/concatenate | solution.py:976
  26.3 4.5 convolution_convert_fusion.1
  62.8 14.9 %collective-permute-done.13 = bf16[128,1024]{1,0:T(8,128)(2,1)} collective-permute-done((bf16[128,1024]{1,0:T(8,128)(2,1)}, bf16[128,1024]{1,0:T(8,128)(2,1)}, u32[]{:S(2)}, u32[]{:S(2)}) %collective-permute-start.13) | collective-permute-done | bytes 262176 | tf_op jit(solution)/shard_map/ppermute | solution.py:46
  78.7 4.6 collective-permute-done.12
  112.3 7.2 %project.1.q_ref.k_ref.v_ref = bf16[576,3072]{1,0:T(8,128)(2,1)S(1)} custom-call(bf16[576,1024]{1,0:T(8,128)(2,1)S(1)} %copy-done.11, bf16[1024,3072]{1,0:T(8,128)(2,1)} %bitcast.130, f32[1,3072]{1,0:T(1,128)S(1)} %bitcast.142), custom_call_target="tpu_custom_call" | custom-call | tf_op jit(solution)/shard_map/project/pallas_call | solution.py:833
  121.3 14.6 %attend.1 = (bf16[576,1024]{1,0:T(8,128)(2,1)S(1)}, f32[576,1024]{1,0:T(8,128)S(1)}) custom-call(bf16[576,3072]{1,0:T(8,128)(2,1)} %copy-done.2, bf16[576,3072]{1,0:T(8,128)(2,1)} %copy-done.2, bf16[576,3072]{1,0:T(8,128)(2,1)} %copy-done.2), custom_call_target="tpu_custom_call" | custom-call | tf_op jit(solution)/shard_map/attend/pallas_call | solution.py:538
  144.2 5.2 %attn_out.1 = (f32[576,1024]{1,0:T(8,128)S(1)}, bf16[576,1024]{1,0:T(8,128)(2,1)}) custom-call(bf16[576,1024]{1,0:T(8,128)(2,1)S(1)} %copy-done.22, bf16[32,5,32,1024]{3,2,1,0:T(8,128)(2,1)} %bitcast.145, bf16[576,1024]{1,0:T(8,128)(2,1)S(1)} %bitcast.137, f32[17,1024]{1,0:T(8,128)S(1)} %reshape.192.t_ref.refs_5_.table_ref), custom_call_target="tpu_custom_call" | custom-call | tf_op jit(solution)/shard_map/attn_out/pallas_call | solution.py:743
  150.8 16.2 %mlp_in.1 = (bf16[576,4096]{1,0:T(8,128)(2,1)}, bf16[576,4096]{1,0:T(8,128)(2,1)}) custom-call(bf16[576,1024]{1,0:T(8,128)(2,1)} %get-tuple-element.404.n_ref.refs_0_, bf16[32,5,32,1024]{3,2,1,0:T(8,128)(2,1)} %bitcast.146, f32[1,4096]{1,0:T(1,128)S(1)} %bitcast.141), custom_call_target="tpu_custom_call" | custom-call | tf_op jit(solution)/shard_map/mlp_in/pallas_call | solution.py:616
  170.2 7.1 %collective-permute-done.33.refs_3_ = bf16[576,384]{1,0:T(8,128)(2,1)S(1)} collective-permute-done((bf16[576,384]{1,0:T(8,128)(2,1)S(1)}, bf16[576,384]{1,0:T(8,128)(2,1)S(1)}, u32[]{:S(2)}, u32[]{:S(2)}) %collective-permute-start.33) | collective-permute-done | bytes 442400 | tf_op jit(solution)/shard_map/ppermute | solution.py:1003
  185.3 11.8 %weight_grad.3 = (bf16[4,2,256,256]{3,2,1,0:T(8,128)(2,1)}, bf16[4,2,256,256]{3,2,1,0:T(8,128)(2,1)}, bf16[4,2,256,256]{3,2,1,0:T(8,128)(2,1)}, bf16[4,2,256,256]{3,2,1,0:T(8,128)(2,1)}) custom-call(s32[4]{0:T(128)} %copy-done.46, bf16[576,4096]{1,0:T(8,128)(2,1)} %get-tuple-element.584.refs_0_.a_ref, bf16[576,4096]{1,0:T(8,128)(2,1)} %collective-permute-done.31.refs_1_, ...), custom_call_target="tpu_custom_call" | custom-call | tf_op jit(solution)/shard_map/weight_grad/pallas_call | solution.py:290
  197.1 4.0 assemble.3
  206.1 17.0 %mlp_back.1 = (bf16[576,4096]{1,0:T(8,128)(2,1)}, f32[1,4096]{1,0:T(1,128)S(1)}, f32[576,1024]{1,0:T(8,128)S(1)}) custom-call(bf16[576,1024]{1,0:T(8,128)(2,1)S(1)} %bitcast.133, bf16[576,4096]{1,0:T(8,128)(2,1)} %get-tuple-element.432.slope_ref, bf16[32,5,32,1024]{3,2,1,0:T(8,128)(2,1)} %bitcast.147, bf16[4096,1024]{1,0:T(8,128)(2,1)} %bitcast.128), custom_call_target="tpu_custom_call" | custom-call | tf_op jit(solution)/shard_map/mlp_back/pallas_call | solution.py:641
  224.5 7.3 %norm_two.1 = (f32[576,1024]{1,0:T(8,128)S(1)}, bf16[576,1024]{1,0:T(8,128)(2,1)S(1)}, bf16[576,1024]{1,0:T(8,128)(2,1)S(1)}, f32[3,1024]{1,0:T(4,128)S(1)}) custom-call(f32[576,1024]{1,0:T(8,128)} %copy-done.36, f32[576,1024]{1,0:T(8,128)} %copy-done.13, bf16[576,1024]{1,0:T(8,128)(2,1)S(1)} %bitcast.134, f32[17,1024]{1,0:T(8,128)S(1)} %reshape.192.t_ref.refs_5_.table_ref, ...), custom_call_target="tpu_custom_call" | custom-call | tf_op jit(solution)/shard_map/norm_two/pallas_call | solution.py:743
  242.8 4.1 slice.249
  250.3 8.2 %adapter.1 = (f32[576,1024]{1,0:T(8,128)S(1)}, f32[576,1024]{1,0:T(8,128)}, f32[1,1024]{1,0:T(1,128)S(1)}, f32[1,1024]{1,0:T(1,128)S(1)}, f32[1,1024]{1,0:T(1,128)S(1)}) custom-call(s32[1]{0:T(128)} %bitcast.30.pos_ref, bf16[576,384]{1,0:T(8,128)(2,1)S(1)} %copy-done.24, bf16[576,384]{1,0:T(8,128)(2,1)} %collective-permute-done.22.refs_1_, ...), custom_call_target="tpu_custom_call" | custom-call | tf_op jit(solution)/shard_map/adapter/pallas_call | solution.py:687
  260.0 4.7 fold_z.3
  277.2 7.6 %collective-permute-start.43 = (f32[2,2176]{1,0:T(2,128)S(1)}, f32[2,2176]{1,0:T(2,128)S(1)}, u32[]{:S(2)}, u32[]{:S(2)}) collective-permute-start(f32[2,2176]{1,0:T(2,128)S(1)} %get-tuple-element.700), channel_id=1, source_target_pairs={{2,0},{3,1},{4,2},{5,3},{6,4},{7,5},{8,6},{9,7},{10,8},{11,9},{12,... | collective-permute-start | bytes 52232 | tf_op jit(solution)/shard_map/ppermute | solution.py:499
  284.8 15.3 %weight_grad.4 = (bf16[4,2,64,1280]{3,2,1,0:T(8,128)(2,1)}, bf16[4,2,64,1280]{3,2,1,0:T(8,128)(2,1)}, bf16[4,2,64,1280]{3,2,1,0:T(8,128)(2,1)}, bf16[4,2,64,1280]{3,2,1,0:T(8,128)(2,1)}) custom-call(s32[4]{0:T(128)} %copy-done.46, bf16[576,1024]{1,0:T(8,128)(2,1)} %get-tuple-element.404.n_ref.refs_0_, bf16[576,1024]{1,0:T(8,128)(2,1)} %collective-permute-done.32.refs_1_, ...), custom_call_target="tpu_custom_call" | custom-call | tf_op jit(solution)/shard_map/weight_grad/pallas_call | solution.py:290
  300.3 4.7 collective-permute-start.45
  305.2 25.5 %attend_back.1 = (bf16[576,1024]{1,0:T(8,128)(2,1)S(1)}, bf16[576,1024]{1,0:T(8,128)(2,1)S(1)}, bf16[576,1024]{1,0:T(8,128)(2,1)S(1)}) custom-call(bf16[576,3072]{1,0:T(8,128)(2,1)} %copy-done.2, bf16[576,3072]{1,0:T(8,128)(2,1)} %copy-done.2, bf16[576,3072]{1,0:T(8,128)(2,1)} %copy-done.2, bf16[576,1024]{1,0:T(8,128)(2,1)S(1)} %copy-done.40, ...), custom_call_target="tpu_custom_call" | custom-call | tf_op jit(solution)/shard_map/attend_back/pallas_call | solution.py:578
  333.7 5.5 %adapter_back.1 = (bf16[576,1024]{1,0:T(8,128)(2,1)S(1)}, f32[9,1024]{1,0:T(8,128)S(1)}, f32[1,1024]{1,0:T(1,128)S(1)}, f32[1,1024]{1,0:T(1,128)S(1)}) custom-call(bf16[576,1024]{1,0:T(8,128)(2,1)S(1)} %bitcast.136, f32[576,1024]{1,0:T(8,128)S(1)} %copy-done.34, f32[1,1024]{1,0:T(1,128)S(1)} %get-tuple-element.586.gate_ref.g_ref, ...), custom_call_target="tpu_custom_call" | custom-call | tf_op jit(solution)/shard_map/adapter_back/pallas_call | solution.py:718
  350.8 4.7 collective-permute-done.52.refs_5_.refs_7_.refs_9_.refs_11_
  361.6 17.2 %weight_grad.5 = (bf16[4,2,64,1408]{3,2,1,0:T(8,128)(2,1)}, bf16[4,2,64,1408]{3,2,1,0:T(8,128)(2,1)}, bf16[4,2,64,1408]{3,2,1,0:T(8,128)(2,1)}, bf16[4,2,64,1408]{3,2,1,0:T(8,128)(2,1)}) custom-call(s32[4]{0:T(128)} %copy-done.46, bf16[576,1024]{1,0:T(8,128)(2,1)} %fusion.5.n_ref.refs_0_, bf16[576,1024]{1,0:T(8,128)(2,1)} %copy-done.58, ...), custom_call_target="tpu_custom_call" | custom-call | tf_op jit(solution)/shard_map/weight_grad/pallas_call | solution.py:290
  379.9 5.3 %fold_z.4 = (f32[64,2560]{1,0:T(8,128)}, bf16[64,2560]{1,0:T(8,128)(2,1)}, bf16[64,2560]{1,0:T(8,128)(2,1)}, bf16[64,2560]{1,0:T(8,128)(2,1)}) custom-call(s32[4]{0:T(128)} %copy-done.46, bf16[4,2,64,1280]{3,2,1,0:T(8,128)(2,1)} %get-tuple-element.542.refs_0_, bf16[4,2,64,1280]{3,2,1,0:T(8,128)(2,1)} %collective-permute-done.47.refs_1_, ...), custom_call_target="tpu_custom_call" | custom-call | tf_op jit(solution)/shard_map/fold_z/pallas_call | solution.py:406
  385.2 5.7 %collective-permute-done.57 = bf16[576,384]{1,0:T(8,128)(2,1)} collective-permute-done((bf16[576,384]{1,0:T(8,128)(2,1)}, bf16[576,384]{1,0:T(8,128)(2,1)}, u32[]{:S(2)}, u32[]{:S(2)}) %collective-permute-start.57) | collective-permute-done | bytes 442400 | tf_op jit(solution)/shard_map/ppermute | solution.py:1003
  399.4 9.9 %layer_output.1 = bf16[576,1024]{1,0:T(8,128)(2,1)} custom-call(bf16[576,4096]{1,0:T(8,128)(2,1)} %get-tuple-element.584.refs_0_.a_ref, bf16[4096,1024]{1,0:T(8,128)(2,1)} %bitcast.129, f32[576,1024]{1,0:T(8,128)S(1)} %copy-done.14, f32[17,1024]{1,0:T(8,128)S(1)} %reshape.192.t_ref.refs_5_.table_ref, f32[1,1024]{1,0:T(1,128)S(1)} %get-tuple-element.586.gate_ref.g_ref, ...), custom_call_target="tpu_custom_call" | custom-call | tf_op jit(solution)/shard_map/layer_output/pallas_call | solution.py:833
  409.3 13.5 %norm_one.1 = (bf16[576,1024]{1,0:T(8,128)(2,1)}, f32[4,1024]{1,0:T(4,128)S(1)}) custom-call(bf16[576,1024]{1,0:T(8,128)(2,1)S(1)} %copy-done.16, bf16[576,1024]{1,0:T(8,128)(2,1)S(1)} %copy-done.18, bf16[576,1024]{1,0:T(8,128)(2,1)S(1)} %copy-done.20, bf16[1024,3072]{1,0:T(8,128)(2,1)} %bitcast.131, bf16[576,1024]{1,0:T(8,128)(2,1)S(1)} %bitcast.138, ...), custom_call_target="tpu_custom_call" | custom-call | tf_op jit(solution)/shard_map/norm_one/pallas_call | solution.py:743
  443.3 5.0 collective-permute-done.66.refs_2_
  450.0 5.3 %fold_z.5 = (f32[64,2816]{1,0:T(8,128)}, bf16[64,2816]{1,0:T(8,128)(2,1)}, bf16[64,2816]{1,0:T(8,128)(2,1)}, bf16[64,2816]{1,0:T(8,128)(2,1)}) custom-call(s32[4]{0:T(128)} %copy-done.46, bf16[4,2,64,1408]{3,2,1,0:T(8,128)(2,1)} %get-tuple-element.622.refs_0_, bf16[4,2,64,1408]{3,2,1,0:T(8,128)(2,1)} %collective-permute-done.62.refs_1_, ...), custom_call_target="tpu_custom_call" | custom-call | tf_op jit(solution)/shard_map/fold_z/pallas_call | solution.py:406
  468.6 19.4 %collective-permute-done.71.refs_2_ = bf16[64,2816]{1,0:T(8,128)(2,1)S(1)} collective-permute-done((bf16[64,2816]{1,0:T(8,128)(2,1)}, bf16[64,2816]{1,0:T(8,128)(2,1)S(1)}, u32[]{:S(2)}, u32[]{:S(2)}) %collective-permute-start.71) | collective-permute-done | bytes 360480 | tf_op jit(solution)/shard_map/ppermute | solution.py:46
  488.0 4.8 collective-permute-done.72.refs_3_
  503.6 4.0 convolution_convert_fusion.2
  (425 shorter events, 209.0 us)
Async XLA Ops:
  7.2 134.5 %all-gather.5.cloned.1.call-start = ((), (), s32[]{:S(2)}) async-start(), calls=%async_computation | async-start | bytes 10813440 | tf_op jit(solution)/shard_map/all_gather | solution.py:983
  12.4 230.5 %all-gather.7.cloned.1.call-start = ((), (), s32[]{:S(2)}) async-start(), calls=%async_computation.1 | async-start | bytes 5406720 | tf_op jit(solution)/shard_map/all_gather | solution.py:1072
  12.5 25.2 %collective-permute-start.1 = (bf16[32,3072]{1,0:T(8,128)(2,1)}, bf16[32,3072]{1,0:T(8,128)(2,1)}, u32[]{:S(2)}, u32[]{:S(2)}) collective-permute-start(bf16[32,3072]{1,0:T(8,128)(2,1)} %param.29), channel_id=1, source_target_pairs={{0,16},{1,17},{2,18},{3,19},{4,20},{5,21},{6,22},{7,23},{8,24},{9,... | collective-permute-start | bytes 589832 | tf_op jit(solution)/shard_map/ppermute | solution.py:46
  52.7 30.6 %collective-permute-start.12 = (bf16[128,1024]{1,0:T(8,128)(2,1)}, bf16[128,1024]{1,0:T(8,128)(2,1)}, u32[]{:S(2)}, u32[]{:S(2)}) collective-permute-start(bf16[128,1024]{1,0:T(8,128)(2,1)} %param.37), channel_id=1, source_target_pairs={{0,8},{1,9},{2,10},{3,11},{4,12},{5,13},{6,14},{7,15},{8,16},{9,17... | collective-permute-start | bytes 786440 | tf_op jit(solution)/shard_map/ppermute | solution.py:46
  54.9 31.1 %collective-permute-start.10 = (bf16[8,32,1536]{2,1,0:T(8,128)(2,1)S(1)}, bf16[8,32,1536]{2,1,0:T(8,128)(2,1)}, u32[]{:S(2)}, u32[]{:S(2)}) collective-permute-start(bf16[8,32,1536]{2,1,0:T(8,128)(2,1)S(1)} %pad_maximum_fusion.2.refs_0_), channel_id=1, source_target_pairs={{0,2},{1,3},{2,0},{3,1},{4,6},{5,7},{6,4},{7,5},{8,10},{9,11},{10,... | collective-permute-start | bytes 2359304 | tf_op jit(solution)/shard_map/ppermute | solution.py:46
  56.9 29.1 %collective-permute-start.11 = (bf16[8,32,1536]{2,1,0:T(8,128)(2,1)S(1)}, bf16[8,32,1536]{2,1,0:T(8,128)(2,1)}, u32[]{:S(2)}, u32[]{:S(2)}) collective-permute-start(bf16[8,32,1536]{2,1,0:T(8,128)(2,1)S(1)} %pad_maximum_fusion.3.refs_2_), channel_id=1, source_target_pairs={{0,4},{1,5},{2,6},{3,7},{4,0},{5,1},{6,2},{7,3},{8,12},{9,13},{10,... | collective-permute-start | bytes 2359304 | tf_op jit(solution)/shard_map/ppermute | solution.py:46
  96.1 39.9 %collective-permute-start.20 = (bf16[4,128,512]{2,1,0:T(8,128)(2,1)}, bf16[4,128,512]{2,1,0:T(8,128)(2,1)}, u32[]{:S(2)}, u32[]{:S(2)}) collective-permute-start(bf16[4,128,512]{2,1,0:T(8,128)(2,1)} %pad_maximum_fusion.4), channel_id=1, source_target_pairs={{0,4},{1,5},{2,6},{3,7},{4,0},{5,1},{6,2},{7,3},{8,12},{9,13},{10,... | collective-permute-start | bytes 1572872 | tf_op jit(solution)/shard_map/ppermute | solution.py:46
  97.2 38.8 %collective-permute-start.21 = (bf16[4,128,512]{2,1,0:T(8,128)(2,1)}, bf16[4,128,512]{2,1,0:T(8,128)(2,1)}, u32[]{:S(2)}, u32[]{:S(2)}) collective-permute-start(bf16[4,128,512]{2,1,0:T(8,128)(2,1)} %pad_maximum_fusion.5), channel_id=1, source_target_pairs={{0,2},{1,3},{2,0},{3,1},{4,6},{5,7},{6,4},{7,5},{8,10},{9,11},{10,... | collective-permute-start | bytes 1572872 | tf_op jit(solution)/shard_map/ppermute | solution.py:46
  99.3 41.5 %collective-permute-start.22 = (bf16[576,384]{1,0:T(8,128)(2,1)}, bf16[576,384]{1,0:T(8,128)(2,1)}, u32[]{:S(2)}, u32[]{:S(2)}) collective-permute-start(bf16[576,384]{1,0:T(8,128)(2,1)} %get-tuple-element.386), channel_id=1, source_target_pairs={{0,1},{1,2},{2,3},{3,0},{4,5},{5,6},{6,7},{7,4},{8,9},{9,10},{10,1... | collective-permute-start | bytes 1327112 | tf_op jit(solution)/shard_map/ppermute | solution.py:1003
  100.7 40.1 %collective-permute-start.23 = (bf16[576,384]{1,0:T(8,128)(2,1)}, bf16[576,384]{1,0:T(8,128)(2,1)}, u32[]{:S(2)}, u32[]{:S(2)}) collective-permute-start(bf16[576,384]{1,0:T(8,128)(2,1)} %get-tuple-element.387), channel_id=1, source_target_pairs={{0,2},{1,3},{2,0},{3,1},{4,6},{5,7},{6,4},{7,5},{8,10},{9,11},{10,... | collective-permute-start | bytes 1327112 | tf_op jit(solution)/shard_map/ppermute | solution.py:1003
  140.9 26.3 %collective-permute-start.26 = (bf16[576,1024]{1,0:T(8,128)(2,1)}, bf16[576,1024]{1,0:T(8,128)(2,1)}, u32[]{:S(2)}, u32[]{:S(2)}) collective-permute-start(bf16[576,1024]{1,0:T(8,128)(2,1)} %copy-done.21), channel_id=1, source_target_pairs={{0,1},{1,0},{2,3},{3,2},{4,5},{5,4},{6,7},{7,6},{8,9},{9,8},{10,11... | collective-permute-start | bytes 3538952 | tf_op jit(solution)/shard_map/ppermute | solution.py:46
  140.9 26.1 %collective-permute-start.24 = (bf16[8,128,512]{2,1,0:T(8,128)(2,1)}, bf16[8,128,512]{2,1,0:T(8,128)(2,1)}, u32[]{:S(2)}, u32[]{:S(2)}) collective-permute-start(bf16[8,128,512]{2,1,0:T(8,128)(2,1)} %pad_maximum_fusion.refs_0_), channel_id=1, source_target_pairs={{0,2},{1,3},{2,0},{3,1},{4,6},{5,7},{6,4},{7,5},{8,10},{9,11},{10,... | collective-permute-start | bytes 3145736 | tf_op jit(solution)/shard_map/ppermute | solution.py:46
  141.5 25.7 %collective-permute-start.25 = (bf16[8,128,512]{2,1,0:T(8,128)(2,1)}, bf16[8,128,512]{2,1,0:T(8,128)(2,1)}, u32[]{:S(2)}, u32[]{:S(2)}) collective-permute-start(bf16[8,128,512]{2,1,0:T(8,128)(2,1)} %pad_maximum_fusion.1.refs_2_), channel_id=1, source_target_pairs={{0,4},{1,5},{2,6},{3,7},{4,0},{5,1},{6,2},{7,3},{8,12},{9,13},{10,... | collective-permute-start | bytes 3145736 | tf_op jit(solution)/shard_map/ppermute | solution.py:46
  204.3 29.8 %collective-permute-start.34 = (bf16[4,2,256,256]{3,2,1,0:T(8,128)(2,1)}, bf16[4,2,256,256]{3,2,1,0:T(8,128)(2,1)}, u32[]{:S(2)}, u32[]{:S(2)}) collective-permute-start(bf16[4,2,256,256]{3,2,1,0:T(8,128)(2,1)} %get-tuple-element.430), channel_id=1, source_target_pairs={{0,2},{1,3},{2,0},{3,1},{4,6},{5,7},{6,4},{7,5},{8,10},{9,11},{10,... | collective-permute-start | bytes 3145736 | tf_op jit(solution)/shard_map/ppermute | solution.py:46
  205.0 29.2 %collective-permute-start.35 = (bf16[4,2,256,256]{3,2,1,0:T(8,128)(2,1)}, bf16[4,2,256,256]{3,2,1,0:T(8,128)(2,1)}, u32[]{:S(2)}, u32[]{:S(2)}) collective-permute-start(bf16[4,2,256,256]{3,2,1,0:T(8,128)(2,1)} %get-tuple-element.431), channel_id=1, source_target_pairs={{0,4},{1,5},{2,6},{3,7},{4,0},{5,1},{6,2},{7,3},{8,12},{9,13},{10,... | collective-permute-start | bytes 3145736 | tf_op jit(solution)/shard_map/ppermute | solution.py:46
  239.2 25.6 %collective-permute-start.38 = (bf16[576,2048]{1,0:T(8,128)(2,1)}, bf16[576,2048]{1,0:T(8,128)(2,1)}, u32[]{:S(2)}, u32[]{:S(2)}) collective-permute-start(bf16[576,2048]{1,0:T(8,128)(2,1)} %constant_dynamic-slice_fusion.11), channel_id=1, source_target_pairs={{0,1},{1,0},{2,3},{3,2},{4,5},{5,4},{6,7},{7,6},{8,9},{9,8},{10,11... | collective-permute-start | bytes 7077896 | tf_op jit(solution)/shard_map/ppermute | solution.py:46
  273.2 26.9 %collective-permute-start.42 = (f32[2,2176]{1,0:T(2,128)S(1)}, f32[2,2176]{1,0:T(2,128)S(1)}, u32[]{:S(2)}, u32[]{:S(2)}) collective-permute-start(f32[2,2176]{1,0:T(2,128)S(1)} %get-tuple-element.701), channel_id=1, source_target_pairs={{0,2},{1,3},{2,4},{3,5},{4,6},{5,7},{6,8},{7,9},{8,10},{9,11},{10,... | collective-permute-start | bytes 52232 | tf_op jit(solution)/shard_map/ppermute | solution.py:499
  300.1 39.1 %collective-permute-start.47 = (bf16[4,2,64,1280]{3,2,1,0:T(8,128)(2,1)}, bf16[4,2,64,1280]{3,2,1,0:T(8,128)(2,1)}, u32[]{:S(2)}, u32[]{:S(2)}) collective-permute-start(bf16[4,2,64,1280]{3,2,1,0:T(8,128)(2,1)} %get-tuple-element.496), channel_id=1, source_target_pairs={{0,2},{1,3},{2,0},{3,1},{4,6},{5,7},{6,4},{7,5},{8,10},{9,11},{10,... | collective-permute-start | bytes 3932168 | tf_op jit(solution)/shard_map/ppermute | solution.py:46
  300.2 39.0 %collective-permute-start.48 = (bf16[4,2,64,1280]{3,2,1,0:T(8,128)(2,1)}, bf16[4,2,64,1280]{3,2,1,0:T(8,128)(2,1)}, u32[]{:S(2)}, u32[]{:S(2)}) collective-permute-start(bf16[4,2,64,1280]{3,2,1,0:T(8,128)(2,1)} %get-tuple-element.497), channel_id=1, source_target_pairs={{0,4},{1,5},{2,6},{3,7},{4,0},{5,1},{6,2},{7,3},{8,12},{9,13},{10,... | collective-permute-start | bytes 3932168 | tf_op jit(solution)/shard_map/ppermute | solution.py:46
  300.3 42.5 %collective-permute-start.44 = (bf16[256,512]{1,0:T(8,128)(2,1)}, bf16[256,512]{1,0:T(8,128)(2,1)S(1)}, u32[]{:S(2)}, u32[]{:S(2)}) collective-permute-start(bf16[256,512]{1,0:T(8,128)(2,1)} %get-tuple-element.493), channel_id=1, source_target_pairs={{0,8},{1,9},{2,10},{3,11},{4,12},{5,13},{6,14},{7,15},{8,16},{9,17... | collective-permute-start | bytes 786440 | tf_op jit(solution)/shard_map/ppermute | solution.py:46
  300.3 42.5 %collective-permute-start.45 = (bf16[256,512]{1,0:T(8,128)(2,1)}, bf16[256,512]{1,0:T(8,128)(2,1)S(1)}, u32[]{:S(2)}, u32[]{:S(2)}) collective-permute-start(bf16[256,512]{1,0:T(8,128)(2,1)} %get-tuple-element.494), channel_id=1, source_target_pairs={{0,16},{1,17},{2,18},{3,19},{4,20},{5,21},{6,22},{7,23},{8,24},{9,... | collective-permute-start | bytes 786440 | tf_op jit(solution)/shard_map/ppermute | solution.py:46
  305.0 37.8 %collective-permute-start.46 = (bf16[256,512]{1,0:T(8,128)(2,1)}, bf16[256,512]{1,0:T(8,128)(2,1)S(1)}, u32[]{:S(2)}, u32[]{:S(2)}) collective-permute-start(bf16[256,512]{1,0:T(8,128)(2,1)} %get-tuple-element.495), channel_id=1, source_target_pairs={{0,24},{1,25},{2,26},{3,27},{4,28},{5,29},{6,30},{7,31},{8,0},{9,1... | collective-permute-start | bytes 786440 | tf_op jit(solution)/shard_map/ppermute | solution.py:46
  358.5 26.7 %collective-permute-start.56 = (bf16[576,384]{1,0:T(8,128)(2,1)}, bf16[576,384]{1,0:T(8,128)(2,1)}, u32[]{:S(2)}, u32[]{:S(2)}) collective-permute-start(bf16[576,384]{1,0:T(8,128)(2,1)} %get-tuple-element.674), channel_id=1, source_target_pairs={{0,1},{1,2},{2,3},{3,0},{4,5},{5,6},{6,7},{7,4},{8,9},{9,10},{10,1... | collective-permute-start | bytes 1327112 | tf_op jit(solution)/shard_map/ppermute | solution.py:1003
  360.0 30.9 %collective-permute-start.57 = (bf16[576,384]{1,0:T(8,128)(2,1)}, bf16[576,384]{1,0:T(8,128)(2,1)}, u32[]{:S(2)}, u32[]{:S(2)}) collective-permute-start(bf16[576,384]{1,0:T(8,128)(2,1)} %get-tuple-element.673), channel_id=1, source_target_pairs={{0,2},{1,3},{2,0},{3,1},{4,6},{5,7},{6,4},{7,5},{8,10},{9,11},{10,... | collective-permute-start | bytes 1327112 | tf_op jit(solution)/shard_map/ppermute | solution.py:1003
  360.5 31.3 %collective-permute-start.58 = (bf16[576,384]{1,0:T(8,128)(2,1)}, bf16[576,384]{1,0:T(8,128)(2,1)}, u32[]{:S(2)}, u32[]{:S(2)}) collective-permute-start(bf16[576,384]{1,0:T(8,128)(2,1)} %get-tuple-element.672), channel_id=1, source_target_pairs={{0,3},{1,0},{2,1},{3,2},{4,7},{5,4},{6,5},{7,6},{8,11},{9,8},{10,9... | collective-permute-start | bytes 1327112 | tf_op jit(solution)/shard_map/ppermute | solution.py:1003
  391.8 33.7 %collective-permute-start.62 = (bf16[4,2,64,1408]{3,2,1,0:T(8,128)(2,1)}, bf16[4,2,64,1408]{3,2,1,0:T(8,128)(2,1)}, u32[]{:S(2)}, u32[]{:S(2)}) collective-permute-start(bf16[4,2,64,1408]{3,2,1,0:T(8,128)(2,1)} %get-tuple-element.582), channel_id=1, source_target_pairs={{0,2},{1,3},{2,0},{3,1},{4,6},{5,7},{6,4},{7,5},{8,10},{9,11},{10,... | collective-permute-start | bytes 4325384 | tf_op jit(solution)/shard_map/ppermute | solution.py:46
  393.1 33.3 %collective-permute-start.63 = (bf16[4,2,64,1408]{3,2,1,0:T(8,128)(2,1)}, bf16[4,2,64,1408]{3,2,1,0:T(8,128)(2,1)}, u32[]{:S(2)}, u32[]{:S(2)}) collective-permute-start(bf16[4,2,64,1408]{3,2,1,0:T(8,128)(2,1)} %get-tuple-element.583), channel_id=1, source_target_pairs={{0,4},{1,5},{2,6},{3,7},{4,0},{5,1},{6,2},{7,3},{8,12},{9,13},{10,... | collective-permute-start | bytes 4325384 | tf_op jit(solution)/shard_map/ppermute | solution.py:46
  394.5 35.7 %collective-permute-start.59 = (bf16[64,2560]{1,0:T(8,128)(2,1)}, bf16[64,2560]{1,0:T(8,128)(2,1)}, u32[]{:S(2)}, u32[]{:S(2)}) collective-permute-start(bf16[64,2560]{1,0:T(8,128)(2,1)} %get-tuple-element.579), channel_id=1, source_target_pairs={{0,8},{1,9},{2,10},{3,11},{4,12},{5,13},{6,14},{7,15},{8,16},{9,17... | collective-permute-start | bytes 983048 | tf_op jit(solution)/shard_map/ppermute | solution.py:46
  396.2 34.0 %collective-permute-start.60 = (bf16[64,2560]{1,0:T(8,128)(2,1)}, bf16[64,2560]{1,0:T(8,128)(2,1)}, u32[]{:S(2)}, u32[]{:S(2)}) collective-permute-start(bf16[64,2560]{1,0:T(8,128)(2,1)} %get-tuple-element.580), channel_id=1, source_target_pairs={{0,16},{1,17},{2,18},{3,19},{4,20},{5,21},{6,22},{7,23},{8,24},{9,... | collective-permute-start | bytes 983048 | tf_op jit(solution)/shard_map/ppermute | solution.py:46
  397.7 32.5 %collective-permute-start.61 = (bf16[64,2560]{1,0:T(8,128)(2,1)}, bf16[64,2560]{1,0:T(8,128)(2,1)}, u32[]{:S(2)}, u32[]{:S(2)}) collective-permute-start(bf16[64,2560]{1,0:T(8,128)(2,1)} %get-tuple-element.581), channel_id=1, source_target_pairs={{0,24},{1,25},{2,26},{3,27},{4,28},{5,29},{6,30},{7,31},{8,0},{9,1... | collective-permute-start | bytes 983048 | tf_op jit(solution)/shard_map/ppermute | solution.py:46
  459.7 28.3 %collective-permute-start.71 = (bf16[64,2816]{1,0:T(8,128)(2,1)}, bf16[64,2816]{1,0:T(8,128)(2,1)S(1)}, u32[]{:S(2)}, u32[]{:S(2)}) collective-permute-start(bf16[64,2816]{1,0:T(8,128)(2,1)} %get-tuple-element.640), channel_id=1, source_target_pairs={{0,16},{1,17},{2,18},{3,19},{4,20},{5,21},{6,22},{7,23},{8,24},{9,... | collective-permute-start | bytes 1081352 | tf_op jit(solution)/shard_map/ppermute | solution.py:46
  461.2 31.6 %collective-permute-start.72 = (bf16[64,2816]{1,0:T(8,128)(2,1)}, bf16[64,2816]{1,0:T(8,128)(2,1)S(1)}, u32[]{:S(2)}, u32[]{:S(2)}) collective-permute-start(bf16[64,2816]{1,0:T(8,128)(2,1)} %get-tuple-element.641), channel_id=1, source_target_pairs={{0,24},{1,25},{2,26},{3,27},{4,28},{5,29},{6,30},{7,31},{8,0},{9,1... | collective-permute-start | bytes 1081352 | tf_op jit(solution)/shard_map/ppermute | solution.py:46
  (126 other events, 1135.2 us)
Sparse Core Ops, SparseCore 0:
  12.5 120.7 all-gather.4
  141.0 65.0 all-gather.6

commit v5 on v4

--- a/solution.py
+++ b/solution.py
@@ -1071,6 +1071,7 @@
 
     mixed_w = lax.all_gather(mixed_shard, AXES)
     a_fc2.second()
+    a_fc2.early()
     attended_far = peer(attended)
     first_sum, normed2 = attn_out_norm(attended, joined, x, table)
     activation, slope = mlp_in(normed2, joined, full_bias_fc1)
@@ -1078,19 +1079,18 @@
         (a_fc2,), activation, slope, normed2, first_sum, cuts, attended_far
     )
 
-    activation_far, normed2_far = peer(activation), peer(normed2)
+    activation_far = peer(activation)
     pieces = pieces + [pooled_piece(k) for k in range(early, n_ch)]
-    a_fc2.early()
-    a_fc2.cross()
     pooled = jnp.zeros((count, n_ch * own_ch), bf16)
     for k in range(n_ch):
         from_ch = lax.rem(ch - k + n_ch, n_ch)
         pooled = lax.dynamic_update_slice(pooled, pieces[k], (0, from_ch * own_ch))
-    activation_far, normed2_far, slope, attended, pieces, pooled = step(
-        (a_fc2,), activation_far, normed2_far, slope, attended, pieces, pooled
-    )
-
-    (full_fc2,) = a_fc2.whole()
+    activation_far, normed2, slope, attended, pieces, pooled = step(
+        (a_fc2,), activation_far, normed2, slope, attended, pieces, pooled
+    )
+
+    a_fc2.cross()
+    normed2_far = peer(normed2)
     ff = activation.shape[1]
     s_one = Scatter(
         grid,
@@ -1098,7 +1098,11 @@
         2 * ff // total,
         d // 4,
     )
-    slope, attended, pieces, full_fc2 = step((s_one,), slope, attended, pieces, full_fc2)
+    a_fc2.c2, s_one.away = lax.optimization_barrier((a_fc2.c2, s_one.away))
+    (full_fc2,) = a_fc2.whole()
+    slope, attended, pieces, full_fc2, normed2_far = step(
+        (s_one,), slope, attended, pieces, full_fc2, normed2_far
+    )
 
     s_one.first()
     d_pre, d_bias_fc1, d_normed2 = mlp_back(dy, slope, joined, full_fc2)
@@ -1172,11 +1176,12 @@
     small = jnp.concatenate(
         [lines, d_bias_fc1.reshape(total, -1), jnp.broadcast_to(gate_sum, (total, 128))], 1
     )
+    later = n_ch // 2
     back = []
     for k in range(n_ch):
         to = lax.rem(ch + k, n_ch)
         piece = lax.dynamic_slice(d_pooled, (0, to * own_ch), (count, own_ch))
-        back.append(along_ch(piece, k) if k else piece)
+        back.append(along_ch(piece, k) if k not in (0, later) else piece)
     wide, low = 3 * d // 4, hidden // 4
     half = d // (hidden // 2)
     s_three = Scatter(
@@ -1246,6 +1251,7 @@
     s_small.v, back = step((s_one, s_two, s_three), s_small.v, back)
 
     s_three.along_z()
+    back[later] = along_ch(back[later], later)
     while s_small.left:
         s_small.next()
     (g_fc2,) = s_one.results()

time: 527 us -> 517 us (0.981)
    ppermute x6, waiting for transfers between devices: 13.7 us -> 5.25 us  [along_ch(): return lax.ppermute(v, AXES, pairs)]
    unnamed x164 -> x168, local copies, waits for them, and re-layouts: 32.1 us -> 32.6 us
  transfers between devices with their start and end apart: 79 -> 79, of which waited for: 27 -> 22; matrix products, arithmetic and copies ran while one was open for 11% -> 11% of each run, Pallas kernels for 42% -> 43%
where the time goes in v5:
time: 517 us; the launch traced here: 510 us
  Pallas kernels  225 us (44%)
  waiting for transfers between devices  87.7 us (17%)
  starting transfers between devices  87.6 us (17%)
  local copies, waits for them, and re-layouts  68.7 us (13%)
  between operations  18.3 us (4%)
  other arithmetic  12.2 us (2%)
  matrix products  10.7 us (2%)
    ppermute x57, waiting for transfers between devices, send(): return lax.ppermute(v, AXES, pairs)  70 us
    ppermute x57, starting transfers between devices, send(): return lax.ppermute(v, AXES, pairs)  55.4 us
    pallas_call x3, Pallas kernels, __init__(): pl.pallas_call(functools.partial(weight_grad_body, (nx, ny), shapes, None...  44.5 us
    unnamed x168, local copies, waits for them, and re-layouts  32.6 us
    pallas_call x3, Pallas kernels, rows_call(): pl.pallas_call(body, grid=(steps,), in_specs=[spec(a.shape, by_rows) for...  25.7 us
    pallas_call x1, Pallas kernels, attend_back(): pl.pallas_call(attend_back_body, grid=(n,), in_specs=[spec(0), spec(1), s...  25.5 us
    pallas_call x1, Pallas kernels, mlp_back(): pl.pallas_call(mlp_back_body, grid=(ff // block,), in_specs=[whole, part,...  17.1 us
    pallas_call x2, Pallas kernels, columns_call(): pl.pallas_call(body, grid=(width // block,), in_specs=[spec(a.shape, by)...  17 us
  transfers between devices with their start and end apart: 79, of which 22 were waited for; matrix products, arithmetic and copies ran while one was open for 11% of the time, Pallas kernels for 43%

profile of v5, /device:TPU:9, one launch (start us, length us, event | category | flops | bytes accessed | tf_op | source)
XLA Modules:
  0.0 509.9 jit_solution(14040468069537650884)
XLA Ops:
  17.0 6.8 %concatenate.85 = bf16[736]{0:T(1024)(128)(2,1)S(1)} concatenate(bf16[32]{0:T(256)(128)(2,1)} %param.27, bf16[32]{0:T(256)(128)(2,1)} %param.28, bf16[32]{0:T(256)(128)(2,1)} %param.32, bf16[32]{0:T(256)(128)(2,1)} %param.33, bf16[32]{0:T(256)(128)(2,1)} %param.34, bf16[32]{0:T(256)(128)(2,1)} %param.38, bf16[32]{0:T(256)(128)(2,1)} %param.40, bf16[32]{0:T(256)(128)(2,1)} %param.42, ...), dimensions={0} | concatenate | bytes 2944 | tf_op jit(solution)/shard_map/concatenate | solution.py:976
  25.4 4.5 convolution_convert_fusion.1
  46.9 6.2 %collective-permute-done.7 = bf16[4,32,1536]{2,1,0:T(8,128)(2,1)S(1)} collective-permute-done((bf16[4,32,1536]{2,1,0:T(8,128)(2,1)S(1)}, bf16[4,32,1536]{2,1,0:T(8,128)(2,1)S(1)}, u32[]{:S(2)}, u32[]{:S(2)}) %collective-permute-start.7) | collective-permute-done | bytes 393248 | tf_op jit(solution)/shard_map/ppermute | solution.py:46
  54.8 5.1 %collective-permute-start.13 = (bf16[128,1024]{1,0:T(8,128)(2,1)S(1)}, bf16[128,1024]{1,0:T(8,128)(2,1)}, u32[]{:S(2)}, u32[]{:S(2)}) collective-permute-start(bf16[128,1024]{1,0:T(8,128)(2,1)S(1)} %copy-done.74), channel_id=1, source_target_pairs={{0,16},{1,17},{2,18},{3,19},{4,20},{5,21},{6,22},{7,23},{8,24},{9,... | collective-permute-start | bytes 786440 | tf_op jit(solution)/shard_map/ppermute | solution.py:46
  67.2 7.9 %collective-permute-done.13 = bf16[128,1024]{1,0:T(8,128)(2,1)} collective-permute-done((bf16[128,1024]{1,0:T(8,128)(2,1)S(1)}, bf16[128,1024]{1,0:T(8,128)(2,1)}, u32[]{:S(2)}, u32[]{:S(2)}) %collective-permute-start.13) | collective-permute-done | bytes 262176 | tf_op jit(solution)/shard_map/ppermute | solution.py:46
  76.1 11.8 %collective-permute-done.14 = bf16[128,1024]{1,0:T(8,128)(2,1)} collective-permute-done((bf16[128,1024]{1,0:T(8,128)(2,1)S(1)}, bf16[128,1024]{1,0:T(8,128)(2,1)}, u32[]{:S(2)}, u32[]{:S(2)}) %collective-permute-start.14) | collective-permute-done | bytes 262176 | tf_op jit(solution)/shard_map/ppermute | solution.py:46
  90.7 5.2 %collective-permute-start.15 = (bf16[8,32,1536]{2,1,0:T(8,128)(2,1)S(1)}, bf16[8,32,1536]{2,1,0:T(8,128)(2,1)}, u32[]{:S(2)}, u32[]{:S(2)}) collective-permute-start(bf16[8,32,1536]{2,1,0:T(8,128)(2,1)S(1)} %pad_maximum_fusion.2.refs_0_), channel_id=1, source_target_pairs={{0,1},{1,0},{2,3},{3,2},{4,5},{5,4},{6,7},{7,6},{8,9},{9,8},{10,11... | collective-permute-start | bytes 2359304 | tf_op jit(solution)/shard_map/ppermute | solution.py:46
  97.0 4.7 collective-permute-done.19.refs_3_
  102.5 4.9 collective-permute-start.20
  120.1 7.1 %project.1.q_ref.k_ref.v_ref = bf16[576,3072]{1,0:T(8,128)(2,1)S(1)} custom-call(bf16[576,1024]{1,0:T(8,128)(2,1)S(1)} %copy-done.11, bf16[1024,3072]{1,0:T(8,128)(2,1)} %bitcast.130, f32[1,3072]{1,0:T(1,128)S(1)} %bitcast.142), custom_call_target="tpu_custom_call" | custom-call | tf_op jit(solution)/shard_map/project/pallas_call | solution.py:833
  129.0 15.0 %attend.1 = (bf16[576,1024]{1,0:T(8,128)(2,1)}, f32[576,1024]{1,0:T(8,128)S(1)}) custom-call(bf16[576,3072]{1,0:T(8,128)(2,1)} %copy-done.2, bf16[576,3072]{1,0:T(8,128)(2,1)} %copy-done.2, bf16[576,3072]{1,0:T(8,128)(2,1)} %copy-done.2), custom_call_target="tpu_custom_call" | custom-call | tf_op jit(solution)/shard_map/attend/pallas_call | solution.py:538
  152.3 4.9 attn_out.1
  158.6 16.3 %mlp_in.1 = (bf16[576,4096]{1,0:T(8,128)(2,1)}, bf16[576,4096]{1,0:T(8,128)(2,1)}) custom-call(bf16[576,1024]{1,0:T(8,128)(2,1)S(1)} %get-tuple-element.439.n_ref.refs_0_, bf16[32,5,32,1024]{3,2,1,0:T(8,128)(2,1)} %bitcast.146, f32[1,4096]{1,0:T(1,128)S(1)} %bitcast.141), custom_call_target="tpu_custom_call" | custom-call | tf_op jit(solution)/shard_map/mlp_in/pallas_call | solution.py:616
  180.8 5.2 %collective-permute-done.30.refs_3_ = bf16[576,384]{1,0:T(8,128)(2,1)S(1)} collective-permute-done((bf16[576,384]{1,0:T(8,128)(2,1)S(1)}, bf16[576,384]{1,0:T(8,128)(2,1)S(1)}, u32[]{:S(2)}, u32[]{:S(2)}) %collective-permute-start.30) | collective-permute-done | bytes 442400 | tf_op jit(solution)/shard_map/ppermute | solution.py:1003
  187.5 12.0 %weight_grad.3 = (bf16[4,2,256,256]{3,2,1,0:T(8,128)(2,1)}, bf16[4,2,256,256]{3,2,1,0:T(8,128)(2,1)}, bf16[4,2,256,256]{3,2,1,0:T(8,128)(2,1)}, bf16[4,2,256,256]{3,2,1,0:T(8,128)(2,1)}) custom-call(s32[4]{0:T(128)} %copy-done.42, bf16[576,4096]{1,0:T(8,128)(2,1)} %get-tuple-element.594.refs_0_.a_ref, bf16[576,4096]{1,0:T(8,128)(2,1)} %collective-permute-done.29.refs_1_, ...), custom_call_target="tpu_custom_call" | custom-call | tf_op jit(solution)/shard_map/weight_grad/pallas_call | solution.py:290
  208.2 17.1 %mlp_back.1 = (bf16[576,4096]{1,0:T(8,128)(2,1)}, f32[1,4096]{1,0:T(1,128)S(1)}, f32[576,1024]{1,0:T(8,128)S(1)}) custom-call(bf16[576,1024]{1,0:T(8,128)(2,1)S(1)} %bitcast.133, bf16[576,4096]{1,0:T(8,128)(2,1)} %get-tuple-element.442.slope_ref, bf16[32,5,32,1024]{3,2,1,0:T(8,128)(2,1)} %bitcast.147, bf16[4096,1024]{1,0:T(8,128)(2,1)} %bitcast.128), custom_call_target="tpu_custom_call" | custom-call | tf_op jit(solution)/shard_map/mlp_back/pallas_call | solution.py:641
  226.6 7.3 %norm_two.1 = (f32[576,1024]{1,0:T(8,128)S(1)}, bf16[576,1024]{1,0:T(8,128)(2,1)S(1)}, bf16[576,1024]{1,0:T(8,128)(2,1)S(1)}, f32[3,1024]{1,0:T(4,128)S(1)}) custom-call(f32[576,1024]{1,0:T(8,128)} %copy-done.34, f32[576,1024]{1,0:T(8,128)} %copy-done.13, bf16[576,1024]{1,0:T(8,128)(2,1)S(1)} %bitcast.134, f32[17,1024]{1,0:T(8,128)S(1)} %reshape.192.t_ref.refs_5_.table_ref, ...), custom_call_target="tpu_custom_call" | custom-call | tf_op jit(solution)/shard_map/norm_two/pallas_call | solution.py:743
  253.6 8.2 %adapter.1 = (f32[576,1024]{1,0:T(8,128)S(1)}, f32[576,1024]{1,0:T(8,128)}, f32[1,1024]{1,0:T(1,128)S(1)}, f32[1,1024]{1,0:T(1,128)S(1)}, f32[1,1024]{1,0:T(1,128)S(1)}) custom-call(s32[1]{0:T(128)} %bitcast.30.pos_ref, bf16[576,384]{1,0:T(8,128)(2,1)S(1)} %copy-done.24, bf16[576,384]{1,0:T(8,128)(2,1)} %collective-permute-done.22.refs_1_, ...), custom_call_target="tpu_custom_call" | custom-call | tf_op jit(solution)/shard_map/adapter/pallas_call | solution.py:687
  263.4 4.7 fold_z.3
  280.5 4.6 collective-permute-start.43
  285.1 15.3 %weight_grad.4 = (bf16[4,2,64,1280]{3,2,1,0:T(8,128)(2,1)}, bf16[4,2,64,1280]{3,2,1,0:T(8,128)(2,1)}, bf16[4,2,64,1280]{3,2,1,0:T(8,128)(2,1)}, bf16[4,2,64,1280]{3,2,1,0:T(8,128)(2,1)}) custom-call(s32[4]{0:T(128)} %copy-done.42, bf16[576,1024]{1,0:T(8,128)(2,1)} %copy-done.21, bf16[576,1024]{1,0:T(8,128)(2,1)} %copy-done.54, ...), custom_call_target="tpu_custom_call" | custom-call | tf_op jit(solution)/shard_map/weight_grad/pallas_call | solution.py:290
  304.7 25.5 %attend_back.1 = (bf16[576,1024]{1,0:T(8,128)(2,1)S(1)}, bf16[576,1024]{1,0:T(8,128)(2,1)S(1)}, bf16[576,1024]{1,0:T(8,128)(2,1)S(1)}) custom-call(bf16[576,3072]{1,0:T(8,128)(2,1)} %copy-done.2, bf16[576,3072]{1,0:T(8,128)(2,1)} %copy-done.2, bf16[576,3072]{1,0:T(8,128)(2,1)} %copy-done.2, bf16[576,1024]{1,0:T(8,128)(2,1)S(1)} %copy-done.38, ...), custom_call_target="tpu_custom_call" | custom-call | tf_op jit(solution)/shard_map/attend_back/pallas_call | solution.py:578
  333.1 5.5 %adapter_back.1 = (bf16[576,1024]{1,0:T(8,128)(2,1)S(1)}, f32[9,1024]{1,0:T(8,128)S(1)}, f32[1,1024]{1,0:T(1,128)S(1)}, f32[1,1024]{1,0:T(1,128)S(1)}) custom-call(bf16[576,1024]{1,0:T(8,128)(2,1)S(1)} %bitcast.136, f32[576,1024]{1,0:T(8,128)S(1)} %copy-done.32, f32[1,1024]{1,0:T(1,128)S(1)} %get-tuple-element.596.gate_ref.g_ref, ...), custom_call_target="tpu_custom_call" | custom-call | tf_op jit(solution)/shard_map/adapter_back/pallas_call | solution.py:718
  349.3 4.7 collective-permute-done.52.refs_5_.refs_7_.refs_9_.refs_11_
  359.6 17.2 %weight_grad.5 = (bf16[4,2,64,1408]{3,2,1,0:T(8,128)(2,1)}, bf16[4,2,64,1408]{3,2,1,0:T(8,128)(2,1)}, bf16[4,2,64,1408]{3,2,1,0:T(8,128)(2,1)}, bf16[4,2,64,1408]{3,2,1,0:T(8,128)(2,1)}) custom-call(s32[4]{0:T(128)} %copy-done.42, bf16[576,1024]{1,0:T(8,128)(2,1)} %fusion.5.n_ref.refs_0_, bf16[576,1024]{1,0:T(8,128)(2,1)} %copy-done.55, ...), custom_call_target="tpu_custom_call" | custom-call | tf_op jit(solution)/shard_map/weight_grad/pallas_call | solution.py:290
  377.9 5.3 %fold_z.4 = (f32[64,2560]{1,0:T(8,128)}, bf16[64,2560]{1,0:T(8,128)(2,1)}, bf16[64,2560]{1,0:T(8,128)(2,1)}, bf16[64,2560]{1,0:T(8,128)(2,1)}) custom-call(s32[4]{0:T(128)} %copy-done.42, bf16[4,2,64,1280]{3,2,1,0:T(8,128)(2,1)} %get-tuple-element.552.refs_0_, bf16[4,2,64,1280]{3,2,1,0:T(8,128)(2,1)} %collective-permute-done.47.refs_1_, ...), custom_call_target="tpu_custom_call" | custom-call | tf_op jit(solution)/shard_map/fold_z/pallas_call | solution.py:406
  390.5 9.9 %layer_output.1 = bf16[576,1024]{1,0:T(8,128)(2,1)} custom-call(bf16[576,4096]{1,0:T(8,128)(2,1)} %get-tuple-element.594.refs_0_.a_ref, bf16[4096,1024]{1,0:T(8,128)(2,1)} %bitcast.129, f32[576,1024]{1,0:T(8,128)S(1)} %copy-done.14, f32[17,1024]{1,0:T(8,128)S(1)} %reshape.192.t_ref.refs_5_.table_ref, f32[1,1024]{1,0:T(1,128)S(1)} %get-tuple-element.596.gate_ref.g_ref, ...), custom_call_target="tpu_custom_call" | custom-call | tf_op jit(solution)/shard_map/layer_output/pallas_call | solution.py:833
  400.4 13.5 %norm_one.1 = (bf16[576,1024]{1,0:T(8,128)(2,1)}, f32[4,1024]{1,0:T(4,128)S(1)}) custom-call(bf16[576,1024]{1,0:T(8,128)(2,1)S(1)} %copy-done.16, bf16[576,1024]{1,0:T(8,128)(2,1)S(1)} %copy-done.18, bf16[576,1024]{1,0:T(8,128)(2,1)S(1)} %copy-done.20, bf16[1024,3072]{1,0:T(8,128)(2,1)} %bitcast.131, bf16[576,1024]{1,0:T(8,128)(2,1)S(1)} %bitcast.138, ...), custom_call_target="tpu_custom_call" | custom-call | tf_op jit(solution)/shard_map/norm_one/pallas_call | solution.py:743
  439.9 5.3 %fold_z.5 = (f32[64,2816]{1,0:T(8,128)}, bf16[64,2816]{1,0:T(8,128)(2,1)}, bf16[64,2816]{1,0:T(8,128)(2,1)}, bf16[64,2816]{1,0:T(8,128)(2,1)}) custom-call(s32[4]{0:T(128)} %copy-done.42, bf16[4,2,64,1408]{3,2,1,0:T(8,128)(2,1)} %get-tuple-element.632.refs_0_, bf16[4,2,64,1408]{3,2,1,0:T(8,128)(2,1)} %collective-permute-done.61.refs_1_, ...), custom_call_target="tpu_custom_call" | custom-call | tf_op jit(solution)/shard_map/fold_z/pallas_call | solution.py:406
  453.8 4.6 collective-permute-start.74
  462.3 15.1 %collective-permute-done.70.refs_2_ = bf16[64,2816]{1,0:T(8,128)(2,1)S(1)} collective-permute-done((bf16[64,2816]{1,0:T(8,128)(2,1)}, bf16[64,2816]{1,0:T(8,128)(2,1)S(1)}, u32[]{:S(2)}, u32[]{:S(2)}) %collective-permute-start.70) | collective-permute-done | bytes 360480 | tf_op jit(solution)/shard_map/ppermute | solution.py:46
  477.3 6.9 %collective-permute-done.71.refs_3_ = bf16[64,2816]{1,0:T(8,128)(2,1)S(1)} collective-permute-done((bf16[64,2816]{1,0:T(8,128)(2,1)}, bf16[64,2816]{1,0:T(8,128)(2,1)S(1)}, u32[]{:S(2)}, u32[]{:S(2)}) %collective-permute-start.71) | collective-permute-done | bytes 360480 | tf_op jit(solution)/shard_map/ppermute | solution.py:46
  (429 shorter events, 203.3 us)
Async XLA Ops:
  7.2 143.8 %all-gather.5.cloned.1.call-start = ((), (), s32[]{:S(2)}) async-start(), calls=%async_computation | async-start | bytes 10813440 | tf_op jit(solution)/shard_map/all_gather | solution.py:983
  12.4 233.8 %all-gather.7.cloned.1.call-start = ((), (), s32[]{:S(2)}) async-start(), calls=%async_computation.1 | async-start | bytes 5406720 | tf_op jit(solution)/shard_map/all_gather | solution.py:1072
  14.9 25.1 %collective-permute-start.2 = (bf16[32,3072]{1,0:T(8,128)(2,1)}, bf16[32,3072]{1,0:T(8,128)(2,1)S(1)}, u32[]{:S(2)}, u32[]{:S(2)}) collective-permute-start(bf16[32,3072]{1,0:T(8,128)(2,1)} %param.29), channel_id=1, source_target_pairs={{0,24},{1,25},{2,26},{3,27},{4,28},{5,29},{6,30},{7,31},{8,0},{9,1... | collective-permute-start | bytes 589832 | tf_op jit(solution)/shard_map/ppermute | solution.py:46
  59.9 28.0 %collective-permute-start.14 = (bf16[128,1024]{1,0:T(8,128)(2,1)S(1)}, bf16[128,1024]{1,0:T(8,128)(2,1)}, u32[]{:S(2)}, u32[]{:S(2)}) collective-permute-start(bf16[128,1024]{1,0:T(8,128)(2,1)S(1)} %copy-done.74), channel_id=1, source_target_pairs={{0,24},{1,25},{2,26},{3,27},{4,28},{5,29},{6,30},{7,31},{8,0},{9,1... | collective-permute-start | bytes 786440 | tf_op jit(solution)/shard_map/ppermute | solution.py:46
  60.8 29.9 %collective-permute-start.10 = (bf16[8,32,1536]{2,1,0:T(8,128)(2,1)S(1)}, bf16[8,32,1536]{2,1,0:T(8,128)(2,1)S(1)}, u32[]{:S(2)}, u32[]{:S(2)}) collective-permute-start(bf16[8,32,1536]{2,1,0:T(8,128)(2,1)S(1)} %pad_maximum_fusion.2.refs_0_), channel_id=1, source_target_pairs={{0,2},{1,3},{2,0},{3,1},{4,6},{5,7},{6,4},{7,5},{8,10},{9,11},{10,... | collective-permute-start | bytes 2359304 | tf_op jit(solution)/shard_map/ppermute | solution.py:46
  62.0 28.7 %collective-permute-start.11 = (bf16[8,32,1536]{2,1,0:T(8,128)(2,1)}, bf16[8,32,1536]{2,1,0:T(8,128)(2,1)}, u32[]{:S(2)}, u32[]{:S(2)}) collective-permute-start(bf16[8,32,1536]{2,1,0:T(8,128)(2,1)} %pad_maximum_fusion.3.refs_2_), channel_id=1, source_target_pairs={{0,4},{1,5},{2,6},{3,7},{4,0},{5,1},{6,2},{7,3},{8,12},{9,13},{10,... | collective-permute-start | bytes 2359304 | tf_op jit(solution)/shard_map/ppermute | solution.py:46
  102.5 41.5 %collective-permute-start.20 = (bf16[4,128,512]{2,1,0:T(8,128)(2,1)}, bf16[4,128,512]{2,1,0:T(8,128)(2,1)}, u32[]{:S(2)}, u32[]{:S(2)}) collective-permute-start(bf16[4,128,512]{2,1,0:T(8,128)(2,1)} %pad_maximum_fusion.4), channel_id=1, source_target_pairs={{0,4},{1,5},{2,6},{3,7},{4,0},{5,1},{6,2},{7,3},{8,12},{9,13},{10,... | collective-permute-start | bytes 1572872 | tf_op jit(solution)/shard_map/ppermute | solution.py:46
  107.4 36.5 %collective-permute-start.21 = (bf16[4,128,512]{2,1,0:T(8,128)(2,1)}, bf16[4,128,512]{2,1,0:T(8,128)(2,1)}, u32[]{:S(2)}, u32[]{:S(2)}) collective-permute-start(bf16[4,128,512]{2,1,0:T(8,128)(2,1)} %pad_maximum_fusion.5), channel_id=1, source_target_pairs={{0,2},{1,3},{2,0},{3,1},{4,6},{5,7},{6,4},{7,5},{8,10},{9,11},{10,... | collective-permute-start | bytes 1572872 | tf_op jit(solution)/shard_map/ppermute | solution.py:46
  107.6 41.2 %collective-permute-start.22 = (bf16[576,384]{1,0:T(8,128)(2,1)}, bf16[576,384]{1,0:T(8,128)(2,1)}, u32[]{:S(2)}, u32[]{:S(2)}) collective-permute-start(bf16[576,384]{1,0:T(8,128)(2,1)} %get-tuple-element.391), channel_id=1, source_target_pairs={{0,1},{1,2},{2,3},{3,0},{4,5},{5,6},{6,7},{7,4},{8,9},{9,10},{10,1... | collective-permute-start | bytes 1327112 | tf_op jit(solution)/shard_map/ppermute | solution.py:1003
  110.4 38.4 %collective-permute-start.23 = (bf16[576,384]{1,0:T(8,128)(2,1)}, bf16[576,384]{1,0:T(8,128)(2,1)}, u32[]{:S(2)}, u32[]{:S(2)}) collective-permute-start(bf16[576,384]{1,0:T(8,128)(2,1)} %get-tuple-element.392), channel_id=1, source_target_pairs={{0,2},{1,3},{2,0},{3,1},{4,6},{5,7},{6,4},{7,5},{8,10},{9,11},{10,... | collective-permute-start | bytes 1327112 | tf_op jit(solution)/shard_map/ppermute | solution.py:1003
  148.8 27.7 %collective-permute-start.28 = (bf16[576,1024]{1,0:T(8,128)(2,1)}, bf16[576,1024]{1,0:T(8,128)(2,1)}, u32[]{:S(2)}, u32[]{:S(2)}) collective-permute-start(bf16[576,1024]{1,0:T(8,128)(2,1)} %get-tuple-element.492.a_ref.refs_4_), channel_id=1, source_target_pairs={{0,1},{1,0},{2,3},{3,2},{4,5},{5,4},{6,7},{7,6},{8,9},{9,8},{10,11... | collective-permute-start | bytes 3538952 | tf_op jit(solution)/shard_map/ppermute | solution.py:46
  149.3 25.6 %collective-permute-start.24 = (bf16[8,128,512]{2,1,0:T(8,128)(2,1)}, bf16[8,128,512]{2,1,0:T(8,128)(2,1)}, u32[]{:S(2)}, u32[]{:S(2)}) collective-permute-start(bf16[8,128,512]{2,1,0:T(8,128)(2,1)} %pad_maximum_fusion.refs_0_), channel_id=1, source_target_pairs={{0,1},{1,0},{2,3},{3,2},{4,5},{5,4},{6,7},{7,6},{8,9},{9,8},{10,11... | collective-permute-start | bytes 3145736 | tf_op jit(solution)/shard_map/ppermute | solution.py:46
  149.4 25.5 %collective-permute-start.25 = (bf16[8,128,512]{2,1,0:T(8,128)(2,1)}, bf16[8,128,512]{2,1,0:T(8,128)(2,1)}, u32[]{:S(2)}, u32[]{:S(2)}) collective-permute-start(bf16[8,128,512]{2,1,0:T(8,128)(2,1)} %pad_maximum_fusion.1.refs_2_), channel_id=1, source_target_pairs={{0,1},{1,0},{2,3},{3,2},{4,5},{5,4},{6,7},{7,6},{8,9},{9,8},{10,11... | collective-permute-start | bytes 3145736 | tf_op jit(solution)/shard_map/ppermute | solution.py:46
  149.8 26.2 %collective-permute-start.26 = (bf16[8,128,512]{2,1,0:T(8,128)(2,1)}, bf16[8,128,512]{2,1,0:T(8,128)(2,1)}, u32[]{:S(2)}, u32[]{:S(2)}) collective-permute-start(bf16[8,128,512]{2,1,0:T(8,128)(2,1)} %pad_maximum_fusion.refs_0_), channel_id=1, source_target_pairs={{0,2},{1,3},{2,0},{3,1},{4,6},{5,7},{6,4},{7,5},{8,10},{9,11},{10,... | collective-permute-start | bytes 3145736 | tf_op jit(solution)/shard_map/ppermute | solution.py:46
  151.0 25.5 %collective-permute-start.27 = (bf16[8,128,512]{2,1,0:T(8,128)(2,1)}, bf16[8,128,512]{2,1,0:T(8,128)(2,1)}, u32[]{:S(2)}, u32[]{:S(2)}) collective-permute-start(bf16[8,128,512]{2,1,0:T(8,128)(2,1)} %pad_maximum_fusion.1.refs_2_), channel_id=1, source_target_pairs={{0,4},{1,5},{2,6},{3,7},{4,0},{5,1},{6,2},{7,3},{8,12},{9,13},{10,... | collective-permute-start | bytes 3145736 | tf_op jit(solution)/shard_map/ppermute | solution.py:46
  207.8 28.6 %collective-permute-start.34 = (bf16[4,2,256,256]{3,2,1,0:T(8,128)(2,1)}, bf16[4,2,256,256]{3,2,1,0:T(8,128)(2,1)}, u32[]{:S(2)}, u32[]{:S(2)}) collective-permute-start(bf16[4,2,256,256]{3,2,1,0:T(8,128)(2,1)} %get-tuple-element.440), channel_id=1, source_target_pairs={{0,2},{1,3},{2,0},{3,1},{4,6},{5,7},{6,4},{7,5},{8,10},{9,11},{10,... | collective-permute-start | bytes 3145736 | tf_op jit(solution)/shard_map/ppermute | solution.py:46
  207.9 28.5 %collective-permute-start.35 = (bf16[4,2,256,256]{3,2,1,0:T(8,128)(2,1)}, bf16[4,2,256,256]{3,2,1,0:T(8,128)(2,1)}, u32[]{:S(2)}, u32[]{:S(2)}) collective-permute-start(bf16[4,2,256,256]{3,2,1,0:T(8,128)(2,1)} %get-tuple-element.441), channel_id=1, source_target_pairs={{0,4},{1,5},{2,6},{3,7},{4,0},{5,1},{6,2},{7,3},{8,12},{9,13},{10,... | collective-permute-start | bytes 3145736 | tf_op jit(solution)/shard_map/ppermute | solution.py:46
  241.4 26.7 %collective-permute-start.38 = (bf16[576,2048]{1,0:T(8,128)(2,1)}, bf16[576,2048]{1,0:T(8,128)(2,1)}, u32[]{:S(2)}, u32[]{:S(2)}) collective-permute-start(bf16[576,2048]{1,0:T(8,128)(2,1)} %constant_dynamic-slice_fusion.11), channel_id=1, source_target_pairs={{0,1},{1,0},{2,3},{3,2},{4,5},{5,4},{6,7},{7,6},{8,9},{9,8},{10,11... | collective-permute-start | bytes 7077896 | tf_op jit(solution)/shard_map/ppermute | solution.py:46
  300.3 38.3 %collective-permute-start.47 = (bf16[4,2,64,1280]{3,2,1,0:T(8,128)(2,1)}, bf16[4,2,64,1280]{3,2,1,0:T(8,128)(2,1)}, u32[]{:S(2)}, u32[]{:S(2)}) collective-permute-start(bf16[4,2,64,1280]{3,2,1,0:T(8,128)(2,1)} %get-tuple-element.506), channel_id=1, source_target_pairs={{0,2},{1,3},{2,0},{3,1},{4,6},{5,7},{6,4},{7,5},{8,10},{9,11},{10,... | collective-permute-start | bytes 3932168 | tf_op jit(solution)/shard_map/ppermute | solution.py:46
  300.4 38.2 %collective-permute-start.48 = (bf16[4,2,64,1280]{3,2,1,0:T(8,128)(2,1)}, bf16[4,2,64,1280]{3,2,1,0:T(8,128)(2,1)}, u32[]{:S(2)}, u32[]{:S(2)}) collective-permute-start(bf16[4,2,64,1280]{3,2,1,0:T(8,128)(2,1)} %get-tuple-element.507), channel_id=1, source_target_pairs={{0,4},{1,5},{2,6},{3,7},{4,0},{5,1},{6,2},{7,3},{8,12},{9,13},{10,... | collective-permute-start | bytes 3932168 | tf_op jit(solution)/shard_map/ppermute | solution.py:46
  301.4 40.9 %collective-permute-start.44 = (bf16[256,512]{1,0:T(8,128)(2,1)}, bf16[256,512]{1,0:T(8,128)(2,1)S(1)}, u32[]{:S(2)}, u32[]{:S(2)}) collective-permute-start(bf16[256,512]{1,0:T(8,128)(2,1)} %get-tuple-element.503), channel_id=1, source_target_pairs={{0,8},{1,9},{2,10},{3,11},{4,12},{5,13},{6,14},{7,15},{8,16},{9,17... | collective-permute-start | bytes 786440 | tf_op jit(solution)/shard_map/ppermute | solution.py:46
  301.6 40.7 %collective-permute-start.45 = (bf16[256,512]{1,0:T(8,128)(2,1)}, bf16[256,512]{1,0:T(8,128)(2,1)S(1)}, u32[]{:S(2)}, u32[]{:S(2)}) collective-permute-start(bf16[256,512]{1,0:T(8,128)(2,1)} %get-tuple-element.504), channel_id=1, source_target_pairs={{0,16},{1,17},{2,18},{3,19},{4,20},{5,21},{6,22},{7,23},{8,24},{9,... | collective-permute-start | bytes 786440 | tf_op jit(solution)/shard_map/ppermute | solution.py:46
  304.5 37.8 %collective-permute-start.46 = (bf16[256,512]{1,0:T(8,128)(2,1)}, bf16[256,512]{1,0:T(8,128)(2,1)S(1)}, u32[]{:S(2)}, u32[]{:S(2)}) collective-permute-start(bf16[256,512]{1,0:T(8,128)(2,1)} %get-tuple-element.505), channel_id=1, source_target_pairs={{0,24},{1,25},{2,26},{3,27},{4,28},{5,29},{6,30},{7,31},{8,0},{9,1... | collective-permute-start | bytes 786440 | tf_op jit(solution)/shard_map/ppermute | solution.py:46
  357.6 25.6 %collective-permute-start.56 = (bf16[576,384]{1,0:T(8,128)(2,1)}, bf16[576,384]{1,0:T(8,128)(2,1)}, u32[]{:S(2)}, u32[]{:S(2)}) collective-permute-start(bf16[576,384]{1,0:T(8,128)(2,1)} %get-tuple-element.684), channel_id=1, source_target_pairs={{0,1},{1,2},{2,3},{3,0},{4,5},{5,6},{6,7},{7,4},{8,9},{9,10},{10,1... | collective-permute-start | bytes 1327112 | tf_op jit(solution)/shard_map/ppermute | solution.py:1003
  383.2 32.5 %collective-permute-start.61 = (bf16[4,2,64,1408]{3,2,1,0:T(8,128)(2,1)}, bf16[4,2,64,1408]{3,2,1,0:T(8,128)(2,1)}, u32[]{:S(2)}, u32[]{:S(2)}) collective-permute-start(bf16[4,2,64,1408]{3,2,1,0:T(8,128)(2,1)} %get-tuple-element.592), channel_id=1, source_target_pairs={{0,2},{1,3},{2,0},{3,1},{4,6},{5,7},{6,4},{7,5},{8,10},{9,11},{10,... | collective-permute-start | bytes 4325384 | tf_op jit(solution)/shard_map/ppermute | solution.py:46
  384.5 33.0 %collective-permute-start.62 = (bf16[4,2,64,1408]{3,2,1,0:T(8,128)(2,1)}, bf16[4,2,64,1408]{3,2,1,0:T(8,128)(2,1)}, u32[]{:S(2)}, u32[]{:S(2)}) collective-permute-start(bf16[4,2,64,1408]{3,2,1,0:T(8,128)(2,1)} %get-tuple-element.593), channel_id=1, source_target_pairs={{0,4},{1,5},{2,6},{3,7},{4,0},{5,1},{6,2},{7,3},{8,12},{9,13},{10,... | collective-permute-start | bytes 4325384 | tf_op jit(solution)/shard_map/ppermute | solution.py:46
  384.5 36.8 %collective-permute-start.58 = (bf16[64,2560]{1,0:T(8,128)(2,1)}, bf16[64,2560]{1,0:T(8,128)(2,1)}, u32[]{:S(2)}, u32[]{:S(2)}) collective-permute-start(bf16[64,2560]{1,0:T(8,128)(2,1)} %get-tuple-element.589), channel_id=1, source_target_pairs={{0,8},{1,9},{2,10},{3,11},{4,12},{5,13},{6,14},{7,15},{8,16},{9,17... | collective-permute-start | bytes 983048 | tf_op jit(solution)/shard_map/ppermute | solution.py:46
  385.2 36.1 %collective-permute-start.59 = (bf16[64,2560]{1,0:T(8,128)(2,1)}, bf16[64,2560]{1,0:T(8,128)(2,1)}, u32[]{:S(2)}, u32[]{:S(2)}) collective-permute-start(bf16[64,2560]{1,0:T(8,128)(2,1)} %get-tuple-element.590), channel_id=1, source_target_pairs={{0,16},{1,17},{2,18},{3,19},{4,20},{5,21},{6,22},{7,23},{8,24},{9,... | collective-permute-start | bytes 983048 | tf_op jit(solution)/shard_map/ppermute | solution.py:46
  388.8 32.5 %collective-permute-start.60 = (bf16[64,2560]{1,0:T(8,128)(2,1)}, bf16[64,2560]{1,0:T(8,128)(2,1)}, u32[]{:S(2)}, u32[]{:S(2)}) collective-permute-start(bf16[64,2560]{1,0:T(8,128)(2,1)} %get-tuple-element.591), channel_id=1, source_target_pairs={{0,24},{1,25},{2,26},{3,27},{4,28},{5,29},{6,30},{7,31},{8,0},{9,1... | collective-permute-start | bytes 983048 | tf_op jit(solution)/shard_map/ppermute | solution.py:46
  448.5 35.7 %collective-permute-start.75 = (bf16[576,384]{1,0:T(8,128)(2,1)S(1)}, bf16[576,384]{1,0:T(8,128)(2,1)S(1)}, u32[]{:S(2)}, u32[]{:S(2)}) collective-permute-start(bf16[576,384]{1,0:T(8,128)(2,1)S(1)} %copy-done.64), channel_id=1, source_target_pairs={{0,2},{1,3},{2,0},{3,1},{4,6},{5,7},{6,4},{7,5},{8,10},{9,11},{10,... | collective-permute-start | bytes 1327112 | tf_op jit(solution)/shard_map/ppermute | solution.py:1003
  450.1 27.2 %collective-permute-start.70 = (bf16[64,2816]{1,0:T(8,128)(2,1)}, bf16[64,2816]{1,0:T(8,128)(2,1)S(1)}, u32[]{:S(2)}, u32[]{:S(2)}) collective-permute-start(bf16[64,2816]{1,0:T(8,128)(2,1)} %get-tuple-element.650), channel_id=1, source_target_pairs={{0,16},{1,17},{2,18},{3,19},{4,20},{5,21},{6,22},{7,23},{8,24},{9,... | collective-permute-start | bytes 1081352 | tf_op jit(solution)/shard_map/ppermute | solution.py:46
  453.8 30.5 %collective-permute-start.71 = (bf16[64,2816]{1,0:T(8,128)(2,1)}, bf16[64,2816]{1,0:T(8,128)(2,1)S(1)}, u32[]{:S(2)}, u32[]{:S(2)}) collective-permute-start(bf16[64,2816]{1,0:T(8,128)(2,1)} %get-tuple-element.651), channel_id=1, source_target_pairs={{0,24},{1,25},{2,26},{3,27},{4,28},{5,29},{6,30},{7,31},{8,0},{9,1... | collective-permute-start | bytes 1081352 | tf_op jit(solution)/shard_map/ppermute | solution.py:46
  (128 other events, 1229.2 us)
Sparse Core Ops, SparseCore 0:
  12.5 114.2 all-gather.4
  151.1 68.8 all-gather.6
